TPU v7x, 32 devices: a whole 2x2x4 slice. The times are simulated.
32 devices in a mesh: dp: 8 (over z, y), mp: 4 (over x, core).
Axes of the slice: x: 2, y: 2, z: 4, core: 2. Of those that a mesh axis runs over, the one named last changes fastest.
Arguments:
- layer_input: float32 [16, 1024, 512], P('dp', 'mp'), may hold values from -6 to 6
- qkv_weight: bfloat16 [512, 1536], replicated, may hold values from -0.25 to 0.25
- gate_weight: bfloat16 [512, 8], replicated, may hold values from -0.25 to 0.25
- gate_bias: float32 [8], replicated, may hold values from 2.9 to 7.5
- out_weight: bfloat16 [512, 512], replicated, may hold values from -0.75 to 0.75
- inner_weight: bfloat16 [512, 2048], P(None, 'mp'), may hold values from -0.25 to 0.25
- outer_weight: bfloat16 [2048, 512], P('mp'), may hold values from -0.125 to 0.125
- leading_norm_gain: float32 [512], replicated, may hold values from 0.1 to 1.9
- leading_norm_bias: float32 [512], replicated, may hold values from -3 to 3
- trailing_norm_gain: float32 [512], replicated, may hold values from 0.1 to 1.9
- trailing_norm_bias: float32 [512], replicated, may hold values from -3 to 3
- random_features: float32 [8, 64, 128], replicated, may hold values from -0.5 to 0.5
- output_grad: float32 [16, 1024, 512], P('dp', 'mp'), may hold values from -6 to 6
Outputs:
- layer_out: float32 [16, 1024, 512], P('dp', 'mp')
- layer_input_gradient: float32 [16, 1024, 512], P('dp', 'mp')
- qkv_weight_grad: float32 [512, 1536], replicated
- gate_weight_grad: float32 [512, 8], replicated
- gate_bias_grad: float32 [8], replicated
- out_weight_grad: float32 [512, 512], replicated
- inner_weight_grad: float32 [512, 2048], P(None, 'mp')
- outer_weight_grad: float32 [2048, 512], P('mp')
- leading_norm_gain_gradient: float32 [512], replicated
- first_shift_grad: float32 [512], replicated
- trailing_norm_gain_gradient: float32 [512], replicated
- second_shift_grad: float32 [512], replicated
All inputs are finite; a program needn't handle non-finite values.
Results may differ from a plain program's by a relative error of at most 0.0066.
Values may be sent and summed in bfloat16 or wider, within the bound.
No kernel may reach another device: no remote copies, remote signals or barrier semaphores. Data moves between devices by JAX's collectives and lax.ppermute only.
A program may use at most 128 MiB of HBM per device.

v0:
```python
import math

import jax
import jax.numpy as jnp
from jax import lax
from jax.sharding import PartitionSpec as P

exact = lax.Precision.HIGHEST
epsilon = 1e-05
guard = 0.01


def prefix(part, axis, combine, identity, reverse):
    count = lax.axis_size(axis)
    place = lax.axis_index(axis)
    ahead = count - 1 - place if reverse else place
    gathered = jax.tree.map(lambda a: lax.all_gather(a, axis), part)
    state = jax.tree.map(lambda a, e: jnp.zeros_like(a) + jnp.asarray(e, a.dtype), part, identity)

    def one(turn, state):
        source = count - 1 - turn if reverse else turn
        return combine(
            state, jax.tree.map(lambda a: lax.dynamic_index_in_dim(a, source, 0, False), gathered)
        )

    return lax.fori_loop(0, ahead, one, state)


def contract(left, right, left_dim, right_dim):
    return lax.dot_general(
        left, right, (((left_dim,), (right_dim,)), ((), ())), preferred_element_type=jnp.float32
    )


def layer_norm_pieces(token_row_values):
    centred = token_row_values - jnp.mean(token_row_values, axis=-1, keepdims=True)
    spread = jnp.mean(centred * centred, axis=-1, keepdims=True)
    inverse_deviation = lax.rsqrt(spread + epsilon)
    return (centred * inverse_deviation, inverse_deviation)


def layer_norm_backward(upstream_gradient, standardized_input, inverse_deviation, norm_gain):
    hidden_output = upstream_gradient * norm_gain
    return inverse_deviation * (
        hidden_output
        - jnp.mean(hidden_output, axis=-1, keepdims=True)
        - standardized_input * jnp.mean(hidden_output * standardized_input, axis=-1, keepdims=True)
    )


def features(values, frequencies):
    angles = jnp.einsum("...hd,hdf->...hf", values, frequencies, precision=exact)
    return jnp.concatenate([jnp.sin(angles), jnp.cos(angles)], axis=-1) / math.sqrt(
        frequencies.shape[-1]
    )


def block_parts(phi_query, phi_keys, values, log_keep, admit):
    length = log_keep.shape[1]
    cumul = jnp.cumsum(jnp.swapaxes(log_keep, 1, 2), axis=-1)
    admit_t = jnp.swapaxes(admit, 1, 2)
    rowid = lax.broadcasted_iota(jnp.int32, (length, length), 0)
    colid = lax.broadcasted_iota(jnp.int32, (length, length), 1)
    causal = rowid >= colid
    gap = cumul[..., :, None] - cumul[..., None, :]
    decay = jnp.where(causal, jnp.exp(jnp.where(causal, gap, 0.0)), 0.0)
    weights = decay * admit_t[..., None, :]
    kernel = jnp.einsum("sthf,suhf->shtu", phi_query, phi_keys, precision=exact)
    scores = kernel * weights
    inner_num = jnp.einsum("shtu,suhd->sthd", scores, values, precision=exact)
    inner_den = jnp.swapaxes(jnp.sum(scores, axis=-1), 1, 2)
    total = cumul[..., -1]
    carried = jnp.exp(total)
    tail = jnp.exp(total[..., None] - cumul) * admit_t
    scaled = phi_keys * jnp.swapaxes(tail, 1, 2)[..., None]
    state_part = jnp.einsum("suhf,suhd->shfd", scaled, values, precision=exact)
    norm_part = jnp.sum(scaled, axis=1)
    return (cumul, inner_num, inner_den, carried, state_part, norm_part)


def block_finish(phi_query, cumul, inner_num, inner_den, state, norm):
    growth = jnp.exp(jnp.swapaxes(cumul, 1, 2))
    numer = (
        growth[..., None] * jnp.einsum("sthf,shfd->sthd", phi_query, state, precision=exact)
        + inner_num
    )
    sden = growth * jnp.einsum("sthf,shf->sth", phi_query, norm, precision=exact) + inner_den
    denom = jnp.sqrt(sden * sden + guard)
    return (numer / denom[..., None], numer, denom, sden, growth)


def local_attend(query, keys, values, logit, state, norm, frequencies):
    phi_query = features(query, frequencies)
    phi_keys = features(keys, frequencies)
    cumul, inner_num, inner_den, carried, state_part, norm_part = block_parts(
        phi_query, phi_keys, values, jax.nn.log_sigmoid(logit), jax.nn.sigmoid(-logit)
    )
    mixed, numer, denom, sden, growth = block_finish(
        phi_query, cumul, inner_num, inner_den, state, norm
    )
    results = (
        mixed,
        carried[..., None, None] * state + state_part,
        carried[..., None] * norm + norm_part,
    )
    return (results, (phi_query, numer, denom, sden, growth, carried))


def chain_forward(earlier, later):
    return (
        earlier[0] * later[0],
        later[0][..., None, None] * earlier[1] + later[1],
        later[0][..., None] * earlier[2] + later[2],
    )


def chain_backward(earlier, later):
    return (
        earlier[0] * later[0],
        later[1] + later[0][..., None, None] * earlier[1],
        later[2] + later[0][..., None] * earlier[2],
    )


def gelu_back(pre, upstream_gradient):
    _, pullback = jax.vjp(jax.nn.gelu, pre)
    return pullback(upstream_gradient)[0]


def per_device(
    layer_input,
    qkv_weight,
    gate_weight,
    gate_bias,
    out_weight,
    inner_weight,
    outer_weight,
    leading_norm_gain,
    leading_norm_bias,
    trailing_norm_gain,
    trailing_norm_bias,
    random_features,
    output_grad,
):
    seqs, length, width = layer_input.shape
    heads = gate_weight.shape[1]
    head = width // heads
    count = seqs * length
    token_row_values = layer_input.reshape(count, width)
    standardized_input_one, inverse_deviation_one = layer_norm_pieces(token_row_values)
    leading_normalized = (standardized_input_one * leading_norm_gain + leading_norm_bias).astype(
        jnp.bfloat16
    )
    proj = jnp.dot(leading_normalized, qkv_weight, preferred_element_type=jnp.float32)
    logit = (
        jnp.dot(leading_normalized, gate_weight, preferred_element_type=jnp.float32) + gate_bias
    ).reshape(seqs, length, heads)
    query = proj[:, :width].reshape(seqs, length, heads, head)
    keys = proj[:, width : 2 * width].reshape(seqs, length, heads, head)
    values = proj[:, 2 * width :].reshape(seqs, length, heads, head)
    phi_query = features(query, random_features)
    phi_keys = features(keys, random_features)
    cumul, inner_num, inner_den, carried, state_part, norm_part = block_parts(
        phi_query, phi_keys, values, jax.nn.log_sigmoid(logit), jax.nn.sigmoid(-logit)
    )
    identity = (jnp.ones_like(carried), jnp.zeros_like(state_part), jnp.zeros_like(norm_part))
    _, state, norm = prefix((carried, state_part, norm_part), "mp", chain_forward, identity, False)
    mixed = block_finish(phi_query, cumul, inner_num, inner_den, state, norm)[0]
    mixed_low = mixed.reshape(count, width).astype(jnp.bfloat16)
    residual_stream = token_row_values + jnp.dot(
        mixed_low, out_weight, preferred_element_type=jnp.float32
    )
    standardized_input_two, inverse_deviation_two = layer_norm_pieces(residual_stream)
    trailing_normalized = (standardized_input_two * trailing_norm_gain + trailing_norm_bias).astype(
        jnp.bfloat16
    )
    gathered = lax.all_gather(trailing_normalized, "mp", axis=0, tiled=True)
    pre = jnp.dot(gathered, inner_weight, preferred_element_type=jnp.float32)
    active = jax.nn.gelu(pre).astype(jnp.bfloat16)
    ffn_out = lax.psum_scatter(
        jnp.dot(active, outer_weight, preferred_element_type=jnp.float32).astype(jnp.bfloat16),
        "mp",
        scatter_dimension=0,
        tiled=True,
    ).astype(jnp.float32)
    layer_out = residual_stream + ffn_out
    gradient_row_values = output_grad.reshape(count, width)
    out_low = gradient_row_values.astype(jnp.bfloat16)
    grad_gathered = lax.all_gather(out_low, "mp", axis=0, tiled=True)
    active_grad = contract(grad_gathered, outer_weight, 1, 1)
    outer_part = contract(active, grad_gathered, 0, 0)
    pre_grad = gelu_back(pre, active_grad).astype(jnp.bfloat16)
    inner_part = contract(gathered, pre_grad, 0, 0)
    trailing_normalized_gradient = lax.psum_scatter(
        contract(pre_grad, inner_weight, 1, 1), "mp", scatter_dimension=0, tiled=True
    )
    ffn_parts = (inner_part, outer_part)
    inner_total, outer_total = lax.psum((ffn_parts[0], ffn_parts[1]), "dp")
    trailing_norm_gain_gradient = jnp.sum(
        trailing_normalized_gradient * standardized_input_two, axis=0
    )
    second_shift_grad = jnp.sum(trailing_normalized_gradient, axis=0)
    residual_stream_gradient = gradient_row_values + layer_norm_backward(
        trailing_normalized_gradient,
        standardized_input_two,
        inverse_deviation_two,
        trailing_norm_gain,
    )
    branch_low = residual_stream_gradient.astype(jnp.bfloat16)
    out_weight_part = contract(mixed_low, branch_low, 0, 0)
    mixed_grad = contract(branch_low, out_weight, 1, 1).reshape(seqs, length, heads, head)

    def attend_piece(part_q, part_k, part_v, part_l, part_s, part_n):
        return local_attend(part_q, part_k, part_v, part_l, part_s, part_n, random_features)

    _, pullback, saved = jax.vjp(
        attend_piece, query, keys, values, logit, state, norm, has_aux=True
    )
    phi_again, numer, denom, sden, growth, carried_again = saved
    numer_grad = mixed_grad / denom[..., None]
    sden_grad = -jnp.sum(mixed_grad * numer, axis=-1) * sden / (denom * denom * denom)
    lifted = phi_again * growth[..., None]
    state_direct = jnp.einsum("sthf,sthd->shfd", lifted, numer_grad, precision=exact)
    norm_direct = jnp.einsum("sthf,sth->shf", lifted, sden_grad, precision=exact)
    _, state_grad, norm_grad = prefix(
        (carried_again, state_direct, norm_direct), "mp", chain_backward, identity, True
    )
    query_grad, keys_grad, values_grad, logit_grad, _, _ = pullback(
        (mixed_grad, state_grad, norm_grad)
    )
    proj_grad = jnp.concatenate(
        [
            query_grad.reshape(count, width),
            keys_grad.reshape(count, width),
            values_grad.reshape(count, width),
        ],
        axis=1,
    ).astype(jnp.bfloat16)
    logit_low = logit_grad.reshape(count, heads).astype(jnp.bfloat16)
    qkv_part = contract(leading_normalized, proj_grad, 0, 0)
    gate_weight_part = contract(leading_normalized, logit_low, 0, 0)
    gate_bias_part = jnp.sum(logit_low.astype(jnp.float32), axis=0)
    leading_normalized_gradient = contract(proj_grad, qkv_weight, 1, 1) + contract(
        logit_low, gate_weight, 1, 1
    )
    leading_norm_gain_gradient = jnp.sum(
        leading_normalized_gradient * standardized_input_one, axis=0
    )
    first_shift_grad = jnp.sum(leading_normalized_gradient, axis=0)
    layer_input_gradient = residual_stream_gradient + layer_norm_backward(
        leading_normalized_gradient,
        standardized_input_one,
        inverse_deviation_one,
        leading_norm_gain,
    )
    norm_parts = jnp.stack(
        [
            leading_norm_gain_gradient,
            first_shift_grad,
            trailing_norm_gain_gradient,
            second_shift_grad,
        ]
    )
    qkv_total, out_total, gate_weight_total, gate_bias_total, norm_total = lax.psum(
        (qkv_part, out_weight_part, gate_weight_part, gate_bias_part, norm_parts), ("dp", "mp")
    )
    return (
        layer_out.reshape(seqs, length, width),
        layer_input_gradient.reshape(seqs, length, width),
        qkv_total,
        gate_weight_total,
        gate_bias_total,
        out_total,
        inner_total,
        outer_total,
        norm_total[0],
        norm_total[1],
        norm_total[2],
        norm_total[3],
    )


def solution(mesh):
    in_specs = (
        P("dp", "mp", None),
        P(),
        P(),
        P(),
        P(),
        P(None, "mp"),
        P("mp", None),
        P(),
        P(),
        P(),
        P(),
        P(),
        P("dp", "mp", None),
    )
    out_specs = (
        P("dp", "mp", None),
        P("dp", "mp", None),
        P(),
        P(),
        P(),
        P(),
        P(None, "mp"),
        P("mp", None),
        P(),
        P(),
        P(),
        P(),
    )
    return jax.shard_map(
        per_device, mesh=mesh, in_specs=in_specs, out_specs=out_specs, check_vma=False
    )
```

profile of v0, /device:TPU:0, one launch (start us, length us, event | category | flops | bytes accessed | tf_op | source)
XLA Modules:
  0.0 625.7 jit_solution(4556693680280404480)
XLA Ops:
  22.7 3.9 fusion.57
  28.0 8.2 %sine_bitcast_fusion.1 = (f32[2,256,8,128]{1,3,0,2:T(8,128)}, f32[2,256,8,128]{1,3,0,2:T(8,128)}) fusion(f32[8,2,256,128]{2,3,1,0:T(8,128)S(1)} %fusion.57), kind=kLoop, calls=%fused_computation.83 | loop fusion | bytes 6291456 | tf_op jit(solution)/shard_map/sin | solution.py:53
  38.9 3.9 fusion.55
  44.1 8.2 %sine_bitcast_fusion = (f32[2,256,8,128]{1,3,0,2:T(8,128)}, f32[2,256,8,128]{1,3,0,2:T(8,128)}) fusion(f32[8,2,256,128]{2,3,1,0:T(8,128)S(1)} %fusion.55), kind=kLoop, calls=%fused_computation.81 | loop fusion | bytes 6291456 | tf_op jit(solution)/shard_map/sin | solution.py:53
  55.5 7.8 %fusion.32 = (f32[2,256,8,256]{1,3,0,2:T(8,128)}, f32[2,256,8,256]{1,3,0,2:T(8,128)}, f32[2,256,8,256]{1,3,0,2:T(8,128)}, f32[2,8,256]{2,0,1:T(2,128)S(1)}, f32[2,256,8,256]{1,3,0,2:T(8,128)S(1)}) fusion(f32[2,256,8,128]{1,3,0,2:T(8,128)} %get-tuple-element.352, f32[2,256,8,128]{1,3,0,2:T(8,128)} %get-tuple-element.351, f32[2,256,8]{1,0,2:T(2,128)S(1)} %copy.403, ...), kind=kLoop, calls=%fused_computation.53 | loop fusion | flops 7335936 | bytes 25214976 | tf_op jit(solution)/shard_map/mul | solution.py:222
  65.3 5.2 fusion.21
  72.9 6.6 %all-gather.2 = f32[8,8,256]{2,1,0:T(8,128)} all-gather(f32[2,8,256]{2,1,0:T(8,128)S(1)} %copy.371), channel_id=4, replica_groups=mesh['dp'=8,'mp'=4] {'mp'}, dimensions={0}, use_global_device_ids=true | all-gather | bytes 81920 | tf_op jit(solution)/shard_map/all_gather | solution.py:17
  79.5 5.4 all-gather
  85.9 13.2 %fusion.86 = (f32[2,8,256]{2,1,0:T(8,128)S(1)}, f32[2,8,256,256]{3,2,1,0:T(8,128)}) fusion(f32[2,8,256]{2,1,0:T(8,128)S(1)} %copy.379, f32[2,8,256]{2,1,0:T(8,128)S(1)} %add_bitcast_fusion, pred[256,256]{1,0:T(8,128)(4,1)S(1)} %iota_compare_fusion, f32[2,256,8,256]{1,3,0,2:T(8,128)} %get-tuple-element.387, f32[2,256,8,256]{1,3,0,2:T(8,128)} %get-tuple-element.346), kind=kOutput, calls=%fused_computation.97 | convolution fusion | flops 3227512832 | bytes 12697600 | tf_op jit(solution)/shard_map/sthf,suhf->shtu/dot_general | solution.py:68
  100.7 7.2 %all-gather.14.cloned.1.call-done = f32[8,8,256,64]{2,3,1,0:T(8,128)} async-done(((f32[2,8,256,64]{2,3,1,0:T(8,128)}), f32[8,8,256,64]{2,3,1,0:T(8,128)}) %all-gather.14.cloned.1.call-update) | async-done | bytes 4194320 | tf_op jit(solution)/shard_map/all_gather | solution.py:17
  110.4 4.3 fusion.27
  119.0 6.5 %fusion.62 = f32[2,256,8,64]{1,3,2,0:T(8,128)S(1)} fusion(f32[2,8,256,64]{3,2,1,0:T(8,128)} %get-tuple-element.184, f32[2,256,8,256]{1,3,0,2:T(8,128)} %get-tuple-element.346), kind=kOutput, calls=%fused_computation.85 | convolution fusion | flops 805306368 | bytes 6291456 | tf_op jit(solution)/shard_map/sthf,shfd->sthd/dot_general | solution.py:84
  125.6 5.9 divide_convert_fusion
  135.4 4.9 fusion.144
  140.3 41.7 %all-gather.10.cloned.1.call-done = bf16[2048,512]{1,0:T(8,128)(2,1)} async-done(((bf16[512,512]{1,0:T(8,128)(2,1)}), bf16[2048,512]{1,0:T(8,128)(2,1)}) %all-gather.10.cloned.1.call-update) | async-done | bytes 2097168 | tf_op jit(solution)/shard_map/all_gather | solution.py:177
  182.1 8.5 %fusion.6 = (bf16[2048,512]{1,0:T(8,128)(2,1)S(1)}, f32[2048,512]{1,0:T(8,128)}) fusion(f32[2048,512]{1,0:T(8,128)} %fusion.144, bf16[2048,512]{1,0:T(8,128)(2,1)} %all-gather.10.cloned.1.call-done, bf16[512,512]{1,0:T(8,128)(2,1)} %param.22), kind=kOutput, calls=%fused_computation.16 | convolution fusion | flops 1094713344 | bytes 13107200 | tf_op jit(solution)/shard_map/dot_general | solution.py:178
  192.0 3.3 fusion.145
  195.3 5.2 convolution_convert_fusion
  200.8 39.1 %reduce-scatter.5.cloned.1.call-done = f32[512,512]{1,0:T(8,128)} async-done(((f32[2048,512]{1,0:T(8,128)}), f32[512,512]{1,0:T(8,128)}) %reduce-scatter.5.cloned.1.call-update) | async-done | bytes 1048592 | tf_op jit(solution)/shard_map/reduce_scatter | solution.py:194
  243.4 30.5 %reduce-scatter.3.cloned.1.call-done = bf16[512,512]{1,0:T(8,128)(2,1)} async-done(((bf16[2048,512]{1,0:T(8,128)(2,1)}), bf16[512,512]{1,0:T(8,128)(2,1)}) %reduce-scatter.3.cloned.1.call-update) | async-done | bytes 524304 | tf_op jit(solution)/shard_map/reduce_scatter | solution.py:180
  273.9 3.1 bitcast_add_fusion.5
  281.4 7.8 %fusion.17 = f32[2,8,256,64]{2,3,1,0:T(8,128)} fusion(f32[2,256,8,256]{1,3,0,2:T(8,128)} %get-tuple-element.345, f32[2,256,8,64]{1,0,3,2:T(2,128)S(1)} %reshape.274, f32[2,256,8]{1,2,0:T(8,128)S(1)} %copy.382), kind=kOutput, calls=%fused_computation.37 | convolution fusion | flops 805568512 | bytes 6307840 | tf_op jit(solution)/shard_map/sthf,sthd->shfd/dot_general | solution.py:223
  293.1 4.8 fusion.148
  297.9 2.7 fusion.134
  301.1 7.1 %fusion.84 = f32[2,8,64,256]{3,2,1,0:T(8,128)} fusion(f32[2,8,256,256]{3,2,1,0:T(8,128)} %get-tuple-element.377, f32[2,8,256]{2,1,0:T(8,128)S(1)} %copy.379, f32[2,8,256]{2,1,0:T(8,128)S(1)} %add_bitcast_fusion, pred[256,256]{1,0:T(8,128)(4,1)S(1)} %iota_compare_fusion, f32[2,256,8,64]{1,0,3,2:T(2,128)S(1)} %reshape.274, f32[2,256,8]{1,2,0:T(8,128)S(1)} %copy.382), kind=kOutput, calls=%fused_computation.96 | convolution fusion | flops 810811392 | bytes 6406144 | tf_op jit(solution)/shard_map/transpose(jvp(shtu,suhd->sthd))/dot_general | solution.py:70
  314.2 5.8 fusion.15
  320.1 5.7 all-gather.4
  329.1 26.6 %while.31 = (s32[]{:T(128)}, f32[2,8,256,64]{3,2,1,0:T(8,128)}, f32[2,8,256]{2,1,0:T(8,128)S(1)}, s32[]{:T(128)}, f32[4,2,8,256,64]{3,4,2,1,0:T(8,128)}, /*index...) while((s32[]{:T(128)}, f32[2,8,256,64]{3,2,1,0:T(8,128)}, ...), condition=%wide.region_17.18_spmd, body=%wide.region_16.17_spmd.sunk | while | flops 532486 | bytes 7389607 | solution.py:26
  333.0 4.0 bitcast_add_fusion.13
  341.8 4.0 bitcast_add_fusion.13
  350.5 4.0 bitcast_add_fusion.13
  356.4 3.5 multiply_reduce_fusion.1
  359.9 7.5 %fusion.8 = (f32[2,256,8]{1,0,2:T(2,128)S(1)}, f32[2,8,256,256]{3,2,0,1:T(8,128)}) fusion(f32[2,8,256]{2,0,1:T(2,128)S(1)} %copy.408, f32[2,256,8,128]{1,3,0,2:T(8,128)} %get-tuple-element.354, f32[2,256,8,128]{1,3,0,2:T(8,128)S(1)} %copy-done.7, f32[2,256,8,64]{1,0,3,2:T(2,128)} %copy-done.17, f32[2,8,256,64]{3,2,1,0:T(8,128)S(1)} %copy-done.2), kind=kOutput, calls=%fused_computation.23 | convolution fusion | flops 810545152 | bytes 10518528 | tf_op jit(solution)/shard_map/transpose(jvp(suhf,suhd->shfd))/dot_general | solution.py:76
  368.3 2.9 bitcast_multiply_fusion.4
  379.3 9.2 %add_multiply_fusion = (f32[2,8,256,256]{3,2,1,0:T(8,128)}, f32[2,8,256,256]{3,2,1,0:T(8,128)}) fusion(f32[2,8,256,256]{3,2,1,0:T(8,128)} %get-tuple-element.377, f32[2,8,256]{2,1,0:T(8,128)S(1)} %add_multiply_fusion.1, f32[2,8,256]{2,1,0:T(8,128)S(1)} %copy-done.53, f32[2,8,256]{2,1,0:T(8,128)S(1)} %add_bitcast_fusion, ...), kind=kOutput, calls=%fused_computation.47 | convolution fusion | flops 812908544 | bytes 14811136 | tf_op jit(solution)/shard_map/transpose(jvp(shtu,suhd->sthd))/dot_general | solution.py:70
  390.1 4.0 fusion.37
  400.1 5.1 reduce-window.16
  405.4 7.6 %fusion.81 = bf16[2,256,8,64]{1,3,2,0:T(8,128)(2,1)} fusion(f32[2,8,64,256]{3,2,1,0:T(8,128)} %fusion.84, f32[2,8,256,64]{3,2,1,0:T(8,128)} %get-tuple-element.187, f32[2,256,8,256]{1,3,0,2:T(8,128)} %copy-done.4), kind=kOutput, calls=%fused_computation.95 | convolution fusion | flops 805830656 | bytes 6815744 | tf_op jit(solution)/shard_map/transpose(jvp(suhf,suhd->shfd))/dot_general | solution.py:76
  413.1 7.5 %fusion.7 = f32[2,256,8,256]{1,3,0,2:T(8,128)S(1)} fusion(f32[2,8,256,256]{3,2,0,1:T(8,128)} %get-tuple-element.385, f32[2,8,256,256]{3,2,1,0:T(8,128)S(1)} %copy-done.3, f32[2,256,8]{1,0,2:T(2,128)S(1)} %copy-done.61, f32[2,8,256]{2,0,1:T(2,128)S(1)} %copy-done.55, f32[2,256,8,128]{1,3,0,2:T(8,128)} %get-tuple-element.352, ...), kind=kOutput, calls=%fused_computation.20 | convolution fusion | flops 3227516928 | bytes 16809984 | tf_op jit(solution)/shard_map/transpose(jvp(sthf,suhf->shtu))/dot_general | solution.py:68
  420.5 11.7 %fusion.75 = bf16[2,256,8,64]{1,3,0,2:T(8,128)(2,1)S(1)} fusion(f32[2,256,8,256]{1,3,0,2:T(8,128)S(1)} %fusion.7, f32[8,64,128]{2,1,0:T(8,128)S(1)} %copy-done.29, f32[8,2,256,128]{2,3,1,0:T(8,128)S(1)} %copy-done.11), kind=kOutput, calls=%fused_computation.93 | convolution fusion | flops 405012480 | bytes 7077888 | tf_op jit(solution)/shard_map/transpose(jvp(...hd,hdf->...hf))/dot_general | solution.py:52
  439.2 8.9 %fusion.25 = f32[2,8,256,256]{2,3,0,1:T(8,128)S(1)} fusion(f32[2,8,256,256]{3,2,1,0:T(8,128)} %get-tuple-element.344, f32[2,256,8,128]{1,3,0,2:T(8,128)} %get-tuple-element.354, f32[2,256,8,128]{1,3,0,2:T(8,128)} %get-tuple-element.353), kind=kOutput, calls=%fused_computation.45 | convolution fusion | flops 3223322624 | bytes 12582912 | tf_op jit(solution)/shard_map/transpose(jvp(sthf,suhf->shtu))/dot_general | solution.py:68
  448.1 4.3 multiply_bitcast_fusion
  452.4 11.8 %fusion.78 = bf16[2,256,8,64]{1,3,0,2:T(8,128)(2,1)S(1)} fusion(f32[2,256,8,256]{1,3,0,2:T(8,128)S(1)} %multiply_bitcast_fusion, f32[8,64,128]{2,1,0:T(8,128)S(1)} %copy-done.29, f32[8,2,256,128]{2,3,1,0:T(8,128)S(1)} %copy-done.9), kind=kOutput, calls=%fused_computation.94 | convolution fusion | flops 405012480 | bytes 7077888 | tf_op jit(solution)/shard_map/transpose(jvp(...hd,hdf->...hf))/dot_general | solution.py:52
  469.9 2.7 convert_reduce_fusion
  477.2 40.2 %all-reduce.1 = (f32[512,8]{0,1:T(8,128)}, f32[8]{0:T(128)}, f32[4,512]{1,0:T(4,128)S(1)}) all-reduce(f32[512,8]{0,1:T(8,128)S(1)} %convolution_bitcast_fusion.1, f32[8]{0:T(128)S(1)} %copy-done.79, f32[4,512]{1,0:T(4,128)S(1)} %pad_maximum_fusion.2), channel_id=1, replica_groups=mesh['dp'=8,'mp'=4] {'dp','mp'}, use_global_device_ids=true, to_apply=%region_31.32 | all-reduce | flops 6152 | bytes 49216 | tf_op jit(solution)/shard_map/psum | solution.py:264
  518.1 2.9 multiply_add_fusion
  521.0 90.6 %all-reduce.7.cloned.1.call-done = (f32[512,1536]{1,0:T(8,128)}, f32[512,512]{1,0:T(8,128)}) async-done(((f32[512,1536]{1,0:T(8,128)}, f32[512,512]{1,0:T(8,128)}), (f32[512,1536]{1,0:T(8,128)}, f32[512,512]{1,0:T(8,128)})) %all-reduce.7.cloned.1.call-update) | async-done | bytes 4194320 | tf_op jit(solution)/shard_map/psum | solution.py:264
  611.6 3.9 copy.602
  (307 shorter events, 116.9 us)
Async XLA Ops:
  7.2 10.1 %copy-start = (bf16[512,1536]{1,0:T(8,128)(2,1)S(1)}, bf16[512,1536]{1,0:T(8,128)(2,1)}, u32[]{:S(2)}) copy-start(bf16[512,1536]{1,0:T(8,128)(2,1)} %param.18) | copy-start | bytes 4718596
  7.2 100.6 %all-gather.14.cloned.1.call-start = ((), (), s32[]{:S(2)}) async-start(), calls=%async_computation.6 | async-start | bytes 5242880 | tf_op jit(solution)/shard_map/all_gather | solution.py:17
  44.1 8.2 %copy-start.32 = (f32[512,512]{1,0:T(8,128)S(1)}, f32[512,512]{1,0:T(8,128)}, u32[]{:S(2)}) copy-start(f32[512,512]{1,0:T(8,128)} %get-tuple-element.348) | copy-start | bytes 3145732
  55.5 7.8 %copy-start.17 = (f32[2,256,8,64]{1,0,3,2:T(2,128)}, f32[2,256,8,64]{1,0,3,2:T(2,128)S(1)}, u32[]{:S(2)}) copy-start(f32[2,256,8,64]{1,0,3,2:T(2,128)S(1)} %reshape.270) | copy-start | bytes 3145732
  70.5 64.9 %all-gather.12.cloned.1.call-start = ((), (), s32[]{:S(2)}) async-start(), calls=%async_computation.4 | async-start | bytes 2621440 | tf_op jit(solution)/shard_map/all_gather | solution.py:189
  72.6 109.4 %all-gather.10.cloned.1.call-start = ((), (), s32[]{:S(2)}) async-start(), calls=%async_computation.2 | async-start | bytes 2621440 | tf_op jit(solution)/shard_map/all_gather | solution.py:177
  85.9 215.1 %copy-start.52 = (f32[2,8,256]{2,1,0:T(8,128)}, f32[2,8,256]{2,1,0:T(8,128)S(1)}, u32[]{:S(2)}) copy-start(f32[2,8,256]{2,1,0:T(8,128)S(1)} %copy.379) | copy-start | bytes 49156
  99.1 8.7 %copy-start.50 = (f32[2,8,256]{2,1,0:T(8,128)}, f32[2,8,256]{2,1,0:T(8,128)S(1)}, u32[]{:S(2)}) copy-start(f32[2,8,256]{2,1,0:T(8,128)S(1)} %get-tuple-element.376) | copy-start | bytes 49156
  115.5 10.0 %copy-start.18 = (f32[2,256,8,64]{1,0,3,2:T(2,128)S(1)}, f32[2,256,8,64]{1,0,3,2:T(2,128)}, u32[]{:S(2)}) copy-start(f32[2,256,8,64]{1,0,3,2:T(2,128)} %copy-done.17) | copy-start | bytes 3145732
  115.5 10.0 %copy-start.57 = (f32[2,256,8]{1,2,0:T(8,128)S(1)}, f32[2,256,8]{1,2,0:T(8,128)}, u32[]{:S(2)}) copy-start(f32[2,256,8]{1,2,0:T(8,128)} %copy.360) | copy-start | bytes 49156
  119.0 6.5 %copy-start.27 = (f32[2,8,256,256]{3,2,1,0:T(8,128)S(1)}, f32[2,8,256,256]{3,2,1,0:T(8,128)}, u32[]{:S(2)}) copy-start(f32[2,8,256,256]{3,2,1,0:T(8,128)} %get-tuple-element.377) | copy-start | bytes 12582916
  125.5 6.0 copy-start.30
  125.6 6.6 %copy-start.5 = (f32[2,256,512]{2,1,0:T(8,128)S(1)}, f32[2,256,512]{2,1,0:T(8,128)}, u32[]{:S(2)}) copy-start(f32[2,256,512]{2,1,0:T(8,128)} %param.17) | copy-start | bytes 3145732
  125.6 6.6 %copy-start.38 = (bf16[512,512]{1,0:T(8,128)(2,1)S(1)}, bf16[512,512]{1,0:T(8,128)(2,1)}, u32[]{:S(2)}) copy-start(bf16[512,512]{1,0:T(8,128)(2,1)} %param.21) | copy-start | bytes 1572868
  135.2 104.8 %reduce-scatter.5.cloned.1.call-start = ((), (), s32[]{:S(2)}) async-start(), calls=%async_computation.5 | async-start | bytes 5242880 | tf_op jit(solution)/shard_map/reduce_scatter | solution.py:194
  182.1 9.9 %copy-start.49 = (bf16[512,512]{1,0:T(8,128)(2,1)S(1)}, bf16[512,512]{1,0:T(8,128)(2,1)}, u32[]{:S(2)}) copy-start(bf16[512,512]{1,0:T(8,128)(2,1)} %param.22) | copy-start | bytes 1572868
  195.3 78.7 %reduce-scatter.3.cloned.1.call-start = ((), (), s32[]{:S(2)}) async-start(), calls=%async_computation.3 | async-start | bytes 2621440 | tf_op jit(solution)/shard_map/reduce_scatter | solution.py:180
  200.6 126.9 %all-gather.16.cloned.1.call-start = ((), (), s32[]{:S(2)}) async-start(), calls=%async_computation.7 | async-start | bytes 5242880 | tf_op jit(solution)/shard_map/all_gather | solution.py:17
  281.4 28.2 %copy-start.13 = (f32[2,256,8,64]{1,0,3,2:T(2,128)}, f32[2,256,8,64]{1,0,3,2:T(2,128)S(1)}, u32[]{:S(2)}) copy-start(f32[2,256,8,64]{1,0,3,2:T(2,128)S(1)} %reshape.274) | copy-start | bytes 3145732
  289.2 231.8 %all-reduce.9.cloned.1.call-start = ((), (), s32[]{:S(2)}) async-start(), calls=%async_computation.9 | async-start | bytes 4194304 | tf_op jit(solution)/shard_map/psum | solution.py:198
  300.7 310.9 %all-reduce.7.cloned.1.call-start = ((), (), s32[]{:S(2)}) async-start(), calls=%async_computation.8 | async-start | bytes 8388608 | tf_op jit(solution)/shard_map/psum | solution.py:264
  301.0 7.2 %copy-start.16 = (f32[512,512]{1,0:T(8,128)S(1)}, f32[512,512]{1,0:T(8,128)}, u32[]{:S(2)}) copy-start(f32[512,512]{1,0:T(8,128)} %copy-done.15) | copy-start | bytes 3145732
  301.0 7.2 %copy-start.26 = (bf16[64,8,2,256]{3,1,2,0:T(8,128)(2,1)S(1)}, bf16[64,8,2,256]{3,1,2,0:T(8,128)(2,1)}, u32[]{:S(2)}) copy-start(bf16[64,8,2,256]{3,1,2,0:T(8,128)(2,1)} %copy-done.25) | copy-start | bytes 1572868
  301.0 8.6 %copy-start.31 = (f32[2,256,8,64]{1,3,2,0:T(8,128)S(1)}, f32[2,256,8,64]{1,3,2,0:T(8,128)}, u32[]{:S(2)}) copy-start(f32[2,256,8,64]{1,3,2,0:T(8,128)} %copy-done.30) | copy-start | bytes 3145732
  301.0 8.6 %copy-start.48 = (f32[2,256,8,64]{1,3,2,0:T(8,128)S(1)}, f32[2,256,8,64]{1,3,2,0:T(8,128)}, u32[]{:S(2)}) copy-start(f32[2,256,8,64]{1,3,2,0:T(8,128)} %get-tuple-element.379) | copy-start | bytes 3145732
  301.1 8.6 %copy-start.58 = (f32[2,256,8]{1,2,0:T(8,128)S(1)}, f32[2,256,8]{1,2,0:T(8,128)}, u32[]{:S(2)}) copy-start(f32[2,256,8]{1,2,0:T(8,128)} %copy.386) | copy-start | bytes 49156
  311.8 14.0 %copy-start.60 = (f32[2,256,8]{1,2,0:T(8,128)S(1)}, f32[2,256,8]{1,2,0:T(8,128)}, u32[]{:S(2)}) copy-start(f32[2,256,8]{1,2,0:T(8,128)} %get-tuple-element.294) | copy-start | bytes 49156
  355.7 11.7 %copy-start.54 = (f32[2,8,256]{2,0,1:T(2,128)}, f32[2,8,256]{2,0,1:T(2,128)S(1)}, u32[]{:S(2)}) copy-start(f32[2,8,256]{2,0,1:T(2,128)S(1)} %copy.408) | copy-start | bytes 49156
  359.9 12.3 %copy-start.51 = (f32[2,8,256]{2,1,0:T(8,128)S(1)}, f32[2,8,256]{2,1,0:T(8,128)}, u32[]{:S(2)}) copy-start(f32[2,8,256]{2,1,0:T(8,128)} %copy-done.50) | copy-start | bytes 49156
  359.9 19.4 %copy-start.14 = (f32[2,256,8,64]{1,0,3,2:T(2,128)S(1)}, f32[2,256,8,64]{1,0,3,2:T(2,128)}, u32[]{:S(2)}) copy-start(f32[2,256,8,64]{1,0,3,2:T(2,128)} %copy-done.13) | copy-start | bytes 3145732
  359.9 19.4 %copy-start.53 = (f32[2,8,256]{2,1,0:T(8,128)S(1)}, f32[2,8,256]{2,1,0:T(8,128)}, u32[]{:S(2)}) copy-start(f32[2,8,256]{2,1,0:T(8,128)} %copy-done.52) | copy-start | bytes 49156
  388.5 8.1 %copy-start.20 = (f32[2,256,8]{2,0,1:T(2,128)S(1)}, f32[2,256,8]{2,0,1:T(2,128)}, u32[]{:S(2)}) copy-start(f32[2,256,8]{2,0,1:T(2,128)} %copy-done.19) | copy-start | bytes 49156
  388.5 8.1 %copy-start.22 = (f32[2,8,1,256]{1,0,3,2:T(2,128)S(1)}, f32[2,8,1,256]{1,0,3,2:T(2,128)}, u32[]{:S(2)}) copy-start(f32[2,8,1,256]{1,0,3,2:T(2,128)} %copy.445) | copy-start | bytes 49156
  388.5 8.1 %copy-start.35 = (f32[2,256,8]{2,0,1:T(2,128)S(1)}, f32[2,256,8]{2,0,1:T(2,128)}, u32[]{:S(2)}) copy-start(f32[2,256,8]{2,0,1:T(2,128)} %copy.420) | copy-start | bytes 49156
  388.5 8.1 %copy-start.42 = (f32[2,256,8]{2,0,1:T(2,128)S(1)}, f32[2,256,8]{2,0,1:T(2,128)}, u32[]{:S(2)}) copy-start(f32[2,256,8]{2,0,1:T(2,128)} %copy.426) | copy-start | bytes 49156
  399.1 13.9 %copy-start.55 = (f32[2,8,256]{2,0,1:T(2,128)S(1)}, f32[2,8,256]{2,0,1:T(2,128)}, u32[]{:S(2)}) copy-start(f32[2,8,256]{2,0,1:T(2,128)} %copy-done.54) | copy-start | bytes 49156
  399.1 14.0 %copy-start.61 = (f32[2,256,8]{1,0,2:T(2,128)S(1)}, f32[2,256,8]{1,0,2:T(2,128)}, u32[]{:S(2)}) copy-start(f32[2,256,8]{1,0,2:T(2,128)} %copy.412) | copy-start | bytes 49156
  405.4 7.6 %copy-start.3 = (f32[2,8,256,256]{3,2,1,0:T(8,128)S(1)}, f32[2,8,256,256]{3,2,1,0:T(8,128)}, u32[]{:S(2)}) copy-start(f32[2,8,256,256]{3,2,1,0:T(8,128)} %get-tuple-element.344) | copy-start | bytes 12582916
  405.4 7.6 %copy-start.12 = (f32[2,256,8,128]{1,3,0,2:T(8,128)S(1)}, f32[2,256,8,128]{1,3,0,2:T(8,128)}, u32[]{:S(2)}) copy-start(f32[2,256,8,128]{1,3,0,2:T(8,128)} %get-tuple-element.351) | copy-start | bytes 6291460
  413.0 7.5 %copy-start.11 = (f32[8,2,256,128]{2,3,1,0:T(8,128)S(1)}, f32[8,2,256,128]{2,3,1,0:T(8,128)}, u32[]{:S(2)}) copy-start(f32[8,2,256,128]{2,3,1,0:T(8,128)} %copy-done.10) | copy-start | bytes 6291460
  413.0 7.5 %copy-start.29 = (f32[8,64,128]{2,1,0:T(8,128)S(1)}, f32[8,64,128]{2,1,0:T(8,128)}, u32[]{:S(2)}) copy-start(f32[8,64,128]{2,1,0:T(8,128)} %param.28) | copy-start | bytes 786436
  420.5 11.8 %copy-start.46 = (f32[2,8,256]{1,0,2:T(2,128)S(1)}, f32[2,8,256]{1,0,2:T(2,128)}, u32[]{:S(2)}) copy-start(f32[2,8,256]{1,0,2:T(2,128)} %get-tuple-element.358) | copy-start | bytes 49156
  439.1 8.9 %copy-start.1 = (f32[2,8,256,64]{3,2,1,0:T(8,128)S(1)}, f32[2,8,256,64]{3,2,1,0:T(8,128)}, u32[]{:S(2)}) copy-start(f32[2,8,256,64]{3,2,1,0:T(8,128)} %get-tuple-element.184) | copy-start | bytes 3145732
  439.1 8.9 %copy-start.33 = (f32[2,8,64,256]{3,2,1,0:T(8,128)S(1)}, f32[2,8,64,256]{3,2,1,0:T(8,128)}, u32[]{:S(2)}) copy-start(f32[2,8,64,256]{3,2,1,0:T(8,128)} %get-tuple-element.355) | copy-start | bytes 3145732
  439.1 8.9 %copy-start.59 = (f32[2,8,256]{2,0,1:T(2,128)S(1)}, f32[2,8,256]{2,0,1:T(2,128)}, u32[]{:S(2)}) copy-start(f32[2,8,256]{2,0,1:T(2,128)} %copy.395) | copy-start | bytes 49156
  452.4 12.5 %copy-start.41 = (bf16[64,8,2,256]{3,1,2,0:T(8,128)(2,1)S(1)}, bf16[64,8,2,256]{3,1,2,0:T(8,128)(2,1)}, u32[]{:S(2)}) copy-start(bf16[64,8,2,256]{3,1,2,0:T(8,128)(2,1)} %copy.486) | copy-start | bytes 1572868
  452.4 12.5 %copy-start.40 = (bf16[64,8,2,256]{3,1,2,0:T(8,128)(2,1)S(1)}, bf16[64,8,2,256]{3,1,2,0:T(8,128)(2,1)}, u32[]{:S(2)}) copy-start(bf16[64,8,2,256]{3,1,2,0:T(8,128)(2,1)} %copy.487) | copy-start | bytes 1572868
  611.6 5.9 copy-start.43
  (42 other events, 124.8 us)
Sparse Core Ops, SparseCore 0:
  70.6 37.1 all-gather.13
  109.9 22.6 all-gather.11
  135.3 46.7 all-gather.9
  195.4 44.4 reduce-scatter.4
  242.5 31.4 reduce-scatter.2
  289.3 34.4 all-gather.15
  327.5 102.1 all-reduce.8
  469.0 142.5 all-reduce.6
where the time goes:
time: 636 us; the launch traced here: 626 us
  waiting for transfers between devices  209 us (33%)
  matrix products  174 us (27%)
  local copies, waits for them, and re-layouts  92.7 us (15%)
  other arithmetic  74.6 us (12%)
  blocking collectives  57.9 us (9%)
  between operations  15.5 us (2%)
    psum x1, waiting for transfers between devices, per_device(): lax.psum((qkv_part, out_weight_part, gate_weight_part, gate_bias_part, no...  90.6 us
    all_gather x1, waiting for transfers between devices, per_device(): gathered = lax.all_gather(trailing_normalized, 'mp', axis=0, tiled=True)  41.7 us
    psum x1, blocking collectives, per_device(): lax.psum((qkv_part, out_weight_part, gate_weight_part, gate_bias_part, no...  40.2 us
    reduce_scatter x1, waiting for transfers between devices, per_device(): lax.psum_scatter(contract(pre_grad, inner_weight, 1, 1), 'mp', scatter_di...  39.1 us
    dot_general x4, matrix products, features(): jnp.einsum('...hd,hdf->...hf', values, frequencies, precision=exact)  31.3 us
    reduce_scatter x1, waiting for transfers between devices, per_device(): lax.psum_scatter(jnp.dot(active, outer_weight, preferred_element_type=jnp...  30.5 us
    dot_general x3, matrix products, block_parts(): kernel = jnp.einsum('sthf,suhf->shtu', phi_query, phi_keys, precision=exact)  29.5 us
    dot_general x10, matrix products, contract(): lax.dot_general(left, right, (((left_dim,), (right_dim,)), ((), ())), pre...  25.7 us
  transfers between devices with their start and end apart: 8, of which 5 were waited for; matrix products, arithmetic and copies ran while one was open for 38% of the time, Pallas kernels for 0%

commit v1 on v0

v1 whole, which is shorter than its diff:
```python
import math

import jax
import jax.numpy as jnp
from jax import lax
from jax.experimental import pallas as pl
from jax.experimental.pallas import tpu as pltpu
from jax.sharding import PartitionSpec as P

BF = jnp.bfloat16
F32 = jnp.float32
epsilon = 1e-05
guard = 0.01
LANES = 128
EXTRA = 16
VMEM_BYTES = 56 * 1024 * 1024


def nn(a, b):
    return lax.dot_general(a, b, (((1,), (0,)), ((), ())), preferred_element_type=F32)


def nt(a, b):
    return lax.dot_general(a, b, (((1,), (1,)), ((), ())), preferred_element_type=F32)


def tn(a, b):
    return lax.dot_general(a, b, (((0,), (0,)), ((), ())), preferred_element_type=F32)


def two_terms(v):
    high = v.astype(BF)
    return high, (v - high.astype(F32)).astype(BF)


def iota(shape, dim):
    return lax.broadcasted_iota(jnp.int32, shape, dim)


def triangle(length, upper):
    rows, cols = iota((length, length), 0), iota((length, length), 1)
    return jnp.where((cols >= rows) if upper else (rows >= cols), 1.0, 0.0).astype(BF)


def running_sum(v, upper):
    ones = triangle(v.shape[0], upper)
    high, rest = two_terms(v)
    low = (v - high.astype(F32) - rest.astype(F32)).astype(BF)
    return nn(ones, high) + nn(ones, rest) + nn(ones, low)


def norm_rows(v):
    centred = v - jnp.mean(v, axis=-1, keepdims=True)
    scale = lax.rsqrt(jnp.mean(centred * centred, axis=-1, keepdims=True) + epsilon)
    return centred * scale, scale


def norm_rows_backward(grad, xhat, scale, gain):
    g = grad * gain
    return scale * (
        g
        - jnp.mean(g, axis=-1, keepdims=True)
        - xhat * jnp.mean(g * xhat, axis=-1, keepdims=True)
    )


def pair_frequencies(freq_ref, pair):
    even, odd = freq_ref[2 * pair], freq_ref[2 * pair + 1]
    none = jnp.zeros_like(even)
    return jnp.concatenate(
        [jnp.concatenate([even, none], axis=1), jnp.concatenate([none, odd], axis=1)], axis=0
    )


def scaled_sine_cosine(angles, scale):
    turns = jnp.floor(angles * (1.0 / math.pi) + 0.5)
    r = angles - turns * 3.140625
    r = r - turns * 0.0009675025939941406
    r = r - turns * 1.509958e-07
    odd = turns - 2.0 * jnp.floor(turns * 0.5)
    sign = scale - (2.0 * scale) * odd
    r2 = r * r
    sine = -0.00018362251175623582 * r2 + 0.008306273552368303
    sine = sine * r2 - 0.1666482311215342
    sine = sine * r2 + 0.9999966031254778
    cosine = -0.0012711240835350962 * r2 + 0.041487518673719546
    cosine = cosine * r2 - 0.4999123281046797
    cosine = cosine * r2 + 0.9999933132015835
    return sine * (r * sign), cosine * sign


def pair_features(values, freq, scale):
    high, low = two_terms(values)
    freq_high, freq_low = two_terms(freq)
    angles = nn(high, freq_high) + nn(low, freq_high) + nn(high, freq_low)
    sine, cosine = scaled_sine_cosine(angles, scale)
    sine, cosine = sine.astype(BF), cosine.astype(BF)
    feat = freq.shape[1] // 2
    return [
        jnp.concatenate([sine[:, h * feat : (h + 1) * feat], cosine[:, h * feat : (h + 1) * feat]], axis=1)
        for h in (0, 1)
    ]


def own_lanes(shape, half):
    lane = iota(shape, len(shape) - 1)
    return (lane >= LANES // 2) if half else (lane < LANES // 2)


def one_lane(shape, half):
    return iota(shape, len(shape) - 1) == (0 if half else LANES // 2)


def second_lane(shape, half):
    return iota(shape, len(shape) - 1) == (1 if half else LANES // 2 + 1)


def with_ones(values, half, both=False):
    v = values.astype(F32)
    ones = one_lane(v.shape, half) | (both & second_lane(v.shape, half))
    return jnp.where(own_lanes(v.shape, half), v, jnp.where(ones, 1.0, 0.0))


def pack_states(even, odd, decay_even, decay_odd):
    half = LANES // 2
    row = iota(even.shape, 0)
    states = jnp.where(row < half, even, odd).astype(BF)
    extra = iota((EXTRA, even.shape[1]), 0)
    parts = []
    for value in (even[half : half + 1], odd[0:1], decay_even, decay_odd):
        high = value.astype(BF).astype(F32)
        parts += [high, value - high]
    rows = jnp.zeros((EXTRA, even.shape[1]), F32)
    for at, part in enumerate(parts):
        rows = jnp.where(extra == at, part, rows)
    return states, rows.astype(BF)


def extra_row(packed, at):
    at = LANES + 2 * at
    return packed[at : at + 1] + packed[at + 1 : at + 2]


def decays(packed):
    return extra_row(packed, 2), extra_row(packed, 3)


def unpack_states(packed):
    half = LANES // 2
    states = packed[:LANES]
    row = iota(states.shape, 0)
    even = jnp.where(row < half, states, jnp.where(row == half, extra_row(packed, 0), 0.0))
    odd = jnp.where(row >= half, states, jnp.where(row == 0, extra_row(packed, 1), 0.0))
    return even, odd


def join_states(first, second):
    return [
        a + decay * b
        for a, b, decay in zip(unpack_states(first), unpack_states(second), decays(first))
    ]


def as_operand(state, half):
    at = 0 if half else LANES // 2
    norm = state[at : at + 1]
    rest = norm - norm.astype(BF).astype(F32)
    return jnp.where(iota(state.shape, 0) == at + 1, rest, state).astype(BF)


def decay_weights(c_col, c_row, a_row):
    length = c_col.shape[0]
    gap = jnp.minimum(c_col - c_row, 0.0)
    causal = iota((length, length), 0) >= iota((length, length), 1)
    return jnp.where(causal, jnp.exp(gap) * a_row, 0.0)


def lane_sum(v):
    return jnp.sum(v, axis=1, keepdims=True)


def front_kernel(
    x_ref, wqkv_ref, gw_ref, gb_ref, gain_ref, shift_ref, freq_ref,
    n1_ref, v_ref, c_ref, a_ref, crow_ref, arow_ref, pq_ref, pk_ref, st_ref,
):
    heads = freq_ref.shape[0]
    feat = freq_ref.shape[2]
    width = x_ref.shape[2]
    scale = 1.0 / math.sqrt(feat)
    xhat, _ = norm_rows(x_ref[0])
    n1 = (xhat * gain_ref[...] + shift_ref[...]).astype(BF)
    n1_ref[0] = n1
    z = nn(n1, gw_ref[...]) + gb_ref[...]
    e = jnp.exp(-jnp.abs(z))
    log_keep = jnp.minimum(z, 0.0) - jnp.log1p(e)
    inverse = 1.0 / (1.0 + e)
    admit = jnp.where(z > 0.0, e * inverse, inverse)
    c = running_sum(log_keep, False)
    c_ref[0] = c
    a_ref[0] = admit
    crow_ref[0] = jnp.transpose(c)[:heads]
    arow_ref[0] = jnp.transpose(admit)[:heads]
    last = c[c.shape[0] - 1 :]
    tail = jnp.exp(last - c) * admit
    decay = jnp.exp(last)
    for pair in range(heads // 2):
        at = pair * LANES
        freq = pair_frequencies(freq_ref, pair)
        q = nn(n1, wqkv_ref[:, at : at + LANES])
        k = nn(n1, wqkv_ref[:, width + at : width + at + LANES])
        v = nn(n1, wqkv_ref[:, 2 * width + at : 2 * width + at + LANES])
        v_ref[0, :, at : at + LANES] = v
        phi_q = pair_features(q, freq, scale)
        phi_k = pair_features(k, freq, scale)
        states = []
        for half in (0, 1):
            h = 2 * pair + half
            pq_ref[0, h] = phi_q[half]
            pk_ref[0, h] = phi_k[half]
            weighted = jnp.concatenate(two_terms(with_ones(v, half) * tail[:, h : h + 1]), axis=1)
            both = tn(weighted, phi_k[half])
            states.append(both[:LANES] + both[LANES:])
        main, rest = pack_states(
            *states, decay[:, 2 * pair : 2 * pair + 1], decay[:, 2 * pair + 1 : 2 * pair + 2]
        )
        st_ref[0, pair, :LANES] = main
        st_ref[0, pair, LANES:] = rest


def scores_kernel(pq_ref, pk_ref, v_ref, c_ref, crow_ref, arow_ref, p_ref, num_ref):
    heads = pq_ref.shape[1]
    for h in range(heads):
        pair, half = divmod(h, 2)
        v = with_ones(v_ref[0, :, pair * LANES : (pair + 1) * LANES], half)
        weights = decay_weights(c_ref[0, :, h : h + 1], crow_ref[0, h : h + 1], arow_ref[0, h : h + 1])
        p = (nt(pq_ref[0, h], pk_ref[0, h]) * weights).astype(BF)
        p_ref[0, h] = p
        both = nn(p, jnp.concatenate(two_terms(v), axis=1))
        num_ref[0, h] = both[:, :LANES] + both[:, LANES:]


def mix_kernel(
    place_ref, x_ref, got_ref, swapped_ref, partner_ref, pq_ref, c_ref, num_ref, wo_ref, gain_ref, shift_ref,
    full_ref, start_ref, mixed_ref, resid_ref, n2_ref,
):
    heads = pq_ref.shape[1]
    core = place_ref[0]
    mine = pl.program_id(0) == core
    growth = jnp.exp(c_ref[0])
    for pair in range(heads // 2):
        before = jnp.where(mine, got_ref[pair], swapped_ref[pair]).astype(F32)
        partner = partner_ref[0, pair].astype(F32)
        states = [
            jnp.where(core == 0, a, b)
            for a, b in zip(unpack_states(before), join_states(partner, before))
        ]
        none = jnp.zeros((1, 1), F32)
        main, rest = pack_states(*states, none, none)
        start_ref[0, pair, :LANES] = main
        start_ref[0, pair, LANES:] = rest
        mixed = []
        for half in (0, 1):
            h = 2 * pair + half
            full = num_ref[0, h] + growth[:, h : h + 1] * nt(
                pq_ref[0, h], as_operand(states[half], half)
            )
            full_ref[0, h] = full
            at = 0 if half else LANES // 2
            sden = full[:, at : at + 1] + full[:, at + 1 : at + 2]
            mixed.append(full * lax.rsqrt(sden * sden + guard))
        pair_mixed = jnp.where(own_lanes(mixed[0].shape, 0), mixed[0], mixed[1])
        mixed_ref[0, :, pair * LANES : (pair + 1) * LANES] = pair_mixed.astype(BF)
    resid = x_ref[0] + nn(mixed_ref[0], wo_ref[...])
    resid_ref[0] = resid
    xhat, _ = norm_rows(resid)
    n2_ref[0] = (xhat * gain_ref[...] + shift_ref[...]).astype(BF)


def gelu_and_slope(v):
    root = math.sqrt(2.0 / math.pi)
    v2 = v * v
    t = jnp.tanh(v * (root + (root * 0.044715) * v2))
    half = 0.5 * (1.0 + t)
    slope = half + (0.5 * v) * (1.0 - t * t) * (root + (root * 3.0 * 0.044715) * v2)
    return v * half, slope


def feed_kernel(
    n2_ref, og_ref, resid_ref, wi0, wi1, wi2, wi3, wo0, wo1, wo2, wo3,
    out_ref, dn2_ref, keep_ref, send_ref,
):
    n2 = n2_ref[...]
    out_low = og_ref[...].astype(BF)
    total = resid_ref[...]
    dn2 = None
    for block, (wi, wo) in enumerate(((wi0, wo0), (wi1, wo1), (wi2, wo2), (wi3, wo3))):
        pre = nn(n2, wi[...])
        active, slope = gelu_and_slope(pre)
        active = active.astype(BF)
        total = total + nn(active, wo[...])
        pre_grad = (nt(out_low, wo[...]) * slope).astype(BF)
        part = nt(pre_grad, wi[...])
        dn2 = part if dn2 is None else dn2 + part
        inner = tn(n2, pre_grad)
        outer = tn(active, out_low)
        if block < 2:
            keep_ref[2 * block] = inner
            keep_ref[2 * block + 1] = outer
        else:
            send_ref[2 * block - 4] = inner.astype(BF)
            send_ref[2 * block - 3] = outer.astype(BF)
    out_ref[...] = total
    dn2_ref[...] = dn2


def turn_kernel(
    place_ref, og_ref, dn2_ref, resid_ref, gain_ref, wo_ref, mixed_ref, full_ref, pq_ref, c_ref,
    dres_ref, dwo_ref, sums_ref, ng_ref, r_ref, sd_ref,
):
    heads = pq_ref.shape[1]
    step = pl.program_id(0)
    own = place_ref[2]
    xhat, scale = norm_rows(resid_ref[0])
    dn2 = dn2_ref[0]
    dres = og_ref[0] + norm_rows_backward(dn2, xhat, scale, gain_ref[...])
    dres_ref[0] = dres
    low = dres.astype(BF)

    @pl.when(step == 0)
    def _():
        sums_ref[...] = jnp.zeros_like(sums_ref)
        dwo_ref[...] = jnp.zeros_like(dwo_ref)

    sums_ref[2:3] += jnp.sum(dn2 * xhat, axis=0, keepdims=True)
    sums_ref[3:4] += jnp.sum(dn2, axis=0, keepdims=True)
    rows = dwo_ref.shape[1]
    for block in range(4):
        at = pl.multiple_of((own ^ block) * rows, rows)
        dwo_ref[block] += tn(mixed_ref[0, :, pl.ds(at, rows)], low)
    dmixed = nt(low, wo_ref[...])
    c = c_ref[0]
    growth = jnp.exp(c)
    decay = jnp.exp(c[c.shape[0] - 1 :])
    lane = iota(c.shape, 1)
    r_all = jnp.zeros_like(c)
    for pair in range(heads // 2):
        g = dmixed[:, pair * LANES : (pair + 1) * LANES]
        states = []
        for half in (0, 1):
            h = 2 * pair + half
            full = full_ref[0, h]
            at = 0 if half else LANES // 2
            sden = full[:, at : at + 1] + full[:, at + 1 : at + 2]
            inverse = lax.rsqrt(sden * sden + guard)
            inverse2 = inverse * inverse
            mine = own_lanes(g.shape, half)
            dot = lane_sum(jnp.where(mine, g * full, 0.0)) * inverse
            sden_grad = -dot * sden * inverse2
            r_all = jnp.where(lane == h, dot * inverse2 * guard, r_all)
            grads = jnp.where(
                mine, g * inverse, jnp.where(one_lane(g.shape, half), sden_grad, 0.0)
            )
            ng_ref[0, h] = jnp.concatenate(two_terms(grads), axis=1)
            lifted = jnp.concatenate(two_terms(grads * growth[:, h : h + 1]), axis=1)
            both = tn(lifted, pq_ref[0, h])
            states.append(both[:LANES] + both[LANES:])
        main, rest = pack_states(
            *states, decay[:, 2 * pair : 2 * pair + 1], decay[:, 2 * pair + 1 : 2 * pair + 2]
        )
        sd_ref[0, pair, :LANES] = main
        sd_ref[0, pair, LANES:] = rest
    r_ref[0] = r_all


def angle_grads(phi, dphi):
    feat = phi.shape[1] // 2
    phi = phi.astype(F32)
    return phi[:, feat:] * dphi[:, :feat] - phi[:, :feat] * dphi[:, feat:]


def back_kernel(
    place_ref, pq_ref, pk_ref, v_ref, ng_ref, p_ref, c_ref, crow_ref, arow_ref, start_ref, freq_ref, n1_ref, dwo_ref,
    qg_ref, kg_ref, vg_ref, kcol_ref, keep_ref, send_ref, acc_ref,
):
    heads = pq_ref.shape[1]
    step = pl.program_id(0)
    own = place_ref[2]
    c = c_ref[0]
    growth = jnp.exp(c)
    lane = iota(c.shape, 1)
    kcol = jnp.zeros_like(c)
    for pair in range(heads // 2):
        at = pair * LANES
        freq = pair_frequencies(freq_ref, pair).astype(BF)
        states = unpack_states(start_ref[0, pair].astype(F32))
        q_angles, k_angles, v_grads = [], [], []
        for half in (0, 1):
            h = 2 * pair + half
            phi_q, phi_k = pq_ref[0, h], pk_ref[0, h]
            grads = ng_ref[0, h, :, :LANES]
            v = with_ones(v_ref[0, :, at : at + LANES], half)
            weights = decay_weights(c[:, h : h + 1], crow_ref[0, h : h + 1], arow_ref[0, h : h + 1])
            dk = (nt(grads, v.astype(BF)) * weights).astype(BF)
            lifted = (grads.astype(F32) * growth[:, h : h + 1]).astype(BF)
            dphi_q = nn(dk, phi_k) + nn(lifted, states[half].astype(BF))
            q_angles.append(angle_grads(phi_q, dphi_q))
            k_angles.append(angle_grads(phi_k, tn(dk, phi_q)))
            both = tn(p_ref[0, h], ng_ref[0, h])
            dv = both[:, :LANES] + both[:, LANES:]
            v_grads.append(dv)
            kcol = jnp.where(lane == h, lane_sum(v * dv), kcol)
        qg_ref[0, :, at : at + LANES] = nt(jnp.concatenate(q_angles, axis=1).astype(BF), freq).astype(BF)
        kg_ref[0, :, at : at + LANES] = nt(jnp.concatenate(k_angles, axis=1).astype(BF), freq)
        vg_ref[0, :, at : at + LANES] = jnp.where(own_lanes(v_grads[0].shape, 0), v_grads[0], v_grads[1])
    kcol_ref[0] = kcol

    @pl.when(step == 0)
    def _():
        acc_ref[...] = jnp.zeros_like(acc_ref)

    rows = acc_ref.shape[1]
    width = acc_ref.shape[2]
    for block in range(4):
        at = pl.multiple_of((own ^ block) * rows, rows)
        acc_ref[block] += tn(n1_ref[0, :, pl.ds(at, rows)], qg_ref[0])

    @pl.when(step == pl.num_programs(0) - 1)
    def _():
        for block in range(2):
            keep_ref[block, :, :width] = dwo_ref[block]
            keep_ref[block, :, width:] = acc_ref[block]
            send_ref[block, :, :width] = dwo_ref[2 + block].astype(BF)
            send_ref[block, :, width:] = acc_ref[2 + block].astype(BF)


def last_kernel(
    place_ref, got_ref, swapped_ref, partner_ref, st_ref, start_ref, pk_ref, v_ref, c_ref, a_ref, r_ref, kcol_ref,
    qg_ref, kg_ref, vg_ref, freq_ref, n1_ref, x_ref, dres_ref, wqkv_ref, gw_ref, gain_ref, sums2_ref,
    dx_ref, keep_ref, send_ref, sums_ref, acc_ref, kv_ref,
):
    heads = pk_ref.shape[1]
    step = pl.program_id(0)
    core, own = place_ref[0], place_ref[2]
    mine = step == core
    width = x_ref.shape[2]
    c, a = c_ref[0], a_ref[0]
    tail = jnp.exp(c[c.shape[0] - 1 :] - c) * a
    lane = iota(c.shape, 1)
    lane_row = iota((1, c.shape[1]), 1)
    kcol = kcol_ref[0]
    ends = jnp.zeros((1, c.shape[1]), F32)
    for pair in range(heads // 2):
        at = pair * LANES
        freq = pair_frequencies(freq_ref, pair).astype(BF)
        after = jnp.where(mine, got_ref[pair], swapped_ref[pair]).astype(F32)
        partner = partner_ref[0, pair].astype(F32)
        grads = [
            jnp.where(core == 1, a, b)
            for a, b in zip(unpack_states(after), join_states(partner, after))
        ]
        reached = join_states(st_ref[0, pair].astype(F32), start_ref[0, pair].astype(F32))
        k_angles, v_grads = [], []
        for half in (0, 1):
            h = 2 * pair + half
            phi_k = pk_ref[0, h]
            v = with_ones(v_ref[0, :, at : at + LANES], half, True)
            grad_low = as_operand(grads[half], half)
            weight = tail[:, h : h + 1]
            k_angles.append(angle_grads(phi_k, nn(v.astype(BF), grad_low)) * weight)
            dv = nt(phi_k, grad_low) * weight
            v_grads.append(dv)
            kcol = kcol + jnp.where(lane == h, lane_sum(v * dv), 0.0)
            end = jnp.sum(lane_sum(grads[half] * reached[half]), axis=0, keepdims=True)
            ends = jnp.where(lane_row == h, end, ends)
        kg = kg_ref[0, :, at : at + LANES] + nt(jnp.concatenate(k_angles, axis=1).astype(BF), freq)
        vg = vg_ref[0, :, at : at + LANES] + jnp.where(own_lanes(v_grads[0].shape, 0), v_grads[0], v_grads[1])
        kv_ref[:, at : at + LANES] = kg.astype(BF)
        kv_ref[:, width + at : width + at + LANES] = vg.astype(BF)
    keep_grad = running_sum(r_ref[0] - kcol, True) + ends
    logit_grad = a * keep_grad - (1.0 - a) * kcol
    logit_low = logit_grad.astype(BF)
    n1 = n1_ref[0]
    dn1 = (
        nt(qg_ref[0], wqkv_ref[:, :width])
        + nt(kv_ref[...], wqkv_ref[:, width:])
        + nt(logit_low, gw_ref[...])
    )
    xhat, scale = norm_rows(x_ref[0])
    dx_ref[0] = dres_ref[0] + norm_rows_backward(dn1, xhat, scale, gain_ref[...])

    @pl.when(step == 0)
    def _():
        acc_ref[...] = jnp.zeros_like(acc_ref)
        sums_ref[...] = jnp.zeros_like(sums_ref)
        sums_ref[0:8] = sums2_ref[...]

    sums_ref[0:1] += jnp.sum(dn1 * xhat, axis=0, keepdims=True)
    sums_ref[1:2] += jnp.sum(dn1, axis=0, keepdims=True)
    sums_ref[4:5, :LANES] += jnp.sum(logit_grad, axis=0, keepdims=True)
    sums_ref[8 : 8 + heads] += tn(logit_low, n1)[:heads]
    rows = acc_ref.shape[1]
    for block in range(4):
        at = pl.multiple_of((own ^ block) * rows, rows)
        acc_ref[block] += tn(n1_ref[0, :, pl.ds(at, rows)], kv_ref[...])

    @pl.when(step == pl.num_programs(0) - 1)
    def _():
        for block in range(2):
            keep_ref[block] = acc_ref[block]
            send_ref[block] = acc_ref[2 + block].astype(BF)


def chain_kernel(place_ref, me_ref, partner_ref, out_ref, *, reverse):
    core = place_ref[0]
    lead = (core == 0) if reverse else (core == 1)
    for pair in range(out_ref.shape[0]):
        mine, other = me_ref[core, pair].astype(F32), partner_ref[core, pair].astype(F32)
        first = jnp.where(lead, mine, other)
        second = jnp.where(lead, other, mine)
        none = jnp.zeros((1, 1), F32)
        main, rest = pack_states(*join_states(first, second), none, none)
        out_ref[pair, :LANES] = main
        out_ref[pair, LANES:] = rest


def assemble_kernel(place_ref, g1_ref, g2_ref, qkv_ref, wo_ref):
    width = wo_ref.shape[1]
    wo_ref[...] = g1_ref[0, :, :width].astype(F32)
    qkv_ref[:, :width] = g1_ref[0, :, width:].astype(F32)
    qkv_ref[:, width:] = g2_ref[0].astype(F32)


def params():
    return pltpu.CompilerParams(vmem_limit_bytes=VMEM_BYTES)


def whole(array):
    zeros = (0,) * array.ndim
    return pl.BlockSpec(array.shape, lambda *_: zeros)


def per_step(array):
    rest = (0,) * (array.ndim - 1)
    return pl.BlockSpec((1, *array.shape[1:]), lambda s, *_: (s, *rest))


def scalars():
    return pl.BlockSpec(memory_space=pltpu.SMEM)


def shaped(shape, dtype):
    return jax.ShapeDtypeStruct(shape, dtype)


def core_swap(v):
    return jax.tree.map(lambda a: lax.ppermute(a, "mp", [(i, i ^ 1) for i in range(4)]), v)


def chip_swap(v):
    return jax.tree.map(lambda a: lax.ppermute(a, "mp", [(i, i ^ 2) for i in range(4)]), v)


def sum_and_share(v):
    count = lax.axis_size("dp")
    rows = v.shape[0]
    parts = lax.all_to_all(v.astype(BF), "dp", 0, 0, tiled=True)
    total = jnp.sum(parts.reshape(count, rows // count, -1).astype(F32), axis=0).astype(BF)
    copies = jnp.broadcast_to(total[None], (count, *total.shape)).reshape(rows, -1)
    return lax.all_to_all(copies, "dp", 0, 0, tiled=True)


def sum_over_all(keep, send):
    both = keep + core_swap(send).astype(F32)
    mine = both[0] + chip_swap(both[1].astype(BF)).astype(F32)
    mine = sum_and_share(mine)
    pair = jnp.stack([mine, chip_swap(mine)])
    return jnp.concatenate([pair, core_swap(pair)])


def exchange(packed, partner, place, reverse):
    pairs = packed.shape[1]
    total = pl.pallas_call(
        lambda *refs: chain_kernel(*refs, reverse=reverse),
        out_shape=shaped(packed.shape[1:], BF),
        in_specs=[scalars(), whole(packed), whole(partner)],
        out_specs=pl.BlockSpec(packed.shape[1:], lambda *_: (0, 0, 0)),
        compiler_params=params(),
        name="chain",
    )(place, packed, partner)
    way = [(2, 0), (3, 1)] if reverse else [(0, 2), (1, 3)]
    got = lax.ppermute(total, "mp", way)
    return got, core_swap(got)


def per_device(
    layer_input,
    qkv_weight,
    gate_weight,
    gate_bias,
    out_weight,
    inner_weight,
    outer_weight,
    leading_norm_gain,
    leading_norm_bias,
    trailing_norm_gain,
    trailing_norm_bias,
    random_features,
    output_grad,
):
    seqs, length, width = layer_input.shape
    heads, head, feat = random_features.shape
    pairs = heads // 2
    count = seqs * length
    spot = lax.axis_index("mp")
    core, chip = spot % 2, spot // 2
    place = jnp.stack([core, chip, 2 * core + chip]).astype(jnp.int32)
    gate_wide = jnp.pad(gate_weight, ((0, 0), (0, LANES - heads)))
    bias_wide = jnp.pad(gate_bias, (0, LANES - heads)).reshape(1, LANES)
    gain1, shift1 = leading_norm_gain.reshape(1, width), leading_norm_bias.reshape(1, width)
    gain2, shift2 = trailing_norm_gain.reshape(1, width), trailing_norm_bias.reshape(1, width)

    inner_chip, outer_chip = chip_swap(inner_weight), chip_swap(outer_weight)
    inner_core, outer_core = core_swap(inner_weight), core_swap(outer_weight)
    inner_both, outer_both = core_swap(inner_chip), core_swap(outer_chip)

    front_in = (layer_input, qkv_weight, gate_wide, bias_wide, gain1, shift1, random_features)
    front_out = (
        shaped((seqs, length, width), BF),
        shaped((seqs, length, width), F32),
        shaped((seqs, length, LANES), F32),
        shaped((seqs, length, LANES), F32),
        shaped((seqs, heads, length), F32),
        shaped((seqs, heads, length), F32),
        shaped((seqs, heads, length, 2 * feat), BF),
        shaped((seqs, heads, length, 2 * feat), BF),
        shaped((seqs, pairs, LANES + EXTRA, 2 * feat), BF),
    )
    normed1, values, c, admit, c_row, a_row, phi_q, phi_k, packed = pl.pallas_call(
        front_kernel,
        grid=(seqs,),
        out_shape=front_out,
        in_specs=[per_step(layer_input)] + [whole(a) for a in front_in[1:]],
        out_specs=[per_step(a) for a in front_out],
        compiler_params=params(),
        name="front",
    )(*front_in)

    partner = core_swap(packed)
    got, swapped = exchange(packed, partner, place, False)

    scores_in = (phi_q, phi_k, values, c, c_row, a_row)
    scores_out = (
        shaped((seqs, heads, length, length), BF),
        shaped((seqs, heads, length, LANES), F32),
    )
    scores, num = pl.pallas_call(
        scores_kernel,
        grid=(seqs,),
        out_shape=scores_out,
        in_specs=[per_step(a) for a in scores_in],
        out_specs=[per_step(a) for a in scores_out],
        compiler_params=params(),
        name="scores",
    )(*scores_in)

    mix_in = (place, layer_input, got, swapped, partner, phi_q, c, num, out_weight, gain2, shift2)
    mix_out = (
        shaped((seqs, heads, length, LANES), F32),
        shaped(packed.shape, BF),
        shaped((seqs, length, width), BF),
        shaped((seqs, length, width), F32),
        shaped((seqs, length, width), BF),
    )
    full, start, mixed_low, resid, normed2 = pl.pallas_call(
        mix_kernel,
        grid=(seqs,),
        out_shape=mix_out,
        in_specs=[
            scalars(), per_step(layer_input), whole(got), whole(swapped), per_step(partner), per_step(phi_q),
            per_step(c), per_step(num), whole(out_weight), whole(gain2), whole(shift2),
        ],
        out_specs=[per_step(a) for a in mix_out],
        compiler_params=params(),
        name="mix",
    )(*mix_in)

    hidden = inner_weight.shape[1]
    feed_in = (
        normed2.reshape(count, width), output_grad.reshape(count, width), resid.reshape(count, width),
        inner_weight, inner_chip, inner_core, inner_both, outer_weight, outer_chip, outer_core, outer_both,
    )
    feed_out = (
        shaped((count, width), F32),
        shaped((count, width), F32),
        shaped((4, width, hidden), F32),
        shaped((4, width, hidden), BF),
    )
    layer_out, dn2, ff_keep, ff_send = pl.pallas_call(
        feed_kernel,
        out_shape=feed_out,
        in_specs=[whole(a) for a in feed_in],
        out_specs=[whole(a) for a in feed_out],
        compiler_params=params(),
        name="feed",
    )(*feed_in)

    ff_both = ff_keep + core_swap(ff_send).astype(F32)
    ff_mine = ff_both[:2] + chip_swap(ff_both[2:].astype(BF)).astype(F32)
    ff_total = sum_and_share(ff_mine.reshape(2 * width, hidden)).reshape(2, width, hidden)

    dn2 = dn2.reshape(seqs, length, width)
    turn_in = (place, output_grad, dn2, resid, gain2, out_weight, mixed_low, full, phi_q, c)
    turn_out = (
        shaped((seqs, length, width), F32),
        shaped((4, width // 4, width), F32),
        shaped((8, width), F32),
        shaped((seqs, heads, length, 2 * LANES), BF),
        shaped((seqs, length, LANES), F32),
        shaped(packed.shape, BF),
    )
    dres, dwo, sums2, num_grads, r, packed_grads = pl.pallas_call(
        turn_kernel,
        grid=(seqs,),
        out_shape=turn_out,
        in_specs=[
            scalars(), per_step(output_grad), per_step(dn2), per_step(resid), whole(gain2), whole(out_weight),
            per_step(mixed_low), per_step(full), per_step(phi_q), per_step(c),
        ],
        out_specs=[
            per_step(turn_out[0]), whole(turn_out[1]), whole(turn_out[2]), per_step(turn_out[3]), per_step(turn_out[4]),
            per_step(turn_out[5]),
        ],
        compiler_params=params(),
        name="turn",
    )(*turn_in)

    partner_grads = core_swap(packed_grads)
    got_grads, swapped_grads = exchange(packed_grads, partner_grads, place, True)

    back_in = (
        place, phi_q, phi_k, values, num_grads, scores, c, c_row, a_row, start, random_features, normed1, dwo,
    )
    back_out = (
        shaped((seqs, length, width), BF),
        shaped((seqs, length, width), F32),
        shaped((seqs, length, width), F32),
        shaped((seqs, length, LANES), F32),
        shaped((2, width // 4, 2 * width), F32),
        shaped((2, width // 4, 2 * width), BF),
    )
    q_grad, k_part, v_part, k_col, keep1, send1 = pl.pallas_call(
        back_kernel,
        grid=(seqs,),
        out_shape=back_out,
        in_specs=[scalars()] + [per_step(a) for a in back_in[1:10]] + [
            whole(random_features), per_step(normed1), whole(dwo),
        ],
        out_specs=[per_step(a) for a in back_out[:4]] + [whole(a) for a in back_out[4:]],
        scratch_shapes=[pltpu.VMEM((4, width // 4, width), F32)],
        compiler_params=params(),
        name="back",
    )(*back_in)
    blocks1 = sum_over_all(keep1, send1)

    last_in = (
        place, got_grads, swapped_grads, partner_grads, packed, start, phi_k, values, c, admit, r, k_col,
        q_grad, k_part, v_part, random_features, normed1, layer_input, dres, qkv_weight, gate_wide, gain1, sums2,
    )
    last_out = (
        shaped((seqs, length, width), F32),
        shaped((2, width // 4, 2 * width), F32),
        shaped((2, width // 4, 2 * width), BF),
        shaped((16, width), F32),
    )
    dx, keep2, send2, sums = pl.pallas_call(
        last_kernel,
        grid=(seqs,),
        out_shape=last_out,
        in_specs=[scalars(), whole(got_grads), whole(swapped_grads)]
        + [per_step(a) for a in last_in[3:15]]
        + [whole(random_features)]
        + [per_step(a) for a in last_in[16:19]]
        + [whole(a) for a in last_in[19:]],
        out_specs=[per_step(last_out[0])] + [whole(a) for a in last_out[1:]],
        scratch_shapes=[
            pltpu.VMEM((4, width // 4, 2 * width), F32),
            pltpu.VMEM((length, 2 * width), BF),
        ],
        compiler_params=params(),
        name="last",
    )(*last_in)
    blocks2 = sum_over_all(keep2, send2)
    sums = sums + core_swap(sums)
    sums = sums + chip_swap(sums)
    n_dp = lax.axis_size("dp")
    bit = 1
    while bit < n_dp:
        sums = sums + lax.ppermute(sums, "dp", [(i, i ^ bit) for i in range(n_dp)])
        bit *= 2

    rows = width // 4
    qkv_grad, wo_grad = pl.pallas_call(
        assemble_kernel,
        grid_spec=pltpu.PrefetchScalarGridSpec(
            num_scalar_prefetch=1,
            grid=(4,),
            in_specs=[
                pl.BlockSpec((1, rows, 2 * width), lambda i, p: (i ^ p[2], 0, 0)),
                pl.BlockSpec((1, rows, 2 * width), lambda i, p: (i ^ p[2], 0, 0)),
            ],
            out_specs=[
                pl.BlockSpec((rows, 3 * width), lambda i, p: (i, 0)),
                pl.BlockSpec((rows, width), lambda i, p: (i, 0)),
            ],
        ),
        out_shape=(shaped((width, 3 * width), F32), shaped((width, width), F32)),
        compiler_params=params(),
        name="assemble",
    )(place, blocks1, blocks2)
    return (
        layer_out.reshape(seqs, length, width),
        dx,
        qkv_grad,
        jnp.transpose(sums[8 : 8 + heads]),
        sums[4, :heads],
        wo_grad,
        ff_total[0].astype(F32),
        ff_total[1].astype(F32),
        sums[0],
        sums[1],
        sums[2],
        sums[3],
    )


def solution(mesh):
    in_specs = (
        P("dp", "mp", None),
        P(),
        P(),
        P(),
        P(),
        P(None, "mp"),
        P("mp", None),
        P(),
        P(),
        P(),
        P(),
        P(),
        P("dp", "mp", None),
    )
    out_specs = (
        P("dp", "mp", None),
        P("dp", "mp", None),
        P(),
        P(),
        P(),
        P(),
        P(None, "mp"),
        P("mp", None),
        P(),
        P(),
        P(),
        P(),
    )
    return jax.shard_map(
        per_device, mesh=mesh, in_specs=in_specs, out_specs=out_specs, check_vma=False
    )
```

time: 636 us -> 275 us (0.43); the launches traced: 626 us -> 274 us
  matrix products: 174 us -> 0 us
  waiting for transfers between devices: 209 us -> 118 us
  Pallas kernels: 0 us -> 81.8 us
  local copies, waits for them, and re-layouts: 92.7 us -> 12.9 us
  other arithmetic: 74.6 us -> 12.7 us
  blocking collectives: 57.9 us -> 0 us
  starting transfers between devices: 0.97 us -> 47.5 us
  between operations: 15.5 us -> 1.03 us
    dot_general x33 -> x0, matrix products: 174 us -> none  [the longest x4 31.3 us: features(): jnp.einsum('...hd,hdf->...hf', values, frequencies, precision=exact)]
    psum x2 -> x0, waiting for transfers between devices: 90.6 us -> none  [the longest x1 90.6 us: per_device(): lax.psum((qkv_part, out_weight_part, gate_weight_part, gate_bias_part, no...]
    pallas_call x0 -> x10, Pallas kernels: none -> 81.8 us  [the longest x1 13.3 us: per_device(): pl.pallas_call(front_kernel, grid=(seqs,), out_shape=front_out, in_specs=...]
    ppermute x0 -> x27, waiting for transfers between devices: none -> 75.5 us  [the longest x8 44.6 us: chip_swap(): lax.ppermute(a, 'mp', [(i, i ^ 2) for i in range(4)])]
    reduce_scatter x2 -> x0, waiting for transfers between devices: 69.6 us -> none  [the longest x1 39.1 us: per_device(): lax.psum_scatter(contract(pre_grad, inner_weight, 1, 1), 'mp', scatter_di...]
    all_gather x4 -> x0, waiting for transfers between devices: 48.9 us -> none  [the longest x1 41.7 us: per_device(): gathered = lax.all_gather(trailing_normalized, 'mp', axis=0, tiled=True)]
    all_to_all x0 -> x6, waiting for transfers between devices: none -> 42.6 us  [the longest x3 33.7 us: sum_and_share(): parts = lax.all_to_all(v.astype(BF), 'dp', 0, 0, tiled=True)]
    psum x1 -> x0, blocking collectives: 40.2 us -> none  [per_device(): lax.psum((qkv_part, out_weight_part, gate_weight_part, gate_bias_part, no...]
  transfers between devices with their start and end apart: 8 -> 33, of which waited for: 5 -> 16; matrix products, arithmetic and copies ran while one was open for 38% -> 5% of each run, Pallas kernels for 0% -> 20%
where the time goes in v1:
time: 275 us; the launch traced here: 274 us
  waiting for transfers between devices  118 us (43%)
  Pallas kernels  81.8 us (30%)
  starting transfers between devices  47.5 us (17%)
  local copies, waits for them, and re-layouts  12.9 us (5%)
  other arithmetic  12.7 us (5%)
    ppermute x8, waiting for transfers between devices, chip_swap(): lax.ppermute(a, 'mp', [(i, i ^ 2) for i in range(4)])  44.6 us
    all_to_all x3, waiting for transfers between devices, sum_and_share(): parts = lax.all_to_all(v.astype(BF), 'dp', 0, 0, tiled=True)  33.7 us
    ppermute x2, waiting for transfers between devices, exchange(): got = lax.ppermute(total, 'mp', way)  15.3 us
    all_to_all x3, starting transfers between devices, sum_and_share(): parts = lax.all_to_all(v.astype(BF), 'dp', 0, 0, tiled=True)  15.1 us
    pallas_call x1, Pallas kernels, per_device(): pl.pallas_call(front_kernel, grid=(seqs,), out_shape=front_out, in_specs=...  13.3 us
    pallas_call x1, Pallas kernels, per_device(): pl.pallas_call(feed_kernel, out_shape=feed_out, in_specs=[whole(a) for a...  13.1 us
    ppermute x3, waiting for transfers between devices, per_device(): sums = sums + lax.ppermute(sums, 'dp', [(i, i ^ bit) for i in range(n_dp)])  12.8 us
    pallas_call x1, Pallas kernels, per_device(): pl.pallas_call(turn_kernel, grid=(seqs,), out_shape=turn_out, in_specs=[s...  11.8 us
  transfers between devices with their start and end apart: 33, of which 16 were waited for; matrix products, arithmetic and copies ran while one was open for 5% of the time, Pallas kernels for 20%

profile of v1, /device:TPU:0, one launch (start us, length us, event | category | flops | bytes accessed | tf_op | source)
XLA Modules:
  0.0 273.9 jit_solution(9682511976136022335)
XLA Ops:
  0.7 0.9 copy.25
  1.6 1.2 pad_bitcast_fusion.gb_ref
  3.5 13.3 %front.1 = (bf16[2,256,512]{2,1,0:T(8,128)(2,1)}, f32[2,256,512]{2,1,0:T(8,128)}, f32[2,256,128]{2,1,0:T(8,128)}, f32[2,256,128]{2,1,0:T(8,128)}, f32[2,8,256]{2...) custom-call(f32[2,256,512]{2,1,0:T(8,128)} %x_ref.5, ...), custom_call_target="tpu_custom_call" | custom-call | tf_op jit(solution)/shard_map/front/pallas_call | solution.py:638
  17.3 2.6 collective-permute-start.3
  20.6 0.8 copy-done.1
  21.4 2.1 chain.2
  23.5 4.0 %collective-permute-start.1 = (bf16[4,144,256]{2,1,0:T(8,128)(2,1)}, bf16[4,144,256]{2,1,0:T(8,128)(2,1)S(1)}, u32[]{:S(2)}, u32[]{:S(2)}) collective-permute-start(bf16[4,144,256]{2,1,0:T(8,128)(2,1)} %chain.2), channel_id=1, source_target_pairs={{0,2},{1,3},{4,6},{5,7},{8,10},{9,11},{12,14},{13,15},{16,18},{17,... | collective-permute-start | bytes 884744 | tf_op jit(solution)/shard_map/ppermute | solution.py:591
  28.1 4.5 %collective-permute-done.3.wi1 = bf16[512,512]{1,0:T(8,128)(2,1)S(1)} collective-permute-done((bf16[512,512]{1,0:T(8,128)(2,1)S(1)}, bf16[512,512]{1,0:T(8,128)(2,1)S(1)}, u32[]{:S(2)}, u32[]{:S(2)}) %collective-permute-start.3) | collective-permute-done | bytes 524320 | tf_op jit(solution)/shard_map/ppermute | solution.py:560
  32.7 11.0 %collective-permute-done.6.wo1 = bf16[512,512]{1,0:T(8,128)(2,1)S(1)} collective-permute-done((bf16[512,512]{1,0:T(8,128)(2,1)S(1)}, bf16[512,512]{1,0:T(8,128)(2,1)S(1)}, u32[]{:S(2)}, u32[]{:S(2)}) %collective-permute-start.6) | collective-permute-done | bytes 524320 | tf_op jit(solution)/shard_map/ppermute | solution.py:560
  43.6 5.7 %collective-permute-done.1.got_ref = bf16[4,144,256]{2,1,0:T(8,128)(2,1)S(1)} collective-permute-done((bf16[4,144,256]{2,1,0:T(8,128)(2,1)}, bf16[4,144,256]{2,1,0:T(8,128)(2,1)S(1)}, u32[]{:S(2)}, u32[]{:S(2)}) %collective-permute-start.1) | collective-permute-done | bytes 294944 | tf_op jit(solution)/shard_map/ppermute | solution.py:591
  49.3 5.2 %scores.1 = (bf16[2,8,256,256]{3,2,1,0:T(8,128)(2,1)}, f32[2,8,256,128]{3,2,1,0:T(8,128)}) custom-call(bf16[2,8,256,256]{3,2,1,0:T(8,128)(2,1)} %get-tuple-element.51.pq_ref, bf16[2,8,256,256]{3,2,1,0:T(8,128)(2,1)} %get-tuple-element.53.pk_ref, f32[2,256,512]{2,1,0:T(8,128)} %get-tuple-element.54.v_ref, f32[2,256,128]{2,1,0:T(8,128)} %get-tuple-element.52.c_ref, ...), custom_call_target="tpu_custom_call" | custom-call | tf_op jit(solution)/shard_map/scores/pallas_call | solution.py:656
  55.3 7.4 %mix.1 = (f32[2,8,256,128]{3,2,1,0:T(8,128)}, bf16[2,4,144,256]{3,2,1,0:T(8,128)(2,1)}, bf16[2,256,512]{2,1,0:T(8,128)(2,1)}, f32[2,256,512]{2,1,0:T(8,128)}, bf16[2,256,512]{2,1,0:T(8,128)(2,1)}) custom-call(s32[3]{0:T(128)} %pad_add_fusion.refs_0_.place_ref, f32[2,256,512]{2,1,0:T(8,128)} %x_ref.5, bf16[4,144,256]{2,1,0:T(8,128)(2,1)} %copy-done.14, ...), custom_call_target="tpu_custom_call" | custom-call | tf_op jit(solution)/shard_map/mix/pallas_call | solution.py:674
  64.0 13.1 %feed.1 = (f32[512,512]{1,0:T(8,128)}, f32[512,512]{1,0:T(8,128)}, f32[4,512,512]{2,1,0:T(8,128)}, bf16[4,512,512]{2,1,0:T(8,128)(2,1)}) custom-call(bf16[512,512]{1,0:T(8,128)(2,1)} %bitcast.66, f32[512,512]{1,0:T(8,128)} %bitcast.53, f32[512,512]{1,0:T(8,128)} %bitcast.54, bf16[512,512]{1,0:T(8,128)(2,1)} %wi0.1, bf16[512,512]{1,0:T(8,128)(2,1)} %copy-done.7, ...), custom_call_target="tpu_custom_call" | custom-call | tf_op jit(solution)/shard_map/feed/pallas_call | solution.py:698
  77.5 11.8 %turn.1 = (f32[2,256,512]{2,1,0:T(8,128)}, f32[4,128,512]{2,1,0:T(8,128)}, f32[8,512]{1,0:T(8,128)}, bf16[2,8,256,256]{3,2,1,0:T(8,128)(2,1)}, f32[2,256,128]{2,1,0:T(8,128)}, /*index=5*/bf16[2,4,144,256]{3,2,1,0:T(8,128)(2,1)}) custom-call(s32[3]{0:T(128)} %pad_add_fusion.refs_0_.place_ref, f32[2,256,512]{2,1,0:T(8,128)} %og_ref.1, ...), custom_call_target="tpu_custom_call" | custom-call | tf_op jit(solution)/shard_map/turn/pallas_call | solution.py:721
  89.4 11.8 %back.1 = (bf16[2,256,512]{2,1,0:T(8,128)(2,1)}, f32[2,256,512]{2,1,0:T(8,128)}, f32[2,256,512]{2,1,0:T(8,128)}, f32[2,256,128]{2,1,0:T(8,128)}, f32[2,128,1024]{2,1,0:T(8,128)}, /*index=5*/bf16[2,128,1024]{2,1,0:T(8,128)(2,1)}) custom-call(s32[3]{0:T(128)} %pad_add_fusion.refs_0_.place_ref, bf16[2,8,256,256]{3,2,1,0:T(8,128)(2,1)} %get-tuple-element.51.pq_ref, ...), custom_call_target="tpu_custom_call" | custom-call | tf_op jit(solution)/shard_map/back/pallas_call | solution.py:751
  102.5 2.1 chain.3
  104.6 1.3 collective-permute-start.10
  106.1 9.6 %collective-permute-done.10.got_ref = bf16[4,144,256]{2,1,0:T(8,128)(2,1)S(1)} collective-permute-done((bf16[4,144,256]{2,1,0:T(8,128)(2,1)}, bf16[4,144,256]{2,1,0:T(8,128)(2,1)S(1)}, u32[]{:S(2)}, u32[]{:S(2)}) %collective-permute-start.10) | collective-permute-done | bytes 294944 | tf_op jit(solution)/shard_map/ppermute | solution.py:591
  115.9 1.5 collective-permute-done.11.swapped_ref
  118.1 10.2 %last.1 = (f32[2,256,512]{2,1,0:T(8,128)}, f32[2,128,1024]{2,1,0:T(8,128)}, bf16[2,128,1024]{2,1,0:T(8,128)(2,1)}, f32[16,512]{1,0:T(8,128)}) custom-call(s32[3]{0:T(128)} %pad_add_fusion.refs_0_.place_ref, bf16[4,144,256]{2,1,0:T(8,128)(2,1)} %copy-done.13, bf16[4,144,256]{2,1,0:T(8,128)(2,1)} %copy-done.15, bf16[2,4,144,256]{3,2,1,0:T(8,128)(2,1)} %copy-done.2, ...), custom_call_target="tpu_custom_call" | custom-call | tf_op jit(solution)/shard_map/last/pallas_call | solution.py:775
  129.2 5.9 %all-to-all-start = ((bf16[8,16,1024]{2,1,0:T(8,128)(2,1)}), bf16[8,16,1024]{2,1,0:T(8,128)(2,1)S(1)}, u32[]{:S(2)}, u32[]{:S(2)}) async-start(bf16[8,16,1024]{2,1,0:T(8,128)(2,1)} %bitcast.15), calls=%async_computation | async-start | bytes 524288 | tf_op jit(solution)/shard_map/all_to_all | solution.py:566
  135.1 2.9 %convert_add_fusion = f32[4,512,512]{2,1,0:T(8,128)S(1)} fusion(f32[4,512,512]{2,1,0:T(8,128)} %get-tuple-element.86, bf16[4,512,512]{2,1,0:T(8,128)(2,1)S(1)} %collective-permute-done.25), kind=kLoop, calls=%fused_computation | loop fusion | flops 2097152 | bytes 10485760 | tf_op jit(solution)/shard_map/add | solution.py:707
  138.9 1.2 copy-done.3
  140.9 3.6 %all-to-all-done = bf16[8,16,1024]{2,1,0:T(8,128)(2,1)S(1)} async-done(((bf16[8,16,1024]{2,1,0:T(8,128)(2,1)}), bf16[8,16,1024]{2,1,0:T(8,128)(2,1)S(1)}, u32[]{:S(2)}, u32[]{:S(2)}) %all-to-all-start) | async-done | bytes 262176 | tf_op jit(solution)/shard_map/all_to_all | solution.py:566
  145.3 3.6 %all-to-all-start.1 = ((bf16[8,16,1024]{2,1,0:T(8,128)(2,1)}), bf16[8,16,1024]{2,1,0:T(8,128)(2,1)S(1)}, u32[]{:S(2)}, u32[]{:S(2)}) async-start(bf16[8,16,1024]{2,1,0:T(8,128)(2,1)} %broadcast_in_dim.6), calls=%async_computation.1 | async-start | bytes 524288 | tf_op jit(solution)/shard_map/all_to_all | solution.py:569
  148.9 20.1 %collective-permute-done.17 = bf16[128,1024]{1,0:T(8,128)(2,1)S(1)} collective-permute-done((bf16[128,1024]{1,0:T(8,128)(2,1)S(1)}, bf16[128,1024]{1,0:T(8,128)(2,1)S(1)}, u32[]{:S(2)}, u32[]{:S(2)}) %collective-permute-start.17) | collective-permute-done | bytes 262176 | tf_op jit(solution)/shard_map/ppermute | solution.py:560
  169.8 5.7 %all-to-all-start.2 = ((bf16[8,16,1024]{2,1,0:T(8,128)(2,1)}), bf16[8,16,1024]{2,1,0:T(8,128)(2,1)S(1)}, u32[]{:S(2)}, u32[]{:S(2)}) async-start(bf16[8,16,1024]{2,1,0:T(8,128)(2,1)} %bitcast.21), calls=%async_computation.2 | async-start | bytes 524288 | tf_op jit(solution)/shard_map/all_to_all | solution.py:566
  175.5 3.2 %fusion = bf16[2,512,512]{2,1,0:T(8,128)(2,1)} fusion(f32[4,512,512]{2,1,0:T(8,128)} %copy-done, bf16[2,512,512]{2,1,0:T(8,128)(2,1)} %collective-permute-done.26), kind=kLoop, calls=%fused_computation.3 | loop fusion | flops 1572864 | bytes 4194304 | tf_op jit(solution)/shard_map/convert_element_type | solution.py:566
  178.7 5.0 %all-to-all-done.2 = bf16[8,16,1024]{2,1,0:T(8,128)(2,1)S(1)} async-done(((bf16[8,16,1024]{2,1,0:T(8,128)(2,1)}), bf16[8,16,1024]{2,1,0:T(8,128)(2,1)S(1)}, u32[]{:S(2)}, u32[]{:S(2)}) %all-to-all-start.2) | async-done | bytes 262176 | tf_op jit(solution)/shard_map/all_to_all | solution.py:566
  183.7 3.6 %all-to-all-start.4 = ((bf16[8,128,512]{2,1,0:T(8,128)(2,1)}), bf16[8,128,512]{2,1,0:T(8,128)(2,1)S(1)}, u32[]{:S(2)}, u32[]{:S(2)}) async-start(bf16[8,128,512]{2,1,0:T(8,128)(2,1)} %bitcast.27), calls=%async_computation.4 | async-start | bytes 2097152 | tf_op jit(solution)/shard_map/all_to_all | solution.py:566
  187.3 25.0 %all-to-all-done.4 = bf16[8,128,512]{2,1,0:T(8,128)(2,1)S(1)} async-done(((bf16[8,128,512]{2,1,0:T(8,128)(2,1)}), bf16[8,128,512]{2,1,0:T(8,128)(2,1)S(1)}, u32[]{:S(2)}, u32[]{:S(2)}) %all-to-all-start.4) | async-done | bytes 1048608 | tf_op jit(solution)/shard_map/all_to_all | solution.py:566
  213.1 3.4 %all-to-all-start.3 = ((bf16[8,16,1024]{2,1,0:T(8,128)(2,1)}), bf16[8,16,1024]{2,1,0:T(8,128)(2,1)S(1)}, u32[]{:S(2)}, u32[]{:S(2)}) async-start(bf16[8,16,1024]{2,1,0:T(8,128)(2,1)} %broadcast_in_dim.7), calls=%async_computation.3 | async-start | bytes 524288 | tf_op jit(solution)/shard_map/all_to_all | solution.py:569
  216.7 8.9 %all-to-all-done.3 = bf16[8,16,1024]{2,1,0:T(8,128)(2,1)S(1)} async-done(((bf16[8,16,1024]{2,1,0:T(8,128)(2,1)}), bf16[8,16,1024]{2,1,0:T(8,128)(2,1)S(1)}, u32[]{:S(2)}, u32[]{:S(2)}) %all-to-all-start.3) | async-done | bytes 262176 | tf_op jit(solution)/shard_map/all_to_all | solution.py:569
  225.6 1.1 broadcast_in_dim.8
  226.7 3.6 %all-to-all-start.5 = ((bf16[8,128,512]{2,1,0:T(8,128)(2,1)}), bf16[8,128,512]{2,1,0:T(8,128)(2,1)S(1)}, u32[]{:S(2)}, u32[]{:S(2)}) async-start(bf16[8,128,512]{2,1,0:T(8,128)(2,1)} %broadcast_in_dim.8), calls=%async_computation.5 | async-start | bytes 2097152 | tf_op jit(solution)/shard_map/all_to_all | solution.py:569
  230.3 1.2 collective-permute-done.20
  232.0 3.5 %collective-permute-done.21 = f32[16,512]{1,0:T(8,128)S(1)} collective-permute-done((f32[16,512]{1,0:T(8,128)S(1)}, f32[16,512]{1,0:T(8,128)S(1)}, u32[]{:S(2)}, u32[]{:S(2)}) %collective-permute-start.21) | collective-permute-done | bytes 32800 | tf_op jit(solution)/shard_map/ppermute | solution.py:560
  235.5 2.0 collective-permute-start.22
  237.4 2.2 collective-permute-done.22
  239.6 1.8 collective-permute-start.23
  241.8 5.8 %collective-permute-done.23 = f32[16,512]{1,0:T(8,128)S(1)} collective-permute-done((f32[16,512]{1,0:T(8,128)S(1)}, f32[16,512]{1,0:T(8,128)S(1)}, u32[]{:S(2)}, u32[]{:S(2)}) %collective-permute-start.23) | collective-permute-done | bytes 32800 | tf_op jit(solution)/shard_map/ppermute | solution.py:798
  247.6 4.8 %collective-permute-start.24 = (f32[16,512]{1,0:T(8,128)S(1)}, f32[16,512]{1,0:T(8,128)S(1)}, u32[]{:S(2)}, u32[]{:S(2)}) collective-permute-start(f32[16,512]{1,0:T(8,128)S(1)} %add.54), channel_id=1, source_target_pairs={{0,16},{4,20},{8,24},{12,28},{16,0},{20,4},{24,8},{28,12},{1,17},{... | collective-permute-start | bytes 98312 | tf_op jit(solution)/shard_map/ppermute | solution.py:798
  252.4 4.8 %collective-permute-done.24 = f32[16,512]{1,0:T(8,128)S(1)} collective-permute-done((f32[16,512]{1,0:T(8,128)S(1)}, f32[16,512]{1,0:T(8,128)S(1)}, u32[]{:S(2)}, u32[]{:S(2)}) %collective-permute-start.24) | collective-permute-done | bytes 32800 | tf_op jit(solution)/shard_map/ppermute | solution.py:798
  258.4 5.6 %collective-permute-done.18 = bf16[128,1024]{1,0:T(8,128)(2,1)S(1)} collective-permute-done((bf16[128,1024]{1,0:T(8,128)(2,1)S(1)}, bf16[128,1024]{1,0:T(8,128)(2,1)S(1)}, u32[]{:S(2)}, u32[]{:S(2)}) %collective-permute-start.18) | collective-permute-done | bytes 262176 | tf_op jit(solution)/shard_map/ppermute | solution.py:560
  265.2 1.1 pad_maximum_fusion.g1_ref
  266.3 1.1 pad_maximum_fusion.1.g2_ref
  267.4 4.8 %assemble.1 = (f32[512,1536]{1,0:T(8,128)}, f32[512,512]{1,0:T(8,128)}) custom-call(s32[3]{0:T(128)} %pad_add_fusion.refs_0_.place_ref, bf16[4,128,1024]{2,1,0:T(8,128)(2,1)} %pad_maximum_fusion.g1_ref, bf16[4,128,1024]{2,1,0:T(8,128)(2,1)} %pad_maximum_fusion.1.g2_ref), custom_call_target="tpu_custom_call" | custom-call | tf_op jit(solution)/shard_map/assemble/pallas_call | solution.py:802
  272.3 1.7 bitcast_convert_fusion
  (97 shorter events, 15.9 us)
Async XLA Ops:
  0.6 16.7 %copy-start.5 = (bf16[512,512]{1,0:T(8,128)(2,1)S(1)}, bf16[512,512]{1,0:T(8,128)(2,1)}, u32[]{:S(2)}) copy-start(bf16[512,512]{1,0:T(8,128)(2,1)} %wi0.1) | copy-start | bytes 1572868
  0.7 19.2 %copy-start.6 = (bf16[512,512]{1,0:T(8,128)(2,1)S(1)}, bf16[512,512]{1,0:T(8,128)(2,1)}, u32[]{:S(2)}) copy-start(bf16[512,512]{1,0:T(8,128)(2,1)} %wo0.1) | copy-start | bytes 1572868
  16.8 3.8 %collective-permute-start = (bf16[2,4,144,256]{3,2,1,0:T(8,128)(2,1)}, bf16[2,4,144,256]{3,2,1,0:T(8,128)(2,1)S(1)}, u32[]{:S(2)}, u32[]{:S(2)}) collective-permute-start(bf16[2,4,144,256]{3,2,1,0:T(8,128)(2,1)} %get-tuple-element.50.refs_1_.st_ref), channel_id=1, source_target_pairs={{0,1},{1,0},{2,3},{3,2},{4,5},{5,4},{6,7},{7,6},{8,9},{9,8},{10,11... | collective-permute-start | bytes 1769480 | tf_op jit(solution)/shard_map/ppermute | solution.py:556
  17.3 15.3 %collective-permute-start.3 = (bf16[512,512]{1,0:T(8,128)(2,1)S(1)}, bf16[512,512]{1,0:T(8,128)(2,1)S(1)}, u32[]{:S(2)}, u32[]{:S(2)}) collective-permute-start(bf16[512,512]{1,0:T(8,128)(2,1)S(1)} %copy-done.5), channel_id=1, source_target_pairs={{0,2},{1,3},{2,0},{3,1},{4,6},{5,7},{6,4},{7,5},{8,10},{9,11},{10,... | collective-permute-start | bytes 1572872 | tf_op jit(solution)/shard_map/ppermute | solution.py:560
  19.9 23.7 %collective-permute-start.6 = (bf16[512,512]{1,0:T(8,128)(2,1)S(1)}, bf16[512,512]{1,0:T(8,128)(2,1)S(1)}, u32[]{:S(2)}, u32[]{:S(2)}) collective-permute-start(bf16[512,512]{1,0:T(8,128)(2,1)S(1)} %copy-done.6), channel_id=1, source_target_pairs={{0,2},{1,3},{2,0},{3,1},{4,6},{5,7},{6,4},{7,5},{8,10},{9,11},{10,... | collective-permute-start | bytes 1572872 | tf_op jit(solution)/shard_map/ppermute | solution.py:560
  20.6 0.8 copy-start.1
  23.5 25.8 %collective-permute-start.1 = (bf16[4,144,256]{2,1,0:T(8,128)(2,1)}, bf16[4,144,256]{2,1,0:T(8,128)(2,1)S(1)}, u32[]{:S(2)}, u32[]{:S(2)}) collective-permute-start(bf16[4,144,256]{2,1,0:T(8,128)(2,1)} %chain.2), channel_id=1, source_target_pairs={{0,2},{1,3},{4,6},{5,7},{8,10},{9,11},{12,14},{13,15},{16,18},{17,... | collective-permute-start | bytes 884744 | tf_op jit(solution)/shard_map/ppermute | solution.py:591
  27.5 35.1 %collective-permute-start.4 = (bf16[512,512]{1,0:T(8,128)(2,1)S(1)}, bf16[512,512]{1,0:T(8,128)(2,1)S(1)}, u32[]{:S(2)}, u32[]{:S(2)}) collective-permute-start(bf16[512,512]{1,0:T(8,128)(2,1)S(1)} %copy-done.5), channel_id=1, source_target_pairs={{0,1},{1,0},{2,3},{3,2},{4,5},{5,4},{6,7},{7,6},{8,9},{9,8},{10,11... | collective-permute-start | bytes 1572872 | tf_op jit(solution)/shard_map/ppermute | solution.py:556
  27.6 35.0 %collective-permute-start.7 = (bf16[512,512]{1,0:T(8,128)(2,1)S(1)}, bf16[512,512]{1,0:T(8,128)(2,1)S(1)}, u32[]{:S(2)}, u32[]{:S(2)}) collective-permute-start(bf16[512,512]{1,0:T(8,128)(2,1)S(1)} %copy-done.6), channel_id=1, source_target_pairs={{0,1},{1,0},{2,3},{3,2},{4,5},{5,4},{6,7},{7,6},{8,9},{9,8},{10,11... | collective-permute-start | bytes 1572872 | tf_op jit(solution)/shard_map/ppermute | solution.py:556
  32.7 21.8 %copy-start.7 = (bf16[512,512]{1,0:T(8,128)(2,1)}, bf16[512,512]{1,0:T(8,128)(2,1)S(1)}, u32[]{:S(2)}) copy-start(bf16[512,512]{1,0:T(8,128)(2,1)S(1)} %collective-permute-done.3.wi1) | copy-start | bytes 1572868
  32.7 30.0 %collective-permute-start.5 = (bf16[512,512]{1,0:T(8,128)(2,1)S(1)}, bf16[512,512]{1,0:T(8,128)(2,1)S(1)}, u32[]{:S(2)}, u32[]{:S(2)}) collective-permute-start(bf16[512,512]{1,0:T(8,128)(2,1)S(1)} %collective-permute-done.3.wi1), channel_id=1, source_target_pairs={{0,1},{1,0},{2,3},{3,2},{4,5},{5,4},{6,7},{7,6},{8,9},{9,8},{10,11... | collective-permute-start | bytes 1572872 | tf_op jit(solution)/shard_map/ppermute | solution.py:556
  43.6 10.9 %copy-start.8 = (bf16[512,512]{1,0:T(8,128)(2,1)}, bf16[512,512]{1,0:T(8,128)(2,1)S(1)}, u32[]{:S(2)}) copy-start(bf16[512,512]{1,0:T(8,128)(2,1)S(1)} %collective-permute-done.6.wo1) | copy-start | bytes 1572868
  43.6 19.0 %collective-permute-start.8 = (bf16[512,512]{1,0:T(8,128)(2,1)S(1)}, bf16[512,512]{1,0:T(8,128)(2,1)S(1)}, u32[]{:S(2)}, u32[]{:S(2)}) collective-permute-start(bf16[512,512]{1,0:T(8,128)(2,1)S(1)} %collective-permute-done.6.wo1), channel_id=1, source_target_pairs={{0,1},{1,0},{2,3},{3,2},{4,5},{5,4},{6,7},{7,6},{8,9},{9,8},{10,11... | collective-permute-start | bytes 1572872 | tf_op jit(solution)/shard_map/ppermute | solution.py:556
  49.3 5.2 %copy-start.14 = (bf16[4,144,256]{2,1,0:T(8,128)(2,1)}, bf16[4,144,256]{2,1,0:T(8,128)(2,1)S(1)}, u32[]{:S(2)}) copy-start(bf16[4,144,256]{2,1,0:T(8,128)(2,1)S(1)} %collective-permute-done.1.got_ref) | copy-start | bytes 884740
  49.3 5.2 %collective-permute-start.2 = (bf16[4,144,256]{2,1,0:T(8,128)(2,1)S(1)}, bf16[4,144,256]{2,1,0:T(8,128)(2,1)S(1)}, u32[]{:S(2)}, u32[]{:S(2)}) collective-permute-start(bf16[4,144,256]{2,1,0:T(8,128)(2,1)S(1)} %collective-permute-done.1.got_ref), channel_id=1, source_target_pairs={{0,1},{1,0},{2,3},{3,2},{4,5},{5,4},{6,7},{7,6},{8,9},{9,8},{10,11... | collective-permute-start | bytes 884744 | tf_op jit(solution)/shard_map/ppermute | solution.py:556
  62.6 0.9 copy-start.10
  62.7 1.1 copy-start.11
  62.7 1.3 copy-start.12
  77.1 58.0 %collective-permute-start.25 = (bf16[4,512,512]{2,1,0:T(8,128)(2,1)}, bf16[4,512,512]{2,1,0:T(8,128)(2,1)S(1)}, u32[]{:S(2)}, u32[]{:S(2)}) collective-permute-start(bf16[4,512,512]{2,1,0:T(8,128)(2,1)} %get-tuple-element.87), channel_id=1, source_target_pairs={{0,1},{1,0},{2,3},{3,2},{4,5},{5,4},{6,7},{7,6},{8,9},{9,8},{10,11... | collective-permute-start | bytes 6291464 | tf_op jit(solution)/shard_map/ppermute | solution.py:556
  89.3 12.4 %collective-permute-start.9 = (bf16[2,4,144,256]{3,2,1,0:T(8,128)(2,1)}, bf16[2,4,144,256]{3,2,1,0:T(8,128)(2,1)S(1)}, u32[]{:S(2)}, u32[]{:S(2)}) collective-permute-start(bf16[2,4,144,256]{3,2,1,0:T(8,128)(2,1)} %get-tuple-element.64.refs_1_), channel_id=1, source_target_pairs={{0,1},{1,0},{2,3},{3,2},{4,5},{5,4},{6,7},{7,6},{8,9},{9,8},{10,11... | collective-permute-start | bytes 1769480 | tf_op jit(solution)/shard_map/ppermute | solution.py:556
  101.2 4.7 %copy-start.4 = (f32[2,128,1024]{2,1,0:T(8,128)S(1)}, f32[2,128,1024]{2,1,0:T(8,128)}, u32[]{:S(2)}) copy-start(f32[2,128,1024]{2,1,0:T(8,128)} %get-tuple-element.79) | copy-start | bytes 3145732
  101.2 4.7 %collective-permute-start.12 = (bf16[2,128,1024]{2,1,0:T(8,128)(2,1)}, bf16[2,128,1024]{2,1,0:T(8,128)(2,1)S(1)}, u32[]{:S(2)}, u32[]{:S(2)}) collective-permute-start(bf16[2,128,1024]{2,1,0:T(8,128)(2,1)} %get-tuple-element.80), channel_id=1, source_target_pairs={{0,1},{1,0},{2,3},{3,2},{4,5},{5,4},{6,7},{7,6},{8,9},{9,8},{10,11... | collective-permute-start | bytes 1572872 | tf_op jit(solution)/shard_map/ppermute | solution.py:556
  101.7 0.8 copy-start.2
  104.6 11.1 %collective-permute-start.10 = (bf16[4,144,256]{2,1,0:T(8,128)(2,1)}, bf16[4,144,256]{2,1,0:T(8,128)(2,1)S(1)}, u32[]{:S(2)}, u32[]{:S(2)}) collective-permute-start(bf16[4,144,256]{2,1,0:T(8,128)(2,1)} %chain.3), channel_id=1, source_target_pairs={{2,0},{3,1},{6,4},{7,5},{10,8},{11,9},{14,12},{15,13},{18,16},{19,... | collective-permute-start | bytes 884744 | tf_op jit(solution)/shard_map/ppermute | solution.py:591
  115.8 1.6 copy-start.13
  115.8 1.6 collective-permute-start.11
  115.8 12.7 %collective-permute-start.13 = (bf16[128,1024]{1,0:T(8,128)(2,1)S(1)}, bf16[128,1024]{1,0:T(8,128)(2,1)S(1)}, u32[]{:S(2)}, u32[]{:S(2)}) collective-permute-start(bf16[128,1024]{1,0:T(8,128)(2,1)S(1)} %fusion.5), channel_id=1, source_target_pairs={{0,2},{1,3},{2,0},{3,1},{4,6},{5,7},{6,4},{7,5},{8,10},{9,11},{10,... | collective-permute-start | bytes 786440 | tf_op jit(solution)/shard_map/ppermute | solution.py:560
  128.3 10.6 %collective-permute-start.16 = (bf16[2,128,1024]{2,1,0:T(8,128)(2,1)}, bf16[2,128,1024]{2,1,0:T(8,128)(2,1)S(1)}, u32[]{:S(2)}, u32[]{:S(2)}) collective-permute-start(bf16[2,128,1024]{2,1,0:T(8,128)(2,1)} %get-tuple-element.82), channel_id=1, source_target_pairs={{0,1},{1,0},{2,3},{3,2},{4,5},{5,4},{6,7},{7,6},{8,9},{9,8},{10,11... | collective-permute-start | bytes 1572872 | tf_op jit(solution)/shard_map/ppermute | solution.py:556
  129.2 15.3 %all-to-all-start = ((bf16[8,16,1024]{2,1,0:T(8,128)(2,1)}), bf16[8,16,1024]{2,1,0:T(8,128)(2,1)S(1)}, u32[]{:S(2)}, u32[]{:S(2)}) async-start(bf16[8,16,1024]{2,1,0:T(8,128)(2,1)} %bitcast.15), calls=%async_computation | async-start | bytes 524288 | tf_op jit(solution)/shard_map/all_to_all | solution.py:566
  138.0 2.2 copy-start
  138.0 2.0 copy-start.3
  138.2 37.3 %collective-permute-start.26 = (bf16[2,512,512]{2,1,0:T(8,128)(2,1)S(1)}, bf16[2,512,512]{2,1,0:T(8,128)(2,1)}, u32[]{:S(2)}, u32[]{:S(2)}) collective-permute-start(bf16[2,512,512]{2,1,0:T(8,128)(2,1)S(1)} %slice.99), channel_id=1, source_target_pairs={{0,2},{1,3},{2,0},{3,1},{4,6},{5,7},{6,4},{7,5},{8,10},{9,11},{10,... | collective-permute-start | bytes 3145736 | tf_op jit(solution)/shard_map/ppermute | solution.py:560
  140.2 28.7 %collective-permute-start.17 = (bf16[128,1024]{1,0:T(8,128)(2,1)S(1)}, bf16[128,1024]{1,0:T(8,128)(2,1)S(1)}, u32[]{:S(2)}, u32[]{:S(2)}) collective-permute-start(bf16[128,1024]{1,0:T(8,128)(2,1)S(1)} %fusion.6), channel_id=1, source_target_pairs={{0,2},{1,3},{2,0},{3,1},{4,6},{5,7},{6,4},{7,5},{8,10},{9,11},{10,... | collective-permute-start | bytes 786440 | tf_op jit(solution)/shard_map/ppermute | solution.py:560
  145.3 24.5 %all-to-all-start.1 = ((bf16[8,16,1024]{2,1,0:T(8,128)(2,1)}), bf16[8,16,1024]{2,1,0:T(8,128)(2,1)S(1)}, u32[]{:S(2)}, u32[]{:S(2)}) async-start(bf16[8,16,1024]{2,1,0:T(8,128)(2,1)} %broadcast_in_dim.6), calls=%async_computation.1 | async-start | bytes 524288 | tf_op jit(solution)/shard_map/all_to_all | solution.py:569
  169.8 13.9 %all-to-all-start.2 = ((bf16[8,16,1024]{2,1,0:T(8,128)(2,1)}), bf16[8,16,1024]{2,1,0:T(8,128)(2,1)S(1)}, u32[]{:S(2)}, u32[]{:S(2)}) async-start(bf16[8,16,1024]{2,1,0:T(8,128)(2,1)} %bitcast.21), calls=%async_computation.2 | async-start | bytes 524288 | tf_op jit(solution)/shard_map/all_to_all | solution.py:566
  183.7 28.7 %all-to-all-start.4 = ((bf16[8,128,512]{2,1,0:T(8,128)(2,1)}), bf16[8,128,512]{2,1,0:T(8,128)(2,1)S(1)}, u32[]{:S(2)}, u32[]{:S(2)}) async-start(bf16[8,128,512]{2,1,0:T(8,128)(2,1)} %bitcast.27), calls=%async_computation.4 | async-start | bytes 2097152 | tf_op jit(solution)/shard_map/all_to_all | solution.py:566
  213.1 12.5 %all-to-all-start.3 = ((bf16[8,16,1024]{2,1,0:T(8,128)(2,1)}), bf16[8,16,1024]{2,1,0:T(8,128)(2,1)S(1)}, u32[]{:S(2)}, u32[]{:S(2)}) async-start(bf16[8,16,1024]{2,1,0:T(8,128)(2,1)} %broadcast_in_dim.7), calls=%async_computation.3 | async-start | bytes 524288 | tf_op jit(solution)/shard_map/all_to_all | solution.py:569
  216.5 13.8 %copy-start.17 = (f32[16,512]{1,0:T(8,128)S(1)}, f32[16,512]{1,0:T(8,128)}, u32[]{:S(2)}) copy-start(f32[16,512]{1,0:T(8,128)} %get-tuple-element.84) | copy-start | bytes 98308
  226.7 45.5 %all-to-all-start.5 = ((bf16[8,128,512]{2,1,0:T(8,128)(2,1)}), bf16[8,128,512]{2,1,0:T(8,128)(2,1)S(1)}, u32[]{:S(2)}, u32[]{:S(2)}) async-start(bf16[8,128,512]{2,1,0:T(8,128)(2,1)} %broadcast_in_dim.8), calls=%async_computation.5 | async-start | bytes 2097152 | tf_op jit(solution)/shard_map/all_to_all | solution.py:569
  230.3 1.3 collective-permute-start.20
  231.5 3.9 %collective-permute-start.21 = (f32[16,512]{1,0:T(8,128)S(1)}, f32[16,512]{1,0:T(8,128)S(1)}, u32[]{:S(2)}, u32[]{:S(2)}) collective-permute-start(f32[16,512]{1,0:T(8,128)S(1)} %add.51), channel_id=1, source_target_pairs={{0,2},{1,3},{2,0},{3,1},{4,6},{5,7},{6,4},{7,5},{8,10},{9,11},{10,... | collective-permute-start | bytes 98312 | tf_op jit(solution)/shard_map/ppermute | solution.py:560
  235.5 4.1 %collective-permute-start.22 = (f32[16,512]{1,0:T(8,128)S(1)}, f32[16,512]{1,0:T(8,128)S(1)}, u32[]{:S(2)}, u32[]{:S(2)}) collective-permute-start(f32[16,512]{1,0:T(8,128)S(1)} %add.52), channel_id=1, source_target_pairs={{0,4},{4,0},{8,12},{12,8},{16,20},{20,16},{24,28},{28,24},{1,5},{5... | collective-permute-start | bytes 98312 | tf_op jit(solution)/shard_map/ppermute | solution.py:798
  239.6 8.0 %collective-permute-start.23 = (f32[16,512]{1,0:T(8,128)S(1)}, f32[16,512]{1,0:T(8,128)S(1)}, u32[]{:S(2)}, u32[]{:S(2)}) collective-permute-start(f32[16,512]{1,0:T(8,128)S(1)} %add.53), channel_id=1, source_target_pairs={{0,8},{4,12},{8,0},{12,4},{16,24},{20,28},{24,16},{28,20},{1,9},{5... | collective-permute-start | bytes 98312 | tf_op jit(solution)/shard_map/ppermute | solution.py:798
  241.3 17.0 %collective-permute-start.14 = (bf16[128,1024]{1,0:T(8,128)(2,1)S(1)}, bf16[128,1024]{1,0:T(8,128)(2,1)S(1)}, u32[]{:S(2)}, u32[]{:S(2)}) collective-permute-start(bf16[128,1024]{1,0:T(8,128)(2,1)S(1)} %bitcast.55), channel_id=1, source_target_pairs={{0,2},{1,3},{2,0},{3,1},{4,6},{5,7},{6,4},{7,5},{8,10},{9,11},{10,... | collective-permute-start | bytes 786440 | tf_op jit(solution)/shard_map/ppermute | solution.py:560
  247.6 9.6 %collective-permute-start.24 = (f32[16,512]{1,0:T(8,128)S(1)}, f32[16,512]{1,0:T(8,128)S(1)}, u32[]{:S(2)}, u32[]{:S(2)}) collective-permute-start(f32[16,512]{1,0:T(8,128)S(1)} %add.54), channel_id=1, source_target_pairs={{0,16},{4,20},{8,24},{12,28},{16,0},{20,4},{24,8},{28,12},{1,17},{... | collective-permute-start | bytes 98312 | tf_op jit(solution)/shard_map/ppermute | solution.py:798
  257.3 6.7 %collective-permute-start.18 = (bf16[128,1024]{1,0:T(8,128)(2,1)S(1)}, bf16[128,1024]{1,0:T(8,128)(2,1)S(1)}, u32[]{:S(2)}, u32[]{:S(2)}) collective-permute-start(bf16[128,1024]{1,0:T(8,128)(2,1)S(1)} %bitcast.58), channel_id=1, source_target_pairs={{0,2},{1,3},{2,0},{3,1},{4,6},{5,7},{6,4},{7,5},{8,10},{9,11},{10,... | collective-permute-start | bytes 786440 | tf_op jit(solution)/shard_map/ppermute | solution.py:560
  258.4 6.9 %collective-permute-start.15 = (bf16[2,128,1024]{2,1,0:T(8,128)(2,1)S(1)}, bf16[2,128,1024]{2,1,0:T(8,128)(2,1)S(1)}, u32[]{:S(2)}, u32[]{:S(2)}) collective-permute-start(bf16[2,128,1024]{2,1,0:T(8,128)(2,1)S(1)} %pad_maximum_fusion.2), channel_id=1, source_target_pairs={{0,1},{1,0},{2,3},{3,2},{4,5},{5,4},{6,7},{7,6},{8,9},{9,8},{10,11... | collective-permute-start | bytes 1572872 | tf_op jit(solution)/shard_map/ppermute | solution.py:556
  264.0 2.3 collective-permute-start.19
  (3 other events, 2.2 us)

commit v2 on v0

v2 whole, which is shorter than its diff:
```python
import functools
import math

import jax
import jax.numpy as jnp
from jax import lax
from jax.experimental import pallas as pl
from jax.experimental.pallas import tpu as pltpu
from jax.sharding import PartitionSpec as P

BF = jnp.bfloat16
F32 = jnp.float32
epsilon = 1e-05
guard = 0.01
LANES = 128
EXTRA = 16
VMEM_BYTES = 16 * 1024 * 1024


def nn(a, b):
    return lax.dot_general(a, b, (((1,), (0,)), ((), ())), preferred_element_type=F32)


def nt(a, b):
    return lax.dot_general(a, b, (((1,), (1,)), ((), ())), preferred_element_type=F32)


def tn(a, b):
    return lax.dot_general(a, b, (((0,), (0,)), ((), ())), preferred_element_type=F32)


def two_terms(v):
    high = v.astype(BF)
    return high, (v - high.astype(F32)).astype(BF)


def iota(shape, dim):
    return lax.broadcasted_iota(jnp.int32, shape, dim)


def triangle(length, upper):
    rows, cols = iota((length, length), 0), iota((length, length), 1)
    return jnp.where((cols >= rows) if upper else (rows >= cols), 1.0, 0.0).astype(BF)


def running_sum(v, upper):
    ones = triangle(v.shape[0], upper)
    high, rest = two_terms(v)
    low = (v - high.astype(F32) - rest.astype(F32)).astype(BF)
    return nn(ones, high) + nn(ones, rest) + nn(ones, low)


def norm_rows(v):
    centred = v - jnp.mean(v, axis=-1, keepdims=True)
    scale = lax.rsqrt(jnp.mean(centred * centred, axis=-1, keepdims=True) + epsilon)
    return centred * scale, scale


def norm_rows_backward(grad, xhat, scale, gain):
    g = grad * gain
    return scale * (
        g
        - jnp.mean(g, axis=-1, keepdims=True)
        - xhat * jnp.mean(g * xhat, axis=-1, keepdims=True)
    )


def pair_frequencies(freq_ref, pair):
    even, odd = freq_ref[2 * pair], freq_ref[2 * pair + 1]
    none = jnp.zeros_like(even)
    return jnp.concatenate(
        [jnp.concatenate([even, none], axis=1), jnp.concatenate([none, odd], axis=1)], axis=0
    )


def scaled_sine_cosine(angles, scale):
    turns = jnp.floor(angles * (1.0 / math.pi) + 0.5)
    r = angles - turns * 3.140625
    r = r - turns * 0.0009675025939941406
    r = r - turns * 1.509958e-07
    odd = turns - 2.0 * jnp.floor(turns * 0.5)
    sign = scale - (2.0 * scale) * odd
    r2 = r * r
    sine = -0.00018362251175623582 * r2 + 0.008306273552368303
    sine = sine * r2 - 0.1666482311215342
    sine = sine * r2 + 0.9999966031254778
    cosine = -0.0012711240835350962 * r2 + 0.041487518673719546
    cosine = cosine * r2 - 0.4999123281046797
    cosine = cosine * r2 + 0.9999933132015835
    return sine * (r * sign), cosine * sign


def pair_features(values, freq, scale):
    high, low = two_terms(values)
    freq_high, freq_low = two_terms(freq)
    angles = nn(high, freq_high) + nn(low, freq_high) + nn(high, freq_low)
    sine, cosine = scaled_sine_cosine(angles, scale)
    sine, cosine = sine.astype(BF), cosine.astype(BF)
    feat = freq.shape[1] // 2
    return [
        jnp.concatenate([sine[:, h * feat : (h + 1) * feat], cosine[:, h * feat : (h + 1) * feat]], axis=1)
        for h in (0, 1)
    ]


def own_lanes(shape, half):
    lane = iota(shape, len(shape) - 1)
    return (lane >= LANES // 2) if half else (lane < LANES // 2)


def one_lane(shape, half):
    return iota(shape, len(shape) - 1) == (0 if half else LANES // 2)


def second_lane(shape, half):
    return iota(shape, len(shape) - 1) == (1 if half else LANES // 2 + 1)


def with_ones(values, half, both=False):
    v = values.astype(F32)
    ones = one_lane(v.shape, half) | (both & second_lane(v.shape, half))
    return jnp.where(own_lanes(v.shape, half), v, jnp.where(ones, 1.0, 0.0))


def pack_states(even, odd, decay_even, decay_odd):
    half = LANES // 2
    row = iota(even.shape, 0)
    states = jnp.where(row < half, even, odd).astype(BF)
    extra = iota((EXTRA, even.shape[1]), 0)
    parts = []
    for value in (even[half : half + 1], odd[0:1], decay_even, decay_odd):
        high = value.astype(BF).astype(F32)
        parts += [high, value - high]
    rows = jnp.zeros((EXTRA, even.shape[1]), F32)
    for at, part in enumerate(parts):
        rows = jnp.where(extra == at, part, rows)
    return states, rows.astype(BF)


def extra_row(packed, at):
    at = LANES + 2 * at
    return packed[at : at + 1] + packed[at + 1 : at + 2]


def decays(packed):
    return extra_row(packed, 2), extra_row(packed, 3)


def unpack_states(packed):
    half = LANES // 2
    states = packed[:LANES]
    row = iota(states.shape, 0)
    even = jnp.where(row < half, states, jnp.where(row == half, extra_row(packed, 0), 0.0))
    odd = jnp.where(row >= half, states, jnp.where(row == 0, extra_row(packed, 1), 0.0))
    return even, odd


def join_states(first, second):
    return [
        a + decay * b
        for a, b, decay in zip(unpack_states(first), unpack_states(second), decays(first))
    ]


def as_operand(state, half):
    at = 0 if half else LANES // 2
    norm = state[at : at + 1]
    rest = norm - norm.astype(BF).astype(F32)
    return jnp.where(iota(state.shape, 0) == at + 1, rest, state).astype(BF)


def decay_weights(c_col, c_row, a_row):
    length = c_col.shape[0]
    gap = jnp.minimum(c_col - c_row, 0.0)
    causal = iota((length, length), 0) >= iota((length, length), 1)
    return jnp.where(causal, jnp.exp(gap) * a_row, 0.0)


def lane_sum(v):
    return jnp.sum(v, axis=1, keepdims=True)


def each(count, step):
    lax.fori_loop(0, count, lambda i, none: (step(i), none)[1], 0)


def wide(v, axis):
    none = list(v.shape)
    none[axis] = LANES - v.shape[axis]
    return jnp.concatenate([v, jnp.zeros(none, v.dtype)], axis=axis)


def aligned(at, size):
    return pl.ds(pl.multiple_of(at * size, size), size)


def my_core():
    return lax.axis_index("mp") % 2


def my_chip():
    return lax.axis_index("mp") // 2


def pack_kernel(inner_ref, outer_ref, out_ref, sems):
    rows = out_ref.shape[1]
    mine = aligned(lax.axis_index("dp") % 2, rows)
    copies = [
        pltpu.make_async_copy(source.at[mine], out_ref.at[i], sems.at[i])
        for i, source in enumerate((inner_ref, outer_ref))
    ]
    for copy in copies:
        copy.start()
    for copy in copies:
        copy.wait()


def put_states(s, pair, main, rest, away_ref, home_ref):
    home = s == my_core()

    @pl.when(home)
    def _():
        home_ref[pair, :LANES] = main
        home_ref[pair, LANES:] = rest

    @pl.when(jnp.logical_not(home))
    def _():
        away_ref[pair, :LANES] = main
        away_ref[pair, LANES:] = rest


def keys_kernel(*refs):
    sources, refs = refs[:7], refs[7:]
    n1_ref, v_ref, c_ref, a_ref, crow_ref, arow_ref, pk_ref, away_ref, home_ref = refs[:9]
    buffers, sems = refs[9:16], refs[16]
    copies = [
        pltpu.make_async_copy(source, buffer, sems.at[i])
        for i, (source, buffer) in enumerate(zip(sources, buffers))
    ]
    for copy in copies:
        copy.start()
    for copy in copies:
        copy.wait()
    x_ref, wqkv_ref, gw_ref, gb_ref, gain_ref, shift_ref, freq_ref = buffers
    heads, _, feat = freq_ref.shape
    seqs, length, width = x_ref.shape
    scale = 1.0 / math.sqrt(feat)
    gate_weight, gate_bias = wide(gw_ref[...], 0), wide(gb_ref[...], 1)

    def one(s):
        xhat, _ = norm_rows(x_ref[s])
        n1 = (xhat * gain_ref[...] + shift_ref[...]).astype(BF)
        n1_ref[s] = n1
        z = nt(n1, gate_weight) + gate_bias
        e = jnp.exp(-jnp.abs(z))
        log_keep = jnp.minimum(z, 0.0) - jnp.log1p(e)
        inverse = 1.0 / (1.0 + e)
        admit = jnp.where(z > 0.0, e * inverse, inverse)
        c = running_sum(log_keep, False)
        c_ref[s] = c
        a_ref[s] = admit
        crow_ref[s] = jnp.transpose(c)[:heads]
        arow_ref[s] = jnp.transpose(admit)[:heads]
        last = c[length - 1 :]
        tail = jnp.exp(last - c) * admit
        decay = jnp.exp(last)
        for pair in range(heads // 2):
            at = pair * LANES
            freq = pair_frequencies(freq_ref, pair)
            k = nn(n1, wqkv_ref[:, width + at : width + at + LANES])
            v = nn(n1, wqkv_ref[:, 2 * width + at : 2 * width + at + LANES])
            v_ref[s, :, at : at + LANES] = v
            phi_k = pair_features(k, freq, scale)
            states = []
            for half in (0, 1):
                h = 2 * pair + half
                pk_ref[s, h] = phi_k[half]
                weighted = jnp.concatenate(
                    two_terms(with_ones(v, half) * tail[:, h : h + 1]), axis=1
                )
                both = tn(weighted, phi_k[half])
                states.append(both[:LANES] + both[LANES:])
            main, rest = pack_states(
                *states, decay[:, 2 * pair : 2 * pair + 1], decay[:, 2 * pair + 1 : 2 * pair + 2]
            )
            put_states(s, pair, main, rest, away_ref, home_ref)

    each(seqs, one)


def scores_kernel(wqkv_ref, freq_ref, n1_ref, pk_ref, v_ref, c_ref, crow_ref, arow_ref, pq_ref, p_ref, num_ref):
    seqs, heads = pk_ref.shape[:2]
    scale = 1.0 / math.sqrt(freq_ref.shape[2])

    def one(s):
        for pair in range(heads // 2):
            at = pair * LANES
            q = nn(n1_ref[s], wqkv_ref[:, at : at + LANES])
            phi_q = pair_features(q, pair_frequencies(freq_ref, pair), scale)
            for half in (0, 1):
                h = 2 * pair + half
                pq_ref[s, h] = phi_q[half]
                v = with_ones(v_ref[s, :, at : at + LANES], half)
                weights = decay_weights(
                    c_ref[s, :, h : h + 1], crow_ref[s, h : h + 1], arow_ref[s, h : h + 1]
                )
                p = (nt(phi_q[half], pk_ref[s, h]) * weights).astype(BF)
                p_ref[s, h] = p
                both = nn(p, jnp.concatenate(two_terms(v), axis=1))
                num_ref[s, h] = both[:, :LANES] + both[:, LANES:]

    each(seqs, one)


def mix_kernel(
    x_ref, got_ref, swapped_ref, partner_home_ref, partner_away_ref, wo_ref, gain_ref, shift_ref, pq_ref, c_ref, num_ref,
    full_ref, start_ref, mixed_ref, resid_ref, n2_ref,
):
    seqs, heads = pq_ref.shape[:2]
    core = my_core()

    def one(s):
        growth = jnp.exp(c_ref[s])
        for pair in range(heads // 2):
            before = jnp.where(s == core, got_ref[pair], swapped_ref[pair]).astype(F32)
            partner = jnp.where(s == core, partner_home_ref[pair], partner_away_ref[pair]).astype(F32)
            states = [
                jnp.where(core == 0, a, b)
                for a, b in zip(unpack_states(before), join_states(partner, before))
            ]
            none = jnp.zeros((1, 1), F32)
            main, rest = pack_states(*states, none, none)
            start_ref[s, pair, :LANES] = main
            start_ref[s, pair, LANES:] = rest
            mixed = []
            for half in (0, 1):
                h = 2 * pair + half
                full = num_ref[s, h] + growth[:, h : h + 1] * nt(
                    pq_ref[s, h], as_operand(states[half], half)
                )
                full_ref[s, h] = full
                at = 0 if half else LANES // 2
                sden = full[:, at : at + 1] + full[:, at + 1 : at + 2]
                mixed.append(full * lax.rsqrt(sden * sden + guard))
            pair_mixed = jnp.where(own_lanes(mixed[0].shape, 0), mixed[0], mixed[1])
            mixed_ref[s, :, pair * LANES : (pair + 1) * LANES] = pair_mixed.astype(BF)
        resid = x_ref[s] + nn(mixed_ref[s], wo_ref[...])
        resid_ref[s] = resid
        xhat, _ = norm_rows(resid)
        n2_ref[s] = (xhat * gain_ref[...] + shift_ref[...]).astype(BF)

    each(seqs, one)


def gelu_and_slope(v):
    root = math.sqrt(2.0 / math.pi)
    v2 = v * v
    t = jnp.tanh(v * (root + (root * 0.044715) * v2))
    half = 0.5 * (1.0 + t)
    slope = half + (0.5 * v) * (1.0 - t * t) * (root + (root * 3.0 * 0.044715) * v2)
    return v * half, slope


def feed_kernel(
    og_ref, wi0, wo0, wi2, wo2, half_chip_ref, half_twin_ref, half_both_ref, half_both_twin_ref, n2_ref, resid_ref,
    out_ref, dn2_ref, back_ref, keep_ref, send_ref, far_ref,
):
    twin = lax.axis_index("dp") % 2
    for at, one, two in ((0, half_chip_ref, half_twin_ref), (1, half_both_ref, half_both_twin_ref)):
        for which in range(2):
            rows = one.shape[1]
            far_ref[at, which, aligned(twin, rows)] = one[which]
            far_ref[at, which, aligned(1 - twin, rows)] = two[which]
    (wi1, wo1), (wi3, wo3) = ((far_ref.at[at, 0], far_ref.at[at, 1]) for at in (0, 1))
    n2 = n2_ref[...]
    out_low = og_ref[...].astype(BF)
    total = resid_ref[...]
    dn2 = None
    for block, (wi, wo) in enumerate(((wi0, wo0), (wi1, wo1), (wi2, wo2), (wi3, wo3))):
        active, slope = gelu_and_slope(nn(n2, wi[...]))
        active = active.astype(BF)
        total = total + nn(active, wo[...])
        pre_grad = (nt(out_low, wo[...]) * slope).astype(BF)
        back_ref[block] = pre_grad
        part = nt(pre_grad, wi[...])
        dn2 = part if dn2 is None else dn2 + part
        outer = tn(active, out_low)
        if block < 2:
            keep_ref[block] = outer
        else:
            send_ref[block - 2] = outer.astype(BF)
    out_ref[...] = total
    dn2_ref[...] = dn2


def inner_kernel(n2_ref, back_ref, mixed_ref, low_ref, keep_ref, send_ref):
    own = 2 * my_core() + my_chip()
    width = n2_ref.shape[1]
    rows = width // 4
    for block in range(4):
        inner = tn(n2_ref[...], back_ref[block])
        mixed = tn(mixed_ref[:, aligned(own ^ block, rows)], low_ref[...])
        if block < 2:
            keep_ref[block, :width] = inner
            keep_ref[block, width:] = mixed
        else:
            send_ref[block - 2, :width] = inner.astype(BF)
            send_ref[block - 2, width:] = mixed.astype(BF)


def place_bit(bits):
    place = lax.axis_index("dp")
    return jnp.where(my_core() == 0, (place // (1 << bits[0])) % 2, (place // (1 << bits[1])) % 2)


def split_rows(total, bits, mine_ref, send_ref):
    rows = mine_ref.shape[1]
    high = place_bit(bits) == 1
    first, second = total[:, :rows], total[:, rows:]
    mine_ref[...] = jnp.where(high, second, first)
    send_ref[...] = jnp.where(high, first, second).astype(BF)


def first_kernel(keep1_ref, got1_ref, keep2_ref, got2_ref, mine_ref, send_ref, *, bits):
    total1 = keep1_ref[...] + got1_ref[...].astype(F32)
    total2 = keep2_ref[...] + got2_ref[...].astype(F32)
    split_rows(jnp.concatenate([total1, total2], axis=1), bits, mine_ref, send_ref)


def halve_kernel(keep_ref, got_ref, mine_ref, send_ref, *, bits):
    split_rows(keep_ref[...] + got_ref[...].astype(F32), bits, mine_ref, send_ref)


def third_kernel(keep_ref, got_ref, mine_ref, send_ref, *, bit):
    rows = mine_ref.shape[1]
    total = keep_ref[...] + got_ref[...].astype(F32)
    low, high = total[:, :rows], total[:, rows:]
    by_bit = place_bit((bit, bit)) == 1
    one, two = jnp.where(by_bit, high, low), jnp.where(by_bit, low, high)
    even = my_core() == 0
    for part in range(2):
        of_block = (low, high)[part]
        mine_ref[part] = jnp.where(even, one[part], of_block[0])
        send_ref[part] = jnp.where(even, two[part], of_block[1]).astype(BF)


def fourth_kernel(keep_ref, got_ref, mine_ref, send_ref, *, bit):
    total = keep_ref[...] + got_ref[...].astype(F32)
    second = (my_core() == 1) & (place_bit((bit, bit)) == 1)
    mine_ref[...] = jnp.where(second, total[1], total[0])
    send_ref[...] = jnp.where(second, total[0], total[1]).astype(BF)


def add_kernel(keep_ref, got_ref, out_ref):
    out_ref[...] = (keep_ref[...] + got_ref[...].astype(F32)).astype(out_ref.dtype)


def joined(mine_ref, got_ref, bits):
    high = place_bit(bits) == 1
    mine, got = mine_ref[...].astype(F32), got_ref[...].astype(F32)
    return jnp.concatenate([jnp.where(high, got, mine), jnp.where(high, mine, got)], axis=0)


def join_kernel(mine_ref, got_ref, out_ref, *, bits):
    out_ref[...] = joined(mine_ref, got_ref, bits).astype(BF)


def final_kernel(mine_ref, got_ref, outer_ref, inner_ref, quarter_ref, *, bits):
    both = joined(mine_ref, got_ref, bits)
    rows = outer_ref.shape[0]
    outer_ref[...] = both[:rows]
    inner_ref[...] = both[rows : 2 * rows]
    quarter_ref[...] = both[2 * rows :].astype(BF)


def turn_kernel(
    og_ref, gain_ref, wo_ref, dn2_ref, resid_ref, full_ref, pq_ref, c_ref,
    dres_ref, low_ref, sums_ref, ng_ref, r_ref, away_ref, home_ref,
):
    seqs, heads, length, _ = pq_ref.shape
    sums_ref[...] = jnp.zeros_like(sums_ref)

    def one(s):
        xhat, scale = norm_rows(resid_ref[s])
        dn2 = dn2_ref[s]
        dres = og_ref[s] + norm_rows_backward(dn2, xhat, scale, gain_ref[...])
        dres_ref[s] = dres
        low = dres.astype(BF)
        low_ref[aligned(s, length)] = low
        sums_ref[2:3] += jnp.sum(dn2 * xhat, axis=0, keepdims=True)
        sums_ref[3:4] += jnp.sum(dn2, axis=0, keepdims=True)
        dmixed = nt(low, wo_ref[...])
        c = c_ref[s]
        growth = jnp.exp(c)
        decay = jnp.exp(c[length - 1 :])
        lane = iota(c.shape, 1)
        r_all = jnp.zeros_like(c)
        for pair in range(heads // 2):
            g = dmixed[:, pair * LANES : (pair + 1) * LANES]
            states = []
            for half in (0, 1):
                h = 2 * pair + half
                full = full_ref[s, h]
                at = 0 if half else LANES // 2
                sden = full[:, at : at + 1] + full[:, at + 1 : at + 2]
                inverse = lax.rsqrt(sden * sden + guard)
                inverse2 = inverse * inverse
                mine = own_lanes(g.shape, half)
                dot = lane_sum(jnp.where(mine, g * full, 0.0)) * inverse
                sden_grad = -dot * sden * inverse2
                r_all = jnp.where(lane == h, dot * inverse2 * guard, r_all)
                grads = jnp.where(
                    mine, g * inverse, jnp.where(one_lane(g.shape, half), sden_grad, 0.0)
                )
                ng_ref[s, h] = jnp.concatenate(two_terms(grads), axis=1)
                lifted = jnp.concatenate(two_terms(grads * growth[:, h : h + 1]), axis=1)
                both = tn(lifted, pq_ref[s, h])
                states.append(both[:LANES] + both[LANES:])
            main, rest = pack_states(
                *states, decay[:, 2 * pair : 2 * pair + 1], decay[:, 2 * pair + 1 : 2 * pair + 2]
            )
            put_states(s, pair, main, rest, away_ref, home_ref)
        r_ref[s] = r_all

    each(seqs, one)


def angle_grads(phi, dphi):
    feat = phi.shape[1] // 2
    phi = phi.astype(F32)
    return phi[:, feat:] * dphi[:, :feat] - phi[:, :feat] * dphi[:, feat:]


def weight_grads(left_ref, right_ref, keep_ref, send_ref):
    rows = keep_ref.shape[0]
    core = my_core()
    keep_ref[...] = tn(left_ref[:, aligned(core, rows)], right_ref[...])
    send_ref[...] = tn(left_ref[:, aligned(1 - core, rows)], right_ref[...]).astype(BF)


def back_kernel(
    freq_ref, pq_ref, pk_ref, v_ref, ng_ref, p_ref, c_ref, crow_ref, arow_ref, start_ref,
    qg_ref, kg_ref, vg_ref, kcol_ref,
):
    seqs, heads, length, _ = pq_ref.shape

    def one(s):
        tokens = aligned(s, length)
        c = c_ref[s]
        growth = jnp.exp(c)
        lane = iota(c.shape, 1)
        kcol = jnp.zeros_like(c)
        for pair in range(heads // 2):
            at = pair * LANES
            freq = pair_frequencies(freq_ref, pair).astype(BF)
            states = unpack_states(start_ref[s, pair].astype(F32))
            q_angles, k_angles, v_grads = [], [], []
            for half in (0, 1):
                h = 2 * pair + half
                phi_q, phi_k = pq_ref[s, h], pk_ref[s, h]
                grads = ng_ref[s, h, :, :LANES]
                v = with_ones(v_ref[s, :, at : at + LANES], half)
                weights = decay_weights(c[:, h : h + 1], crow_ref[s, h : h + 1], arow_ref[s, h : h + 1])
                dk = (nt(grads, v.astype(BF)) * weights).astype(BF)
                lifted = (grads.astype(F32) * growth[:, h : h + 1]).astype(BF)
                dphi_q = nn(dk, phi_k) + nn(lifted, states[half].astype(BF))
                q_angles.append(angle_grads(phi_q, dphi_q))
                k_angles.append(angle_grads(phi_k, tn(dk, phi_q)))
                both = tn(p_ref[s, h], ng_ref[s, h])
                dv = both[:, :LANES] + both[:, LANES:]
                v_grads.append(dv)
                kcol = jnp.where(lane == h, lane_sum(v * dv), kcol)
            qg_ref[tokens, at : at + LANES] = nt(
                jnp.concatenate(q_angles, axis=1).astype(BF), freq
            ).astype(BF)
            kg_ref[s, :, at : at + LANES] = nt(jnp.concatenate(k_angles, axis=1).astype(BF), freq)
            vg_ref[s, :, at : at + LANES] = jnp.where(
                own_lanes(v_grads[0].shape, 0), v_grads[0], v_grads[1]
            )
        kcol_ref[s] = kcol

    each(seqs, one)


def queries_kernel(n1_ref, qg_ref, keep_ref, send_ref):
    weight_grads(n1_ref, qg_ref, keep_ref, send_ref)


def cross_kernel(
    got_ref, swapped_ref, partner_home_ref, partner_away_ref, freq_ref, away_ref, home_ref, start_ref, pk_ref, v_ref,
    c_ref, a_ref, r_ref, kcol_ref,
    kg_ref, vg_ref, n1_ref,
    kv_ref, logit_ref, bias_ref, keep_ref, send_ref,
):
    seqs, heads, length, _ = pk_ref.shape
    core = my_core()
    width = kg_ref.shape[2]
    bias_ref[...] = jnp.zeros_like(bias_ref)

    def one(s):
        tokens = aligned(s, length)
        c, a = c_ref[s], a_ref[s]
        tail = jnp.exp(c[length - 1 :] - c) * a
        lane = iota(c.shape, 1)
        lane_row = iota((1, c.shape[1]), 1)
        kcol = kcol_ref[s]
        ends = jnp.zeros((1, c.shape[1]), F32)
        for pair in range(heads // 2):
            at = pair * LANES
            freq = pair_frequencies(freq_ref, pair).astype(BF)
            after = jnp.where(s == core, got_ref[pair], swapped_ref[pair]).astype(F32)
            partner = jnp.where(s == core, partner_home_ref[pair], partner_away_ref[pair]).astype(F32)
            grads = [
                jnp.where(core == 1, a, b)
                for a, b in zip(unpack_states(after), join_states(partner, after))
            ]
            local = jnp.where(s == core, home_ref[pair], away_ref[pair]).astype(F32)
            reached = join_states(local, start_ref[s, pair].astype(F32))
            k_angles, v_grads = [], []
            for half in (0, 1):
                h = 2 * pair + half
                phi_k = pk_ref[s, h]
                v = with_ones(v_ref[s, :, at : at + LANES], half, True)
                grad_low = as_operand(grads[half], half)
                weight = tail[:, h : h + 1]
                k_angles.append(angle_grads(phi_k, nn(v.astype(BF), grad_low)) * weight)
                dv = nt(phi_k, grad_low) * weight
                v_grads.append(dv)
                kcol = kcol + jnp.where(lane == h, lane_sum(v * dv), 0.0)
                end = jnp.sum(lane_sum(grads[half] * reached[half]), axis=0, keepdims=True)
                ends = jnp.where(lane_row == h, end, ends)
            kg = kg_ref[s, :, at : at + LANES] + nt(
                jnp.concatenate(k_angles, axis=1).astype(BF), freq
            )
            vg = vg_ref[s, :, at : at + LANES] + jnp.where(
                own_lanes(v_grads[0].shape, 0), v_grads[0], v_grads[1]
            )
            kv_ref[tokens, at : at + LANES] = kg.astype(BF)
            kv_ref[tokens, width + at : width + at + LANES] = vg.astype(BF)
        keep_grad = running_sum(r_ref[s] - kcol, True) + ends
        logit_grad = a * keep_grad - (1.0 - a) * kcol
        logit_ref[tokens] = logit_grad.astype(BF)
        bias_ref[0:1] += jnp.sum(logit_grad, axis=0, keepdims=True)

    each(seqs, one)
    weight_grads(n1_ref, kv_ref, keep_ref, send_ref)


def close_kernel(
    x_ref, wqkv_ref, gw_ref, gain_ref, qg_ref, kv_ref, logit_ref, bias_ref, n1_ref, dres_ref, sums2_ref,
    dx_ref, small_ref,
):
    width = x_ref.shape[1]
    logit_low = logit_ref[...]
    dn1 = (
        nt(qg_ref[...], wqkv_ref[:, :width])
        + nt(kv_ref[...], wqkv_ref[:, width:])
        + nn(logit_low, wide(gw_ref[...], 0))
    )
    xhat, scale = norm_rows(x_ref[...])
    dx_ref[...] = dres_ref[...] + norm_rows_backward(dn1, xhat, scale, gain_ref[...])
    row = iota((8, width), 0)
    sums = jnp.where(row == 0, jnp.sum(dn1 * xhat, axis=0, keepdims=True), sums2_ref[...])
    sums = jnp.where(row == 1, jnp.sum(dn1, axis=0, keepdims=True), sums)
    bias = jnp.concatenate([bias_ref[0:1], jnp.zeros((1, width - LANES), F32)], axis=1)
    sums = jnp.where(row == 4, bias, sums)
    gates = tn(logit_low, n1_ref[...])[:8]
    stacked = jnp.concatenate([sums, gates, jnp.zeros((LANES - 16, width), F32)], axis=0)
    columns = jnp.transpose(stacked)
    rows = small_ref.shape[0]
    both = columns[:rows] + pltpu.roll(columns[rows:], 16, 1)
    high, low = two_terms(both)
    small_ref[...] = (high.astype(F32) + pltpu.roll(low.astype(F32), LANES // 2, 1)).astype(BF)


def chain_kernel(me_ref, partner_ref, out_ref, *, reverse):
    core = my_core()
    lead = (core == 0) if reverse else (core == 1)
    for pair in range(out_ref.shape[0]):
        mine, other = me_ref[pair].astype(F32), partner_ref[pair].astype(F32)
        first = jnp.where(lead, mine, other)
        second = jnp.where(lead, other, mine)
        none = jnp.zeros((1, 1), F32)
        main, rest = pack_states(*join_states(first, second), none, none)
        out_ref[pair, :LANES] = main
        out_ref[pair, LANES:] = rest


def assemble_kernel(mine_ref, other_ref, quarters_ref, far_ref, qkv_ref, wo_ref, gate_ref, bias_ref, *norm_refs):
    rows, wide = mine_ref.shape[0], qkv_ref.shape[1]
    core, own = my_core(), 2 * my_core() + my_chip()
    qkv_ref[aligned(core, rows)] = mine_ref[:, :wide].astype(F32)
    qkv_ref[aligned(1 - core, rows)] = other_ref[:, :wide].astype(F32)
    for block in range(4):
        quarter = (quarters_ref, far_ref)[block // 2][block % 2]
        wo_ref[aligned(own ^ block, quarter.shape[0])] = quarter.astype(F32)
    columns = mine_ref[:, wide:].astype(F32) + other_ref[:, wide:].astype(F32)
    columns = columns + pltpu.roll(columns, LANES // 2, 1)
    stacked = jnp.transpose(columns)
    heads = gate_ref.shape[0]
    gate_ref[:, :rows] = stacked[8 : 8 + heads]
    gate_ref[:, rows:] = stacked[24 : 24 + heads]
    bias_ref[...] = stacked[4:5, : bias_ref.shape[1]]
    for row, norm_ref in enumerate(norm_refs):
        norm_ref[:, :rows] = stacked[row : row + 1]
        norm_ref[:, rows:] = stacked[16 + row : 17 + row]


class Order:
    def __init__(self):
        self.last = ()

    def call(self, kernel, name, given, kept, outs, scratch=(), wait=(), hbm=False):
        wait = (*self.last, *wait)
        space = pltpu.HBM if hbm else pltpu.VMEM
        given = [pltpu.with_memory_space_constraint(a, space) if hbm else a for a in given]
        kept = [pltpu.with_memory_space_constraint(a, pltpu.VMEM) for a in kept]
        got = pl.pallas_call(
            lambda *refs: kernel(*refs[len(wait) :]),
            out_shape=outs,
            in_specs=[pl.BlockSpec(memory_space=pl.ANY)] * len(wait)
            + [pl.BlockSpec(memory_space=space)] * len(given)
            + [pl.BlockSpec(memory_space=pltpu.VMEM)] * len(kept),
            out_specs=jax.tree.map(lambda _: pl.BlockSpec(memory_space=pltpu.VMEM), outs),
            scratch_shapes=scratch,
            compiler_params=pltpu.CompilerParams(vmem_limit_bytes=VMEM_BYTES),
            cost_estimate=pl.CostEstimate(flops=0, bytes_accessed=0, transcendentals=0),
            name=name,
        )(*wait, *given, *kept)
        self.last = (min(jax.tree.leaves(got), key=lambda a: a.size),)
        return got


def kept(shape, dtype):
    return pltpu.VMEM(shape, dtype)


def shaped(shape, dtype):
    return jax.ShapeDtypeStruct(shape, dtype)


def core_swap(v):
    return jax.tree.map(lambda a: lax.ppermute(a, "mp", [(i, i ^ 1) for i in range(4)]), v)


def chip_swap(v):
    return jax.tree.map(lambda a: lax.ppermute(a, "mp", [(i, i ^ 2) for i in range(4)]), v)


def core_groups():
    count = lax.axis_size("dp")
    return [[4 * d + 2 * x + c for d in range(count) for x in range(2)] for c in range(2)]


def ready_kernel(keep_q_ref, got_q_ref, keep_kv_ref, got_kv_ref, small_ref, out_ref):
    at = 0
    for keep_ref, got_ref in ((keep_q_ref, got_q_ref), (keep_kv_ref, got_kv_ref)):
        width = keep_ref.shape[1]
        out_ref[:, at : at + width] = (keep_ref[...] + got_ref[...].astype(F32)).astype(BF)
        at += width
    out_ref[:, at:] = small_ref[...]


def total_kernel(parts_ref, out_ref, *, width):
    total = jnp.sum(parts_ref[...].astype(F32), axis=0)
    small = total[:, width:]
    small = small + pltpu.roll(small, LANES // 2, 1)
    high, low = two_terms(small)
    lane = iota(small.shape, 1)
    small = jnp.where(lane < LANES // 2, high.astype(F32), low.astype(F32))
    total = jnp.concatenate([total[:, :width], small], axis=1).astype(BF)
    for place in range(out_ref.shape[0]):
        out_ref[place] = total


def to_group(v):
    groups = core_groups()
    return lax.all_to_all(v, ("dp", "mp"), 0, 0, tiled=True, axis_index_groups=groups)


def totals(order, parts, width):
    rows, columns = parts.shape
    count = len(core_groups()[0])
    shape = (count, rows // count, columns)
    kernel = functools.partial(total_kernel, width=width)
    return order.call(kernel, "total", (parts.reshape(shape),), (), shaped(shape, BF)).reshape(rows, columns)


class Stream:
    def __init__(self, order, *first):
        self.order, self.first = order, first
        bits = list(range(lax.axis_size("dp").bit_length() - 1))
        self.bits = [(0, 1), (1, 0)] + [(bit, bit) for bit in bits[2:]]
        self.steps = [self.start]
        self.steps += [functools.partial(self.halve, bits) for bits in self.bits[1:-1]]
        self.steps += [self.third, self.fourth]
        self.steps += [functools.partial(self.double, at) for at in range(len(bits), 0, -1)]

    def step(self):
        self.steps.pop(0)()

    def to_places(self, v, bits):
        way = []
        for place in range(lax.axis_size("dp")):
            for spot in range(4):
                bit = bits[spot % 2]
                to = 4 * place + (spot ^ 2) if bit is None else 4 * (place ^ (1 << bit)) + spot
                way.append((4 * place + spot, to))
        return lax.ppermute(v, ("dp", "mp"), way)

    def split(self, kernel, name, operands, shape, bits):
        self.keep, sent = self.order.call(kernel, name, operands, (), (shaped(shape, F32), shaped(shape, BF)))
        self.got = self.to_places(sent, bits)

    def start(self):
        bits = self.bits[0]
        rows, columns = self.first[0].shape[1] + self.first[2].shape[1], self.first[0].shape[2]
        kernel = functools.partial(first_kernel, bits=bits)
        self.split(kernel, "first", self.first, (2, rows // 2, columns), bits)

    def halve(self, bits):
        _, rows, columns = self.keep.shape
        kernel = functools.partial(halve_kernel, bits=bits)
        self.split(kernel, "halve", (self.keep, self.got), (2, rows // 2, columns), bits)

    def third(self):
        _, rows, columns = self.keep.shape
        bit = self.bits[-1][0]
        kernel = functools.partial(third_kernel, bit=bit)
        self.split(kernel, "third", (self.keep, self.got), (2, rows // 2, columns), (bit, None))

    def fourth(self):
        bit = self.bits[-1][0]
        kernel = functools.partial(fourth_kernel, bit=bit)
        self.split(kernel, "fourth", (self.keep, self.got), self.keep.shape[1:], (None, bit))

    def double(self, at):
        if at == len(self.bits):
            kernel, name, shape = add_kernel, "add", self.keep.shape
        else:
            kernel, name = functools.partial(join_kernel, bits=self.bits[at]), "join"
            shape = (2 * self.keep.shape[0], self.keep.shape[1])
        self.keep = self.order.call(kernel, name, (self.keep, self.got), (), shaped(shape, BF))
        self.got = self.to_places(self.keep, self.bits[at - 1])

    def finish(self, outs):
        while self.steps:
            self.step()
        kernel = functools.partial(final_kernel, bits=self.bits[0])
        return self.order.call(kernel, "final", (self.keep, self.got), (), outs)


def after(v, *others):
    return lax.optimization_barrier((v, others))[0]


def exchange(order, home, partner, reverse, wait=()):
    kernel = functools.partial(chain_kernel, reverse=reverse)
    total = order.call(kernel, "chain", (home, partner), (), shaped(home.shape, BF), wait=wait)
    return lax.ppermute(total, "mp", [(2, 0), (3, 1)] if reverse else [(0, 2), (1, 3)])


def per_device(
    layer_input,
    qkv_weight,
    gate_weight,
    gate_bias,
    out_weight,
    inner_weight,
    outer_weight,
    leading_norm_gain,
    leading_norm_bias,
    trailing_norm_gain,
    trailing_norm_bias,
    random_features,
    output_grad,
):
    seqs, length, width = layer_input.shape
    heads, head, feat = random_features.shape
    pairs = heads // 2
    count = seqs * length
    hidden = inner_weight.shape[1]
    bias = gate_bias.reshape(1, heads)
    gain1, shift1 = leading_norm_gain.reshape(1, width), leading_norm_bias.reshape(1, width)
    gain2, shift2 = trailing_norm_gain.reshape(1, width), trailing_norm_bias.reshape(1, width)

    n_dp = lax.axis_size("dp")
    order = Order()
    halves = order.call(
        pack_kernel,
        "pack",
        (inner_weight, outer_weight),
        (),
        shaped((2, width // 2, hidden), BF),
        [pltpu.SemaphoreType.DMA((2,))],
        hbm=True,
    )
    half_chip = chip_swap(halves)
    inner_core, outer_core = core_swap(inner_weight), core_swap(outer_weight)

    by_seq = (seqs, length, width)
    gates = (seqs, length, LANES)
    states = (pairs, LANES + EXTRA, 2 * feat)
    gate_rows = jnp.transpose(gate_weight)
    sources = (layer_input, qkv_weight, gate_rows, bias, gain1, shift1, random_features)
    normed1, values, c, admit, c_row, a_row, phi_k, away, home = order.call(
        keys_kernel,
        "keys",
        sources,
        (),
        (
            kept(by_seq, BF),
            kept(by_seq, F32),
            kept(gates, F32),
            kept(gates, F32),
            kept((seqs, heads, length), F32),
            kept((seqs, heads, length), F32),
            kept((seqs, heads, length, 2 * feat), BF),
            kept(states, BF),
            kept(states, BF),
        ),
        [pltpu.VMEM(a.shape, a.dtype) for a in sources] + [pltpu.SemaphoreType.DMA((len(sources),))],
        hbm=True,
    )
    partner_home, partner_away = core_swap(away), core_swap(home)
    got = exchange(order, home, partner_home, False, (half_chip,))
    half_twin = lax.ppermute(half_chip, "dp", [(i, i ^ 1) for i in range(n_dp)])

    phi_q, scores, num = order.call(
        scores_kernel,
        "scores",
        (qkv_weight, random_features),
        (normed1, phi_k, values, c, c_row, a_row),
        (
            kept((seqs, heads, length, 2 * feat), BF),
            kept((seqs, heads, length, length), BF),
            kept((seqs, heads, length, LANES), F32),
        ),
    )
    got = after(got, num)
    swapped = core_swap(got)
    half_twin = after(half_twin, num)
    half_both, half_both_twin = core_swap((half_chip, half_twin))
    full, start, mixed_low, resid, normed2 = order.call(
        mix_kernel,
        "mix",
        (layer_input, got, swapped, partner_home, partner_away, out_weight, gain2, shift2),
        (phi_q, c, num),
        (
            kept((seqs, heads, length, LANES), F32),
            kept((seqs, *states), BF),
            kept(by_seq, BF),
            kept(by_seq, F32),
            kept(by_seq, BF),
        ),
    )

    normed1, normed2, mixed_low = (a.reshape(count, width) for a in (normed1, normed2, mixed_low))
    layer_out, dn2, pre_grad, outer_keep, outer_send = order.call(
        feed_kernel,
        "feed",
        (
            output_grad.reshape(count, width), inner_weight, outer_weight, inner_core, outer_core, half_chip, half_twin,
            half_both, half_both_twin,
        ),
        (normed2, resid.reshape(count, width)),
        (
            shaped((count, width), F32),
            kept((count, width), F32),
            kept((4, count, hidden), BF),
            shaped((2, hidden, width), F32),
            shaped((2, hidden, width), BF),
        ),
        [pltpu.VMEM((2, 2, *inner_weight.shape), BF)],
    )
    outer_got = core_swap(outer_send)

    dres, low, sums2, num_grads, r, away_grads, home_grads = order.call(
        turn_kernel,
        "turn",
        (output_grad, gain2, out_weight),
        (dn2.reshape(by_seq), resid, full, phi_q, c),
        (
            kept(by_seq, F32),
            kept((count, width), BF),
            kept((8, width), F32),
            kept((seqs, heads, length, 2 * LANES), BF),
            kept(gates, F32),
            kept(states, BF),
            kept(states, BF),
        ),
    )
    partner_home_grads, partner_away_grads = core_swap(away_grads), core_swap(home_grads)
    got_grads = exchange(order, home_grads, partner_home_grads, True)

    inner_rows = width + width // 4
    inner_keep, inner_send = order.call(
        inner_kernel,
        "inner",
        (),
        (normed2, pre_grad, mixed_low, low),
        (shaped((2, inner_rows, hidden), F32), shaped((2, inner_rows, hidden), BF)),
    )
    stream = Stream(order, outer_keep, outer_got, inner_keep, core_swap(inner_send))
    stream.step()

    q_grad, k_part, v_part, k_col = order.call(
        back_kernel,
        "back",
        (random_features,),
        (phi_q, phi_k, values, num_grads, scores, c, c_row, a_row, start),
        (
            kept((count, width), BF),
            kept(by_seq, F32),
            kept(by_seq, F32),
            kept(gates, F32),
        ),
    )
    keep_q, send_q = order.call(
        queries_kernel,
        "queries",
        (),
        (normed1, q_grad),
        (shaped((width // 2, width), F32), shaped((width // 2, width), BF)),
    )
    got_grads = after(got_grads, k_col)
    swapped_grads = core_swap(got_grads)

    kv_grad, logit_low, bias_sum, keep_kv, send_kv = order.call(
        cross_kernel,
        "cross",
        (got_grads, swapped_grads, partner_home_grads, partner_away_grads, random_features),
        (away, home, start, phi_k, values, c, admit, r, k_col, k_part, v_part, normed1),
        (
            kept((count, 2 * width), BF),
            kept((count, LANES), BF),
            kept((8, LANES), F32),
            shaped((width // 2, 2 * width), F32),
            shaped((width // 2, 2 * width), BF),
        ),
    )
    got_q, got_kv = core_swap(send_q), core_swap(send_kv)
    stream.step()
    dx, small = order.call(
        close_kernel,
        "close",
        (layer_input.reshape(count, width), qkv_weight, gate_rows, gain1),
        (q_grad, kv_grad, logit_low, bias_sum, normed1, dres.reshape(count, width), sums2),
        (shaped((count, width), F32), shaped((width // 2, LANES), BF)),
    )
    ready = order.call(
        ready_kernel,
        "ready",
        (keep_q, got_q, keep_kv, got_kv, small),
        (),
        shaped((width // 2, 3 * width + LANES), BF),
    )
    parts = to_group(ready)
    stream.step()
    total = to_group(totals(order, parts, 3 * width))
    outer_total, inner_total, quarter = stream.finish(
        (shaped((hidden, width), F32), shaped((width, hidden), F32), shaped((width // 4, width), BF))
    )
    quarters = jnp.stack([quarter, chip_swap(quarter)])

    qkv_grad, wo_grad, gate_grad, bias_grad, *norm_grads = order.call(
        assemble_kernel,
        "assemble",
        (total, core_swap(total), quarters, core_swap(quarters)),
        (),
        (
            shaped((width, 3 * width), F32),
            shaped((width, width), F32),
            shaped((heads, width), F32),
            shaped((1, heads), F32),
            *[shaped((1, width), F32)] * 4,
        ),
    )
    return (
        layer_out.reshape(by_seq),
        dx.reshape(by_seq),
        qkv_grad,
        jnp.transpose(gate_grad),
        bias_grad.reshape(heads),
        wo_grad,
        inner_total,
        outer_total,
        *(a.reshape(width) for a in norm_grads),
    )


def solution(mesh):
    in_specs = (
        P("dp", "mp", None),
        P(),
        P(),
        P(),
        P(),
        P(None, "mp"),
        P("mp", None),
        P(),
        P(),
        P(),
        P(),
        P(),
        P("dp", "mp", None),
    )
    out_specs = (
        P("dp", "mp", None),
        P("dp", "mp", None),
        P(),
        P(),
        P(),
        P(),
        P(None, "mp"),
        P("mp", None),
        P(),
        P(),
        P(),
        P(),
    )
    return jax.shard_map(
        per_device, mesh=mesh, in_specs=in_specs, out_specs=out_specs, check_vma=False
    )
```

time: 636 us -> 192 us (0.30); the launches traced: 626 us -> 192 us
  matrix products: 174 us -> 0 us
  waiting for transfers between devices: 209 us -> 93.3 us
  local copies, waits for them, and re-layouts: 92.7 us -> 1.28 us
  other arithmetic: 74.6 us -> 0.03 us
  Pallas kernels: 0 us -> 62.3 us
  blocking collectives: 57.9 us -> 0 us
  starting transfers between devices: 0.97 us -> 33.9 us
  between operations: 15.5 us -> 0.99 us
    dot_general x33 -> x0, matrix products: 174 us -> none  [the longest x4 31.3 us: features(): jnp.einsum('...hd,hdf->...hf', values, frequencies, precision=exact)]
    ppermute x0 -> x28, waiting for transfers between devices: none -> 93.3 us  [the longest x7 74.7 us: to_places(): return lax.ppermute(v, ('dp', 'mp'), way)]
    psum x2 -> x0, waiting for transfers between devices: 90.6 us -> none  [the longest x1 90.6 us: per_device(): lax.psum((qkv_part, out_weight_part, gate_weight_part, gate_bias_part, no...]
    reduce_scatter x2 -> x0, waiting for transfers between devices: 69.6 us -> none  [the longest x1 39.1 us: per_device(): lax.psum_scatter(contract(pre_grad, inner_weight, 1, 1), 'mp', scatter_di...]
    pallas_call x0 -> x24, Pallas kernels: none -> 62.3 us  [call(): pl.pallas_call(lambda *refs: kernel(*refs[len(wait):]), out_shape=outs, i...]
    all_gather x4 -> x0, waiting for transfers between devices: 48.9 us -> none  [the longest x1 41.7 us: per_device(): gathered = lax.all_gather(trailing_normalized, 'mp', axis=0, tiled=True)]
    psum x1 -> x0, blocking collectives: 40.2 us -> none  [per_device(): lax.psum((qkv_part, out_weight_part, gate_weight_part, gate_bias_part, no...]
    ppermute x0 -> x28, starting transfers between devices: none -> 24.3 us  [the longest x7 8.74 us: to_places(): return lax.ppermute(v, ('dp', 'mp'), way)]
  transfers between devices with their start and end apart: 8 -> 30, of which waited for: 5 -> 14; matrix products, arithmetic and copies ran while one was open for 38% -> 0% of each run, Pallas kernels for 0% -> 20%
where the time goes in v2:
time: 192 us
  waiting for transfers between devices  93.3 us (49%)
  Pallas kernels  62.3 us (32%)
  starting transfers between devices  33.9 us (18%)
    ppermute x7, waiting for transfers between devices, to_places(): return lax.ppermute(v, ('dp', 'mp'), way)  74.7 us
    pallas_call x24, Pallas kernels, call(): pl.pallas_call(lambda *refs: kernel(*refs[len(wait):]), out_shape=outs, i...  62.3 us
    ppermute x16, waiting for transfers between devices, core_swap(): lax.ppermute(a, 'mp', [(i, i ^ 1) for i in range(4)])  9.99 us
    all_to_all x2, starting transfers between devices, to_group(): lax.all_to_all(v, ('dp', 'mp'), 0, 0, tiled=True, axis_index_groups=groups)  9.61 us
    ppermute x7, starting transfers between devices, to_places(): return lax.ppermute(v, ('dp', 'mp'), way)  8.74 us
    ppermute x2, starting transfers between devices, exchange(): lax.ppermute(total, 'mp', [(2, 0), (3, 1)] if reverse else [(0, 2), (1, 3)])  4.87 us
    ppermute x2, waiting for transfers between devices, chip_swap(): lax.ppermute(a, 'mp', [(i, i ^ 2) for i in range(4)])  4.61 us
    ppermute x2, starting transfers between devices, chip_swap(): lax.ppermute(a, 'mp', [(i, i ^ 2) for i in range(4)])  4.47 us
  transfers between devices with their start and end apart: 30, of which 14 were waited for; matrix products, arithmetic and copies ran while one was open for 0% of the time, Pallas kernels for 20%

profile of v2, /device:TPU:0, one launch (start us, length us, event | category | flops | bytes accessed | tf_op | source)
XLA Modules:
  0.0 191.8 jit_solution(18067693583375007364)
XLA Ops:
  0.6 1.1 pack.1.refs_0_
  1.7 3.0 %collective-permute-start = (bf16[2,256,512]{2,1,0:T(8,128)(2,1)S(1)}, bf16[2,256,512]{2,1,0:T(8,128)(2,1)S(1)}, u32[]{:S(2)}, u32[]{:S(2)}) collective-permute-start(bf16[2,256,512]{2,1,0:T(8,128)(2,1)S(1)} %pack.1.refs_0_), channel_id=1, source_target_pairs={{0,2},{1,3},{2,0},{3,1},{4,6},{5,7},{6,4},{7,5},{8,10},{9,11},{10,... | collective-permute-start | bytes 1572872 | tf_op jit(solution)/shard_map/ppermute | solution.py:747
  4.7 10.7 %keys.1 = (bf16[2,256,512]{2,1,0:T(8,128)(2,1)S(1)}, f32[2,256,512]{2,1,0:T(8,128)S(1)}, f32[2,256,128]{2,1,0:T(8,128)S(1)}, f32[2,256,128]{2,1,0:T(8,128)S(1)},...) custom-call(bf16[2,256,512]{2,1,0:T(8,128)(2,1)S(1)} %pack.1.refs_0_, ...), custom_call_target="tpu_custom_call" | custom-call | tf_op jit(solution)/shard_map/keys/pallas_call | solution.py:718
  15.5 1.1 collective-permute-done.refs_1_.refs_6_
  16.6 1.8 collective-permute-start.7
  18.6 3.6 %collective-permute-start.2 = (bf16[4,144,256]{2,1,0:T(8,128)(2,1)S(1)}, bf16[4,144,256]{2,1,0:T(8,128)(2,1)S(1)}, u32[]{:S(2)}, u32[]{:S(2)}) collective-permute-start(bf16[4,144,256]{2,1,0:T(8,128)(2,1)S(1)} %chain.2.refs_0_), channel_id=1, source_target_pairs={{0,2},{1,3},{4,6},{5,7},{8,10},{9,11},{12,14},{13,15},{16,18},{17,... | collective-permute-start | bytes 884744 | tf_op jit(solution)/shard_map/ppermute | solution.py:860
  22.3 0.5 collective-permute-start.5
  22.9 7.6 %scores.1 = (bf16[2,8,256,256]{3,2,1,0:T(8,128)(2,1)S(1)}, bf16[2,8,256,256]{3,2,1,0:T(8,128)(2,1)S(1)}, f32[2,8,256,128]{3,2,1,0:T(8,128)S(1)}) custom-call(bf16[4,144,256]{2,1,0:T(8,128)(2,1)S(1)} %chain.2.refs_0_, bf16[512,1536]{1,0:T(8,128)(2,1)S(1)} %copy-done, f32[8,64,128]{2,1,0:T(8,128)S(1)} %copy-done.3, ...), custom_call_target="tpu_custom_call" | custom-call | tf_op jit(solution)/shard_map/scores/pallas_call | solution.py:718
  30.5 0.5 collective-permute-start.8
  31.5 2.2 %collective-permute-done.3.refs_3_ = bf16[4,144,256]{2,1,0:T(8,128)(2,1)S(1)} collective-permute-done((bf16[4,144,256]{2,1,0:T(8,128)(2,1)S(1)}, bf16[4,144,256]{2,1,0:T(8,128)(2,1)S(1)}, u32[]{:S(2)}, u32[]{:S(2)}) %collective-permute-start.3) | collective-permute-done | bytes 294944 | tf_op jit(solution)/shard_map/ppermute | solution.py:743
  33.7 3.6 %mix.1 = (f32[2,8,256,128]{3,2,1,0:T(8,128)S(1)}, bf16[2,4,144,256]{3,2,1,0:T(8,128)(2,1)S(1)}, bf16[2,256,512]{2,1,0:T(8,128)(2,1)S(1)}, f32[2,256,512]{2,1,0:T(8,128)S(1)}, bf16[2,256,512]{2,1,0:T(8,128)(2,1)S(1)}) custom-call(f32[2,8,256,128]{3,2,1,0:T(8,128)S(1)} %get-tuple-element.86.refs_0_.refs_11_, f32[2,256,512]{2,1,0:T(8,128)S(1)} %copy-done.1, ...), custom_call_target="tpu_custom_call" | custom-call | tf_op jit(solution)/shard_map/mix/pallas_call | solution.py:718
  37.4 6.9 %feed.1 = (f32[512,512]{1,0:T(8,128)}, f32[512,512]{1,0:T(8,128)S(1)}, bf16[4,512,512]{2,1,0:T(8,128)(2,1)S(1)}, f32[2,512,512]{2,1,0:T(8,128)S(1)}, bf16[2,512,512]{2,1,0:T(8,128)(2,1)S(1)}) custom-call(bf16[2,256,512]{2,1,0:T(8,128)(2,1)S(1)} %get-tuple-element.89.refs_0_, f32[512,512]{1,0:T(8,128)S(1)} %bitcast.30, bf16[512,512]{1,0:T(8,128)(2,1)S(1)} %copy-done.4, ...), custom_call_target="tpu_custom_call" | custom-call | tf_op jit(solution)/shard_map/feed/pallas_call | solution.py:718
  44.3 1.2 copy-done.7
  45.5 8.4 %turn.1 = (f32[2,256,512]{2,1,0:T(8,128)S(1)}, bf16[512,512]{1,0:T(8,128)(2,1)S(1)}, f32[8,512]{1,0:T(8,128)S(1)}, bf16[2,8,256,256]{3,2,1,0:T(8,128)(2,1)S(1)},...) custom-call(f32[512,512]{1,0:T(8,128)S(1)} %copy-done.7, ...), custom_call_target="tpu_custom_call" | custom-call | tf_op jit(solution)/shard_map/turn/pallas_call | solution.py:718
  53.9 0.4 collective-permute-start.10
  54.4 1.2 collective-permute-done.10.refs_2_.refs_3_
  55.8 1.6 inner.1
  57.3 0.4 collective-permute-start.12
  57.9 4.0 %collective-permute-done.11.refs_2_ = bf16[2,512,512]{2,1,0:T(8,128)(2,1)S(1)} collective-permute-done((bf16[2,512,512]{2,1,0:T(8,128)(2,1)S(1)}, bf16[2,512,512]{2,1,0:T(8,128)(2,1)S(1)}, u32[]{:S(2)}, u32[]{:S(2)}) %collective-permute-start.11) | collective-permute-done | bytes 1048608 | tf_op jit(solution)/shard_map/ppermute | solution.py:743
  61.9 0.7 first.1
  62.6 0.8 collective-permute-start.16
  63.4 1.3 collective-permute-start.13
  64.7 1.0 collective-permute-start.15
  65.7 5.5 %back.1 = (bf16[512,512]{1,0:T(8,128)(2,1)S(1)}, f32[2,256,512]{2,1,0:T(8,128)S(1)}, f32[2,256,512]{2,1,0:T(8,128)S(1)}, f32[2,256,128]{2,1,0:T(8,128)S(1)}) custom-call(f32[2,576,512]{2,1,0:T(8,128)S(1)} %get-tuple-element.105.refs_0_.refs_1_, f32[8,64,128]{2,1,0:T(8,128)S(1)} %copy-done.3, ...), custom_call_target="tpu_custom_call" | custom-call | tf_op jit(solution)/shard_map/back/pallas_call | solution.py:718
  71.2 3.9 %collective-permute-done.13.refs_1_ = bf16[4,144,256]{2,1,0:T(8,128)(2,1)S(1)} collective-permute-done((bf16[4,144,256]{2,1,0:T(8,128)(2,1)S(1)}, bf16[4,144,256]{2,1,0:T(8,128)(2,1)S(1)}, u32[]{:S(2)}, u32[]{:S(2)}) %collective-permute-start.13) | collective-permute-done | bytes 294944 | tf_op jit(solution)/shard_map/ppermute | solution.py:860
  75.2 0.5 queries.1
  75.7 1.0 collective-permute-done.14.refs_2_
  76.7 6.2 %cross.1 = (bf16[512,1024]{1,0:T(8,128)(2,1)S(1)}, bf16[512,128]{1,0:T(8,128)(2,1)S(1)}, f32[8,128]{1,0:T(8,128)S(1)}, f32[256,1024]{1,0:T(8,128)S(1)}, bf16[256,1024]{1,0:T(8,128)(2,1)S(1)}) custom-call(f32[256,512]{1,0:T(8,128)S(1)} %get-tuple-element.111.refs_0_.refs_1_, bf16[4,144,256]{2,1,0:T(8,128)(2,1)S(1)} %collective-permute-done.13.refs_1_, ...), custom_call_target="tpu_custom_call" | custom-call | tf_op jit(solution)/shard_map/cross/pallas_call | solution.py:718
  83.9 2.5 %close.1 = (f32[512,512]{1,0:T(8,128)}, bf16[256,128]{1,0:T(8,128)(2,1)S(1)}) custom-call(f32[2,288,512]{2,1,0:T(8,128)S(1)} %get-tuple-element.119.refs_0_.refs_1_, f32[512,512]{1,0:T(8,128)S(1)} %bitcast.26, bf16[512,1536]{1,0:T(8,128)(2,1)S(1)} %copy-done, bf16[8,512]{1,0:T(8,128)(2,1)S(1)} %bitcast.42, f32[1,512]{1,0:T(1,128)S(1)} %bitcast.44, ...), custom_call_target="tpu_custom_call" | custom-call | tf_op jit(solution)/shard_map/close/pallas_call | solution.py:718
  86.4 1.0 ready.1.refs_0_
  87.5 4.0 %all-to-all-start = ((bf16[16,16,1664]{2,1,0:T(8,128)(2,1)}), bf16[16,16,1664]{2,1,0:T(8,128)(2,1)S(1)}, u32[]{:S(2)}, u32[]{:S(2)}) async-start(bf16[16,16,1664]{2,1,0:T(8,128)(2,1)} %bitcast.16), calls=%async_computation | async-start | bytes 1703936 | tf_op jit(solution)/shard_map/all_to_all | solution.py:778
  91.5 1.9 %collective-permute-start.19 = (bf16[2,288,512]{2,1,0:T(8,128)(2,1)S(1)}, bf16[2,288,512]{2,1,0:T(8,128)(2,1)S(1)}, u32[]{:S(2)}, u32[]{:S(2)}) collective-permute-start(bf16[2,288,512]{2,1,0:T(8,128)(2,1)S(1)} %get-tuple-element.128), channel_id=1, source_target_pairs={{0,8},{1,5},{2,10},{3,7},{4,12},{5,1},{6,14},{7,3},{8,0},{9,13},{1... | collective-permute-start | bytes 1769480 | tf_op jit(solution)/shard_map/ppermute | solution.py:809
  93.4 20.6 %collective-permute-done.19.refs_2_ = bf16[2,288,512]{2,1,0:T(8,128)(2,1)S(1)} collective-permute-done((bf16[2,288,512]{2,1,0:T(8,128)(2,1)S(1)}, bf16[2,288,512]{2,1,0:T(8,128)(2,1)S(1)}, u32[]{:S(2)}, u32[]{:S(2)}) %collective-permute-start.19) | collective-permute-done | bytes 589856 | tf_op jit(solution)/shard_map/ppermute | solution.py:809
  114.2 1.1 total.1.refs_0_
  115.3 5.6 %all-to-all-start.1 = ((bf16[16,16,1664]{2,1,0:T(8,128)(2,1)}), bf16[16,16,1664]{2,1,0:T(8,128)(2,1)S(1)}, u32[]{:S(2)}, u32[]{:S(2)}) async-start(bf16[16,16,1664]{2,1,0:T(8,128)(2,1)} %total.1.refs_0_), calls=%async_computation.1 | async-start | bytes 1703936 | tf_op jit(solution)/shard_map/all_to_all | solution.py:778
  121.0 2.8 %collective-permute-start.20 = (bf16[2,144,512]{2,1,0:T(8,128)(2,1)S(1)}, bf16[2,144,512]{2,1,0:T(8,128)(2,1)S(1)}, u32[]{:S(2)}, u32[]{:S(2)}) collective-permute-start(bf16[2,144,512]{2,1,0:T(8,128)(2,1)S(1)} %get-tuple-element.130), channel_id=1, source_target_pairs={{0,16},{1,3},{2,18},{3,1},{4,20},{5,7},{6,22},{7,5},{8,24},{9,11},... | collective-permute-start | bytes 884744 | tf_op jit(solution)/shard_map/ppermute | solution.py:809
  123.8 27.8 %collective-permute-done.20.refs_2_ = bf16[2,144,512]{2,1,0:T(8,128)(2,1)S(1)} collective-permute-done((bf16[2,144,512]{2,1,0:T(8,128)(2,1)S(1)}, bf16[2,144,512]{2,1,0:T(8,128)(2,1)S(1)}, u32[]{:S(2)}, u32[]{:S(2)}) %collective-permute-start.20) | collective-permute-done | bytes 294944 | tf_op jit(solution)/shard_map/ppermute | solution.py:809
  151.7 1.5 collective-permute-start.21
  153.3 3.7 %collective-permute-done.21.refs_2_ = bf16[144,512]{1,0:T(8,128)(2,1)S(1)} collective-permute-done((bf16[144,512]{1,0:T(8,128)(2,1)S(1)}, bf16[144,512]{1,0:T(8,128)(2,1)S(1)}, u32[]{:S(2)}, u32[]{:S(2)}) %collective-permute-start.21) | collective-permute-done | bytes 147488 | tf_op jit(solution)/shard_map/ppermute | solution.py:809
  157.1 6.1 %collective-permute-done.22.refs_2_ = bf16[144,512]{1,0:T(8,128)(2,1)S(1)} collective-permute-done((bf16[144,512]{1,0:T(8,128)(2,1)S(1)}, bf16[144,512]{1,0:T(8,128)(2,1)S(1)}, u32[]{:S(2)}, u32[]{:S(2)}) %collective-permute-start.22) | collective-permute-done | bytes 147488 | tf_op jit(solution)/shard_map/ppermute | solution.py:809
  163.4 8.0 %collective-permute-done.23.refs_2_ = bf16[288,512]{1,0:T(8,128)(2,1)S(1)} collective-permute-done((bf16[288,512]{1,0:T(8,128)(2,1)S(1)}, bf16[288,512]{1,0:T(8,128)(2,1)S(1)}, u32[]{:S(2)}, u32[]{:S(2)}) %collective-permute-start.23) | collective-permute-done | bytes 294944 | tf_op jit(solution)/shard_map/ppermute | solution.py:809
  171.6 1.5 collective-permute-start.24
  173.1 8.4 %collective-permute-done.24.refs_2_ = bf16[576,512]{1,0:T(8,128)(2,1)S(1)} collective-permute-done((bf16[576,512]{1,0:T(8,128)(2,1)S(1)}, bf16[576,512]{1,0:T(8,128)(2,1)S(1)}, u32[]{:S(2)}, u32[]{:S(2)}) %collective-permute-start.24) | collective-permute-done | bytes 589856 | tf_op jit(solution)/shard_map/ppermute | solution.py:809
  181.5 1.5 final.1
  183.0 1.5 collective-permute-start.26
  184.5 3.5 %collective-permute-done.26 = bf16[128,512]{1,0:T(8,128)(2,1)S(1)} collective-permute-done((bf16[128,512]{1,0:T(8,128)(2,1)S(1)}, bf16[128,512]{1,0:T(8,128)(2,1)S(1)}, u32[]{:S(2)}, u32[]{:S(2)}) %collective-permute-start.26) | collective-permute-done | bytes 131104 | tf_op jit(solution)/shard_map/ppermute | solution.py:747
  188.1 1.5 collective-permute-done.27.refs_4_
  189.6 2.2 %assemble.1 = (f32[512,1536]{1,0:T(8,128)}, f32[512,512]{1,0:T(8,128)}, f32[8,512]{1,0:T(8,128)}, f32[1,8]{1,0:T(1,128)}, f32[1,512]{1,0:T(1,128)}, /*index=5*/f...) custom-call(bf16[128,512]{1,0:T(8,128)(2,1)S(1)} %get-tuple-element.133.refs_0_, bf16[256,1664]{1,0:T(8,128)(2,1)S(1)} %bitcast.33, ...), custom_call_target="tpu_custom_call" | custom-call | tf_op jit(solution)/shard_map/assemble/pallas_call | solution.py:718
  (61 shorter events, 3.1 us)
Async XLA Ops:
  1.7 14.9 %collective-permute-start = (bf16[2,256,512]{2,1,0:T(8,128)(2,1)S(1)}, bf16[2,256,512]{2,1,0:T(8,128)(2,1)S(1)}, u32[]{:S(2)}, u32[]{:S(2)}) collective-permute-start(bf16[2,256,512]{2,1,0:T(8,128)(2,1)S(1)} %pack.1.refs_0_), channel_id=1, source_target_pairs={{0,2},{1,3},{2,0},{3,1},{4,6},{5,7},{6,4},{7,5},{8,10},{9,11},{10,... | collective-permute-start | bytes 1572872 | tf_op jit(solution)/shard_map/ppermute | solution.py:747
  4.7 17.6 %copy-start.4 = (bf16[512,512]{1,0:T(8,128)(2,1)S(1)}, bf16[512,512]{1,0:T(8,128)(2,1)}, u32[]{:S(2)}) copy-start(bf16[512,512]{1,0:T(8,128)(2,1)} %refs_2_.6) | copy-start | bytes 1572868
  4.7 18.1 %copy-start.5 = (bf16[512,512]{1,0:T(8,128)(2,1)S(1)}, bf16[512,512]{1,0:T(8,128)(2,1)}, u32[]{:S(2)}) copy-start(bf16[512,512]{1,0:T(8,128)(2,1)} %refs_3_.2) | copy-start | bytes 1572868
  4.7 18.2 %copy-start = (bf16[512,1536]{1,0:T(8,128)(2,1)S(1)}, bf16[512,1536]{1,0:T(8,128)(2,1)}, u32[]{:S(2)}) copy-start(bf16[512,1536]{1,0:T(8,128)(2,1)} %refs_2_.7) | copy-start | bytes 4718596
  4.7 18.2 %copy-start.3 = (f32[8,64,128]{2,1,0:T(8,128)S(1)}, f32[8,64,128]{2,1,0:T(8,128)}, u32[]{:S(2)}) copy-start(f32[8,64,128]{2,1,0:T(8,128)} %refs_5_.1) | copy-start | bytes 786436
  15.5 3.0 %collective-permute-start.1 = (bf16[4,144,256]{2,1,0:T(8,128)(2,1)S(1)}, bf16[4,144,256]{2,1,0:T(8,128)(2,1)S(1)}, u32[]{:S(2)}, u32[]{:S(2)}) collective-permute-start(bf16[4,144,256]{2,1,0:T(8,128)(2,1)S(1)} %get-tuple-element.80.refs_6_), channel_id=1, source_target_pairs={{0,1},{1,0},{2,3},{3,2},{4,5},{5,4},{6,7},{7,6},{8,9},{9,8},{10,11... | collective-permute-start | bytes 884744 | tf_op jit(solution)/shard_map/ppermute | solution.py:743
  16.6 13.9 %collective-permute-start.7 = (bf16[2,256,512]{2,1,0:T(8,128)(2,1)S(1)}, bf16[2,256,512]{2,1,0:T(8,128)(2,1)S(1)}, u32[]{:S(2)}, u32[]{:S(2)}) collective-permute-start(bf16[2,256,512]{2,1,0:T(8,128)(2,1)S(1)} %collective-permute-done.refs_1_.refs_6_), channel_id=1, source_target_pairs={{0,4},{4,0},{8,12},{12,8},{16,20},{20,16},{24,28},{28,24},{1,5},{5... | collective-permute-start | bytes 1572872 | tf_op jit(solution)/shard_map/ppermute | solution.py:927
  18.6 12.4 %collective-permute-start.2 = (bf16[4,144,256]{2,1,0:T(8,128)(2,1)S(1)}, bf16[4,144,256]{2,1,0:T(8,128)(2,1)S(1)}, u32[]{:S(2)}, u32[]{:S(2)}) collective-permute-start(bf16[4,144,256]{2,1,0:T(8,128)(2,1)S(1)} %chain.2.refs_0_), channel_id=1, source_target_pairs={{0,2},{1,3},{4,6},{5,7},{8,10},{9,11},{12,14},{13,15},{16,18},{17,... | collective-permute-start | bytes 884744 | tf_op jit(solution)/shard_map/ppermute | solution.py:860
  22.2 8.9 %collective-permute-start.4 = (bf16[4,144,256]{2,1,0:T(8,128)(2,1)S(1)}, bf16[4,144,256]{2,1,0:T(8,128)(2,1)S(1)}, u32[]{:S(2)}, u32[]{:S(2)}) collective-permute-start(bf16[4,144,256]{2,1,0:T(8,128)(2,1)S(1)} %get-tuple-element.79.refs_2_.refs_7_), channel_id=1, source_target_pairs={{0,1},{1,0},{2,3},{3,2},{4,5},{5,4},{6,7},{7,6},{8,9},{9,8},{10,11... | collective-permute-start | bytes 884744 | tf_op jit(solution)/shard_map/ppermute | solution.py:743
  22.3 15.1 %collective-permute-start.5 = (bf16[512,512]{1,0:T(8,128)(2,1)S(1)}, bf16[512,512]{1,0:T(8,128)(2,1)S(1)}, u32[]{:S(2)}, u32[]{:S(2)}) collective-permute-start(bf16[512,512]{1,0:T(8,128)(2,1)S(1)} %copy-done.4), channel_id=1, source_target_pairs={{0,1},{1,0},{2,3},{3,2},{4,5},{5,4},{6,7},{7,6},{8,9},{9,8},{10,11... | collective-permute-start | bytes 1572872 | tf_op jit(solution)/shard_map/ppermute | solution.py:743
  22.8 14.6 %collective-permute-start.6 = (bf16[512,512]{1,0:T(8,128)(2,1)S(1)}, bf16[512,512]{1,0:T(8,128)(2,1)S(1)}, u32[]{:S(2)}, u32[]{:S(2)}) collective-permute-start(bf16[512,512]{1,0:T(8,128)(2,1)S(1)} %copy-done.5), channel_id=1, source_target_pairs={{0,1},{1,0},{2,3},{3,2},{4,5},{5,4},{6,7},{7,6},{8,9},{9,8},{10,11... | collective-permute-start | bytes 1572872 | tf_op jit(solution)/shard_map/ppermute | solution.py:743
  22.9 10.8 %copy-start.1 = (f32[2,256,512]{2,1,0:T(8,128)S(1)}, f32[2,256,512]{2,1,0:T(8,128)}, u32[]{:S(2)}) copy-start(f32[2,256,512]{2,1,0:T(8,128)} %refs_1_.9) | copy-start | bytes 3145732
  22.9 10.8 %copy-start.6 = (bf16[512,512]{1,0:T(8,128)(2,1)S(1)}, bf16[512,512]{1,0:T(8,128)(2,1)}, u32[]{:S(2)}) copy-start(bf16[512,512]{1,0:T(8,128)(2,1)} %refs_3_.3) | copy-start | bytes 1572868
  22.9 10.8 %copy-start.10 = (f32[512]{0:T(512)S(1)}, f32[512]{0:T(512)}, u32[]{:S(2)}) copy-start(f32[512]{0:T(512)} %param.22) | copy-start | bytes 6148
  22.9 10.8 %copy-start.11 = (f32[512]{0:T(512)S(1)}, f32[512]{0:T(512)}, u32[]{:S(2)}) copy-start(f32[512]{0:T(512)} %param.23) | copy-start | bytes 6148
  30.5 6.9 %collective-permute-start.8 = (bf16[2,256,512]{2,1,0:T(8,128)(2,1)S(1)}, bf16[2,256,512]{2,1,0:T(8,128)(2,1)S(1)}, u32[]{:S(2)}, u32[]{:S(2)}) collective-permute-start(bf16[2,256,512]{2,1,0:T(8,128)(2,1)S(1)} %collective-permute-done.refs_1_.refs_6_), channel_id=1, source_target_pairs={{0,1},{1,0},{2,3},{3,2},{4,5},{5,4},{6,7},{7,6},{8,9},{9,8},{10,11... | collective-permute-start | bytes 1572872 | tf_op jit(solution)/shard_map/ppermute | solution.py:743
  31.0 6.4 %collective-permute-start.9 = (bf16[2,256,512]{2,1,0:T(8,128)(2,1)S(1)}, bf16[2,256,512]{2,1,0:T(8,128)(2,1)S(1)}, u32[]{:S(2)}, u32[]{:S(2)}) collective-permute-start(bf16[2,256,512]{2,1,0:T(8,128)(2,1)S(1)} %collective-permute-done.7.refs_7_), channel_id=1, source_target_pairs={{0,1},{1,0},{2,3},{3,2},{4,5},{5,4},{6,7},{7,6},{8,9},{9,8},{10,11... | collective-permute-start | bytes 1572872 | tf_op jit(solution)/shard_map/ppermute | solution.py:743
  31.1 2.6 %collective-permute-start.3 = (bf16[4,144,256]{2,1,0:T(8,128)(2,1)S(1)}, bf16[4,144,256]{2,1,0:T(8,128)(2,1)S(1)}, u32[]{:S(2)}, u32[]{:S(2)}) collective-permute-start(bf16[4,144,256]{2,1,0:T(8,128)(2,1)S(1)} %collective-permute-done.2.refs_2_), channel_id=1, source_target_pairs={{0,1},{1,0},{2,3},{3,2},{4,5},{5,4},{6,7},{7,6},{8,9},{9,8},{10,11... | collective-permute-start | bytes 884744 | tf_op jit(solution)/shard_map/ppermute | solution.py:743
  33.7 3.7 %copy-start.2 = (f32[2,256,512]{2,1,0:T(8,128)S(1)}, f32[2,256,512]{2,1,0:T(8,128)}, u32[]{:S(2)}) copy-start(f32[2,256,512]{2,1,0:T(8,128)} %refs_1_.10) | copy-start | bytes 3145732
  44.3 1.2 copy-start.7
  53.9 1.7 collective-permute-start.10
  57.3 4.6 %collective-permute-start.12 = (bf16[2,640,512]{2,1,0:T(8,128)(2,1)S(1)}, bf16[2,640,512]{2,1,0:T(8,128)(2,1)S(1)}, u32[]{:S(2)}, u32[]{:S(2)}) collective-permute-start(bf16[2,640,512]{2,1,0:T(8,128)(2,1)S(1)} %get-tuple-element.104), channel_id=1, source_target_pairs={{0,1},{1,0},{2,3},{3,2},{4,5},{5,4},{6,7},{7,6},{8,9},{9,8},{10,11... | collective-permute-start | bytes 3932168 | tf_op jit(solution)/shard_map/ppermute | solution.py:743
  57.8 4.2 %collective-permute-start.11 = (bf16[2,512,512]{2,1,0:T(8,128)(2,1)S(1)}, bf16[2,512,512]{2,1,0:T(8,128)(2,1)S(1)}, u32[]{:S(2)}, u32[]{:S(2)}) collective-permute-start(bf16[2,512,512]{2,1,0:T(8,128)(2,1)S(1)} %get-tuple-element.103), channel_id=1, source_target_pairs={{0,1},{1,0},{2,3},{3,2},{4,5},{5,4},{6,7},{7,6},{8,9},{9,8},{10,11... | collective-permute-start | bytes 3145736 | tf_op jit(solution)/shard_map/ppermute | solution.py:743
  62.6 20.9 %collective-permute-start.16 = (bf16[2,576,512]{2,1,0:T(8,128)(2,1)S(1)}, bf16[2,576,512]{2,1,0:T(8,128)(2,1)S(1)}, u32[]{:S(2)}, u32[]{:S(2)}) collective-permute-start(bf16[2,576,512]{2,1,0:T(8,128)(2,1)S(1)} %get-tuple-element.118), channel_id=1, source_target_pairs={{0,4},{1,9},{2,6},{3,11},{4,0},{5,13},{6,2},{7,15},{8,12},{9,1},{1... | collective-permute-start | bytes 3538952 | tf_op jit(solution)/shard_map/ppermute | solution.py:809
  63.4 11.7 %collective-permute-start.13 = (bf16[4,144,256]{2,1,0:T(8,128)(2,1)S(1)}, bf16[4,144,256]{2,1,0:T(8,128)(2,1)S(1)}, u32[]{:S(2)}, u32[]{:S(2)}) collective-permute-start(bf16[4,144,256]{2,1,0:T(8,128)(2,1)S(1)} %chain.3.refs_0_), channel_id=1, source_target_pairs={{2,0},{3,1},{6,4},{7,5},{10,8},{11,9},{14,12},{15,13},{18,16},{19,... | collective-permute-start | bytes 884744 | tf_op jit(solution)/shard_map/ppermute | solution.py:860
  64.7 11.0 %collective-permute-start.15 = (bf16[4,144,256]{2,1,0:T(8,128)(2,1)S(1)}, bf16[4,144,256]{2,1,0:T(8,128)(2,1)S(1)}, u32[]{:S(2)}, u32[]{:S(2)}) collective-permute-start(bf16[4,144,256]{2,1,0:T(8,128)(2,1)S(1)} %get-tuple-element.97.refs_1_), channel_id=1, source_target_pairs={{0,1},{1,0},{2,3},{3,2},{4,5},{5,4},{6,7},{7,6},{8,9},{9,8},{10,11... | collective-permute-start | bytes 884744 | tf_op jit(solution)/shard_map/ppermute | solution.py:743
  75.1 1.6 collective-permute-start.14
  82.9 0.9 copy-start.8
  83.0 0.9 copy-start.9
  83.0 3.5 %collective-permute-start.18 = (bf16[256,1024]{1,0:T(8,128)(2,1)S(1)}, bf16[256,1024]{1,0:T(8,128)(2,1)S(1)}, u32[]{:S(2)}, u32[]{:S(2)}) collective-permute-start(bf16[256,1024]{1,0:T(8,128)(2,1)S(1)} %get-tuple-element.127), channel_id=1, source_target_pairs={{0,1},{1,0},{2,3},{3,2},{4,5},{5,4},{6,7},{7,6},{8,9},{9,8},{10,11... | collective-permute-start | bytes 1572872 | tf_op jit(solution)/shard_map/ppermute | solution.py:743
  83.2 3.3 %collective-permute-start.17 = (bf16[256,512]{1,0:T(8,128)(2,1)S(1)}, bf16[256,512]{1,0:T(8,128)(2,1)S(1)}, u32[]{:S(2)}, u32[]{:S(2)}) collective-permute-start(bf16[256,512]{1,0:T(8,128)(2,1)S(1)} %get-tuple-element.125), channel_id=1, source_target_pairs={{0,1},{1,0},{2,3},{3,2},{4,5},{5,4},{6,7},{7,6},{8,9},{9,8},{10,11... | collective-permute-start | bytes 786440 | tf_op jit(solution)/shard_map/ppermute | solution.py:743
  87.5 26.7 %all-to-all-start = ((bf16[16,16,1664]{2,1,0:T(8,128)(2,1)}), bf16[16,16,1664]{2,1,0:T(8,128)(2,1)S(1)}, u32[]{:S(2)}, u32[]{:S(2)}) async-start(bf16[16,16,1664]{2,1,0:T(8,128)(2,1)} %bitcast.16), calls=%async_computation | async-start | bytes 1703936 | tf_op jit(solution)/shard_map/all_to_all | solution.py:778
  91.5 22.6 %collective-permute-start.19 = (bf16[2,288,512]{2,1,0:T(8,128)(2,1)S(1)}, bf16[2,288,512]{2,1,0:T(8,128)(2,1)S(1)}, u32[]{:S(2)}, u32[]{:S(2)}) collective-permute-start(bf16[2,288,512]{2,1,0:T(8,128)(2,1)S(1)} %get-tuple-element.128), channel_id=1, source_target_pairs={{0,8},{1,5},{2,10},{3,7},{4,12},{5,1},{6,14},{7,3},{8,0},{9,13},{1... | collective-permute-start | bytes 1769480 | tf_op jit(solution)/shard_map/ppermute | solution.py:809
  115.3 57.7 %all-to-all-start.1 = ((bf16[16,16,1664]{2,1,0:T(8,128)(2,1)}), bf16[16,16,1664]{2,1,0:T(8,128)(2,1)S(1)}, u32[]{:S(2)}, u32[]{:S(2)}) async-start(bf16[16,16,1664]{2,1,0:T(8,128)(2,1)} %total.1.refs_0_), calls=%async_computation.1 | async-start | bytes 1703936 | tf_op jit(solution)/shard_map/all_to_all | solution.py:778
  121.0 30.7 %collective-permute-start.20 = (bf16[2,144,512]{2,1,0:T(8,128)(2,1)S(1)}, bf16[2,144,512]{2,1,0:T(8,128)(2,1)S(1)}, u32[]{:S(2)}, u32[]{:S(2)}) collective-permute-start(bf16[2,144,512]{2,1,0:T(8,128)(2,1)S(1)} %get-tuple-element.130), channel_id=1, source_target_pairs={{0,16},{1,3},{2,18},{3,1},{4,20},{5,7},{6,22},{7,5},{8,24},{9,11},... | collective-permute-start | bytes 884744 | tf_op jit(solution)/shard_map/ppermute | solution.py:809
  151.7 5.2 %collective-permute-start.21 = (bf16[144,512]{1,0:T(8,128)(2,1)S(1)}, bf16[144,512]{1,0:T(8,128)(2,1)S(1)}, u32[]{:S(2)}, u32[]{:S(2)}) collective-permute-start(bf16[144,512]{1,0:T(8,128)(2,1)S(1)} %get-tuple-element.132), channel_id=1, source_target_pairs={{0,2},{1,17},{2,0},{3,19},{4,6},{5,21},{6,4},{7,23},{8,10},{9,25},... | collective-permute-start | bytes 442376 | tf_op jit(solution)/shard_map/ppermute | solution.py:809
  157.0 6.2 %collective-permute-start.22 = (bf16[144,512]{1,0:T(8,128)(2,1)S(1)}, bf16[144,512]{1,0:T(8,128)(2,1)S(1)}, u32[]{:S(2)}, u32[]{:S(2)}) collective-permute-start(bf16[144,512]{1,0:T(8,128)(2,1)S(1)} %add.1.refs_0_.refs_1_), channel_id=1, source_target_pairs={{0,16},{1,17},{2,18},{3,19},{4,20},{5,21},{6,22},{7,23},{8,24},{9,... | collective-permute-start | bytes 442376 | tf_op jit(solution)/shard_map/ppermute | solution.py:809
  163.3 8.1 %collective-permute-start.23 = (bf16[288,512]{1,0:T(8,128)(2,1)S(1)}, bf16[288,512]{1,0:T(8,128)(2,1)S(1)}, u32[]{:S(2)}, u32[]{:S(2)}) collective-permute-start(bf16[288,512]{1,0:T(8,128)(2,1)S(1)} %join.2.refs_0_.refs_1_), channel_id=1, source_target_pairs={{0,8},{1,5},{2,10},{3,7},{4,12},{5,1},{6,14},{7,3},{8,0},{9,13},{1... | collective-permute-start | bytes 884744 | tf_op jit(solution)/shard_map/ppermute | solution.py:809
  171.6 9.9 %collective-permute-start.24 = (bf16[576,512]{1,0:T(8,128)(2,1)S(1)}, bf16[576,512]{1,0:T(8,128)(2,1)S(1)}, u32[]{:S(2)}, u32[]{:S(2)}) collective-permute-start(bf16[576,512]{1,0:T(8,128)(2,1)S(1)} %join.3.refs_0_.refs_1_), channel_id=1, source_target_pairs={{0,4},{1,9},{2,6},{3,11},{4,0},{5,13},{6,2},{7,15},{8,12},{9,1},{1... | collective-permute-start | bytes 1769480 | tf_op jit(solution)/shard_map/ppermute | solution.py:809
  173.1 16.5 %collective-permute-start.25 = (bf16[256,1664]{1,0:T(8,128)(2,1)S(1)}, bf16[256,1664]{1,0:T(8,128)(2,1)S(1)}, u32[]{:S(2)}, u32[]{:S(2)}) collective-permute-start(bf16[256,1664]{1,0:T(8,128)(2,1)S(1)} %bitcast.32), channel_id=1, source_target_pairs={{0,1},{1,0},{2,3},{3,2},{4,5},{5,4},{6,7},{7,6},{8,9},{9,8},{10,11... | collective-permute-start | bytes 2555912 | tf_op jit(solution)/shard_map/ppermute | solution.py:743
  183.0 5.0 %collective-permute-start.26 = (bf16[128,512]{1,0:T(8,128)(2,1)S(1)}, bf16[128,512]{1,0:T(8,128)(2,1)S(1)}, u32[]{:S(2)}, u32[]{:S(2)}) collective-permute-start(bf16[128,512]{1,0:T(8,128)(2,1)S(1)} %get-tuple-element.133.refs_0_), channel_id=1, source_target_pairs={{0,2},{1,3},{2,0},{3,1},{4,6},{5,7},{6,4},{7,5},{8,10},{9,11},{10,... | collective-permute-start | bytes 393224 | tf_op jit(solution)/shard_map/ppermute | solution.py:747
  188.0 1.6 collective-permute-start.27
